TPU v7x, 512 devices: a whole 4x4x16 slice. The times are simulated.
512 devices in a mesh: slab: 64 (over z, y_hi, core), vec: 8 (over y_lo, x).
Axes of the slice: x: 4, y: 4 (y_hi: 2, y_lo: 2; y = y_hi * 2 + y_lo), z: 16, core: 2. Of those that a mesh axis runs over, the one named last changes fastest.
Arguments:
- vectors: bfloat16 [6, 384, 64, 512], P(None, 'vec', 'slab'), may hold values from -0.3125 to 0.3125
- links: bfloat16 [3, 18, 64, 512], P(None, None, 'slab'), may hold values from -2.5 to 2.5
- momenta: int32 [4, 3], replicated, may hold values from -2 to 2
- directions: int32 [3], replicated, may hold values from 0 to 2, each once
- panel_index: int32 [64], replicated, may hold values from 0 to 383, as said below
Outputs:
- elementals: float32 [64, 2, 3, 4, 384], P('slab', None, None, None, 'vec')
Inputs may be any that keep to these rules, and one draw needn't show every extreme that they name: `panel_index`: 64 distinct eigenvector numbers; 0 and 383 are among them.
All inputs are finite; a program needn't handle non-finite values.
Results may differ from a plain program's by a relative error of at most 0.004.
Values may be sent and summed in bfloat16 or wider, within the bound.
No kernel may reach another device: no remote copies, remote signals or barrier semaphores. Data moves between devices by JAX's collectives and lax.ppermute only.
A program may use at most 64 MiB of HBM per device.

v0:
```python
import math

import jax
import jax.numpy as jnp
from jax import lax
from jax.sharding import PartitionSpec as P

LX = 32
LY = 16


def padded(value, sides, width):
    for axis, dim in sides:
        count, length = (lax.axis_size(axis), value.shape[dim])
        up = [(i, (i + 1) % count) for i in range(count)]
        down = [(j, i) for i, j in up]
        last = lax.slice_in_dim(value, length - width, length, axis=dim)
        leading = lax.slice_in_dim(value, 0, width, axis=dim)
        before = lax.ppermute(last, axis, up)
        after = lax.ppermute(leading, axis, down)
        value = jnp.concatenate([before, value, after], axis=dim)
    return value


def roll_sites(values, axis_id, offset):
    shaped = values.reshape(values.shape[:-1] + (LY, LX))
    rolled = jnp.roll(shaped, offset, axis=-1 - axis_id)
    return rolled.reshape(values.shape)


def times_link(link_rows, vector, dagger):
    real_rows = []
    imag_rows = []
    for row_index in range(3):
        total_real = 0.0
        total_imag = 0.0
        for second in range(3):
            if dagger:
                entry_at = second * 3 + row_index
                link_real = link_rows[entry_at][None]
                link_imag = -link_rows[9 + entry_at][None]
            else:
                entry_at = row_index * 3 + second
                link_real = link_rows[entry_at][None]
                link_imag = link_rows[9 + entry_at][None]
            vec_real = vector[second]
            vec_imag = vector[3 + second]
            total_real = total_real + link_real * vec_real - link_imag * vec_imag
            total_imag = total_imag + link_real * vec_imag + link_imag * vec_real
        real_rows.append(total_real)
        imag_rows.append(total_imag)
    return jnp.stack(real_rows + imag_rows)


def site_phase(momenta, z_coord, extent_z):
    x_coord = jnp.arange(LX, dtype=jnp.int32)
    y_coord = jnp.arange(LY, dtype=jnp.int32)
    modulus = LX * LY * extent_z
    numerator = (
        momenta[:, 0, None, None, None] * x_coord[None, None, None, :] * (LY * extent_z)
        + momenta[:, 1, None, None, None] * y_coord[None, None, :, None] * (LX * extent_z)
        + momenta[:, 2, None, None, None] * z_coord[None, :, None, None] * (LX * LY)
    ) % modulus
    angles = numerator.astype(jnp.float32) * (2.0 * math.pi / modulus)
    shape_out = (momenta.shape[0], z_coord.shape[0] * LY * LX)
    return (jnp.cos(angles).reshape(shape_out), jnp.sin(angles).reshape(shape_out))


def weigh(panel_vals, cos_part, sin_part):
    cos_b = cos_part[:, None, None, :]
    sin_b = sin_part[:, None, None, :]
    real_part = panel_vals[None, :3] * cos_b - panel_vals[None, 3:] * sin_b
    imag_part = -(panel_vals[None, :3] * sin_b + panel_vals[None, 3:] * cos_b)
    return jnp.stack([real_part, imag_part], 1).astype(jnp.bfloat16)


def pick_directions(directions, shifted):
    onehot = (directions[:, None] == jnp.arange(3, dtype=jnp.int32)[None, :]).astype(jnp.float32)
    chosen = 0.0
    for axis_id in range(3):
        factor = onehot[:, axis_id].reshape((-1,) + (1,) * shifted[axis_id].ndim)
        chosen = chosen + factor * shifted[axis_id][None]
    return chosen


def body(vectors, links, momenta, directions, panel_index):
    holding = vectors.shape[1]
    planes = vectors.shape[2]
    site_count = vectors.shape[3]
    npanel = panel_index.shape[0]
    ndir = directions.shape[0]
    slab_id = lax.axis_index("slab")
    extent_z = planes * lax.axis_size("slab")
    row_total = 6 * holding
    centre = vectors.astype(jnp.float32)
    link_f = links.astype(jnp.float32)
    shifted = []
    for axis_id in range(2):
        link_axis = link_f[axis_id]
        forward_term = times_link(link_axis, roll_sites(centre, axis_id, -1), False)
        backward_term = times_link(
            roll_sites(link_axis, axis_id, 1), roll_sites(centre, axis_id, 1), True
        )
        shifted.append(0.5 * (forward_term - backward_term))
    joined = jnp.concatenate([vectors.reshape(row_total, planes, site_count), links[2]], axis=0)
    extended = padded(joined, (("slab", 1),), 1)
    forward_field = (
        extended[:row_total, 2:].reshape(6, holding, planes, site_count).astype(jnp.float32)
    )
    behind_field = (
        extended[:row_total, :-2].reshape(6, holding, planes, site_count).astype(jnp.float32)
    )
    link_below = extended[row_total:, :-2].astype(jnp.float32)
    behind_term = times_link(link_below, behind_field, True)
    shifted.append(0.5 * (times_link(link_f[2], forward_field, False) - behind_term))
    displaced = pick_directions(directions, shifted).astype(jnp.bfloat16)
    displaced = displaced.reshape(ndir, 2, 3, holding, planes * site_count)
    vec_id = lax.axis_index("vec")
    owned_ids = vec_id * holding + jnp.arange(holding, dtype=jnp.int32)
    selector = (panel_index[:, None] == owned_ids[None, :]).astype(jnp.bfloat16)
    picked = jnp.einsum("pn,cnzs->cpzs", selector, vectors, preferred_element_type=jnp.float32)
    gathered = lax.psum(picked.astype(jnp.bfloat16), "vec").astype(jnp.float32)
    panel_vals = gathered.reshape(6, npanel, planes * site_count)
    z_coord = slab_id * planes + jnp.arange(planes, dtype=jnp.int32)
    cos_part, sin_part = site_phase(momenta, z_coord, extent_z)
    share_rows = npanel // lax.axis_size("slab")

    def one_momentum(phase):
        cos_row, sin_row = phase
        weighted = weigh(panel_vals, cos_row[None], sin_row[None])
        return jnp.einsum(
            "mrcpk,dtcnk->mrpdtn", weighted, displaced, preferred_element_type=jnp.float32
        )[0]

    products = lax.map(one_momentum, (cos_part, sin_part))
    real_part = products[:, 0, :, :, 0] - products[:, 1, :, :, 1]
    imag_part = products[:, 0, :, :, 1] + products[:, 1, :, :, 0]
    whole = lax.psum(jnp.stack([real_part, imag_part], 0).transpose(2, 0, 3, 1, 4), "slab")
    return lax.dynamic_slice_in_dim(whole, slab_id * share_rows, share_rows, 0)


def solution(mesh):
    placed = (P(None, "vec", "slab", None), P(None, None, "slab", None), P(), P(), P())
    return jax.shard_map(
        body,
        mesh=mesh,
        in_specs=placed,
        out_specs=P("slab", None, None, None, "vec"),
        check_vma=False,
    )
```

profile of v0, /device:TPU:1, one launch (start us, length us, event | category | flops | bytes accessed | tf_op | source)
XLA Modules:
  0.0 639.8 jit_solution(4455911046167283562)
XLA Ops:
  7.3 1.7 pad_maximum_fusion.4
  9.0 6.2 collective-permute-start.1
  15.2 4.5 collective-permute-start
  19.7 2.1 fusion.16
  21.9 1.7 fusion.81
  23.7 1.7 reshape.10339
  25.3 2.6 fusion.78
  30.3 3.0 fusion.79
  33.3 3.0 fusion.80
  38.5 2.0 fusion.18
  41.7 0.9 mul.4241
  42.6 0.8 mul.4246
  43.3 0.8 mul.4251
  44.1 0.8 neg.248
  44.9 0.8 neg.250
  45.7 0.8 neg.252
  46.5 0.8 mul.4256
  47.2 0.8 mul.4261
  48.0 0.8 mul.4266
  48.8 0.8 neg.254
  49.6 0.8 neg.256
  50.3 0.8 neg.258
  51.1 0.8 mul.4271
  51.9 0.8 mul.4276
  52.7 0.8 mul.4281
  53.4 0.8 neg.260
  54.2 0.8 neg.262
  55.0 0.8 neg.264
  56.2 0.8 copy-done.5
  57.0 1.4 fusion.23
  58.5 1.2 squeeze.64
  59.7 1.2 squeeze.65
  60.8 1.2 squeeze.66
  62.0 1.2 squeeze.67
  63.1 1.2 squeeze.68
  65.1 0.8 copy-done.7
  66.0 1.0 copy-done.3
  66.9 2.0 fusion.28
  69.0 1.2 squeeze.58
  70.2 1.2 squeeze.59
  71.4 1.2 squeeze.60
  72.5 1.2 squeeze.61
  73.7 1.2 squeeze.62
  76.9 0.8 copy-done.9
  78.3 1.8 fusion.33
  80.3 1.2 squeeze.52
  81.5 1.2 squeeze.53
  82.6 1.2 squeeze.54
  83.8 1.2 squeeze.55
  86.5 0.9 subtract_multiply_fusion.1
  87.7 2.0 subtract_multiply_fusion.2
  90.5 1.0 slice_convert_fusion
  92.3 1.0 slice_convert_fusion.1
  93.9 0.9 subtract_multiply_fusion
  94.9 14.3 %all-reduce.3.cloned.1.call-done = bf16[6,64,512]{2,1,0:T(8,128)(2,1)} async-done(((bf16[6,64,512]{2,1,0:T(8,128)(2,1)}), bf16[6,64,512]{2,1,0:T(8,128)(2,1)}) %all-reduce.3.cloned.1.call-update) | async-done | bytes 393232 | tf_op jit(solution)/shard_map/psum | solution.py:122
  109.1 1.1 reshape.10334
  110.2 7.1 %while.11 = (s32[]{:T(128)}, f32[4,2,64,3,2,48]{2,5,4,3,1,0:T(8,128)S(1)}, f32[6,64,512]{2,1,0:T(8,128)S(1)}, f32[4,512]{1,0:T(4,128)S(1)}, f32[4,512]{1,0:T(4,1...) while((s32[]{:T(128)}, ...), condition=%wide.region_2.3_spmd.clone, body=%wide.region_1.2_spmd.clone.sunk | while | flops 117571584 | bytes 3651197 | solution.py:135
  110.4 1.6 fusion.91
  112.2 1.6 fusion.91
  113.9 1.6 fusion.91
  115.7 1.6 fusion.91
  118.3 1.1 maximum_bitcast_fusion.2
  119.4 512.2 %all-reduce.5.cloned.1.call-done = f32[64,2,3,4,48]{4,3,2,1,0:T(4,128)} async-done(((f32[64,2,3,4,48]{4,3,2,1,0:T(4,128)}), f32[64,2,3,4,48]{4,3,2,1,0:T(4,128)}) %all-reduce.5.cloned.1.call-update) | async-done | bytes 294928 | tf_op jit(solution)/shard_map/psum | solution.py:138
  631.7 1.3 constant_dynamic-slice_fusion.2
  (264 shorter events, 14.9 us)
Async XLA Ops:
  6.5 102.6 %all-reduce.3.cloned.1.call-start = ((), (), s32[]{:S(2)}) async-start(), calls=%async_computation | async-start | bytes 786432 | tf_op jit(solution)/shard_map/psum | solution.py:122
  9.0 80.7 %collective-permute-start.1 = (bf16[306,1,512]{2,0,1:T(8,128)(2,1)}, bf16[306,1,512]{2,0,1:T(8,128)(2,1)}, u32[]{:S(2)}, u32[]{:S(2)}) collective-permute-start(bf16[306,1,512]{2,0,1:T(8,128)(2,1)} %pad_maximum_fusion.4), channel_id=1, source_target_pairs={{0,8},{8,16},{16,24},{24,32},{32,40},{40,48},{48,56},{56,64},{64,7... | collective-permute-start | bytes 940040 | tf_op jit(solution)/shard_map/ppermute | solution.py:19
  15.2 77.1 %collective-permute-start = (bf16[306,1,512]{2,0,1:T(8,128)(2,1)}, bf16[306,1,512]{2,0,1:T(8,128)(2,1)}, u32[]{:S(2)}, u32[]{:S(2)}) collective-permute-start(bf16[306,1,512]{2,0,1:T(8,128)(2,1)} %pad_maximum_fusion.4), channel_id=1, source_target_pairs={{8,0},{16,8},{24,16},{32,24},{40,32},{48,40},{56,48},{64,56},{72,6... | collective-permute-start | bytes 940040 | tf_op jit(solution)/shard_map/ppermute | solution.py:20
  21.9 609.8 %all-reduce.5.cloned.1.call-start = ((), (), s32[]{:S(2)}) async-start(), calls=%async_computation.1 | async-start | bytes 1572864 | tf_op jit(solution)/shard_map/psum | solution.py:138
  25.3 2.9 copy-start.12
  41.5 15.5 %copy-start.4 = (f32[6,48,1,15,32]{4,3,1,0,2:T(8,128)S(1)}, f32[6,48,1,15,32]{4,3,1,0,2:T(8,128)}, u32[]{:S(2)}) copy-start(f32[6,48,1,15,32]{4,3,1,0,2:T(8,128)} %get-tuple-element.126) | copy-start | bytes 1658884
  58.4 6.1 copy-start.73
  58.4 6.1 copy-start.74
  58.4 6.1 copy-start.75
  58.4 6.1 copy-start.76
  58.4 6.1 copy-start.77
  58.4 6.1 copy-start.78
  58.4 6.2 copy-start.67
  58.4 6.2 copy-start.68
  58.4 6.2 copy-start.69
  58.4 6.2 copy-start.70
  58.5 6.2 copy-start.71
  58.5 6.2 copy-start.72
  58.5 6.3 copy-start.61
  58.5 6.3 copy-start.62
  58.5 6.3 copy-start.63
  58.5 6.3 copy-start.64
  58.5 6.3 copy-start.65
  58.5 6.3 copy-start.66
  64.5 2.4 copy-start.3
  68.9 6.1 copy-start.24
  68.9 6.2 copy-start.23
  68.9 6.3 copy-start.22
  68.9 6.3 copy-start.21
  68.9 6.4 %copy-start.19 = (f32[1,1,16,32]{3,2,0,1:T(8,128)S(1)}, f32[1,1,16,32]{3,2,0,1:T(8,128)}, u32[]{:S(2)}) copy-start(f32[1,1,16,32]{3,2,0,1:T(8,128)} %get-tuple-element.137) | copy-start | bytes 6148
  68.9 6.5 %copy-start.17 = (f32[1,1,16,32]{3,2,0,1:T(8,128)S(1)}, f32[1,1,16,32]{3,2,0,1:T(8,128)}, u32[]{:S(2)}) copy-start(f32[1,1,16,32]{3,2,0,1:T(8,128)} %get-tuple-element.139) | copy-start | bytes 6148
  68.9 6.6 %copy-start.16 = (f32[1,1,16,32]{3,2,0,1:T(8,128)S(1)}, f32[1,1,16,32]{3,2,0,1:T(8,128)}, u32[]{:S(2)}) copy-start(f32[1,1,16,32]{3,2,0,1:T(8,128)} %get-tuple-element.140) | copy-start | bytes 6148
  68.9 6.6 %copy-start.20 = (f32[1,1,16,32]{3,2,0,1:T(8,128)S(1)}, f32[1,1,16,32]{3,2,0,1:T(8,128)}, u32[]{:S(2)}) copy-start(f32[1,1,16,32]{3,2,0,1:T(8,128)} %get-tuple-element.143) | copy-start | bytes 6148
  68.9 6.7 %copy-start.18 = (f32[1,1,16,32]{3,2,0,1:T(8,128)S(1)}, f32[1,1,16,32]{3,2,0,1:T(8,128)}, u32[]{:S(2)}) copy-start(f32[1,1,16,32]{3,2,0,1:T(8,128)} %get-tuple-element.145) | copy-start | bytes 6148
  69.0 6.9 %copy-start.15 = (f32[1,1,16,32]{3,2,0,1:T(8,128)S(1)}, f32[1,1,16,32]{3,2,0,1:T(8,128)}, u32[]{:S(2)}) copy-start(f32[1,1,16,32]{3,2,0,1:T(8,128)} %get-tuple-element.144) | copy-start | bytes 6148
  74.8 2.9 copy-start
  76.4 1.9 copy-start.1
  80.2 5.2 copy-start.55
  80.2 5.2 copy-start.56
  80.2 5.2 copy-start.57
  80.2 5.2 copy-start.58
  80.2 5.2 copy-start.59
  80.2 5.2 copy-start.60
  80.2 5.3 copy-start.49
  80.2 5.3 copy-start.50
  80.2 5.3 copy-start.51
  80.2 5.3 copy-start.52
  80.2 5.3 copy-start.53
  80.2 5.3 copy-start.54
  80.3 5.3 copy-start.43
  80.3 5.3 copy-start.44
  80.3 5.3 copy-start.45
  80.3 5.3 copy-start.46
  80.3 5.3 copy-start.47
  80.3 5.3 copy-start.48
  85.6 2.1 copy-start.10
  91.6 1.7 copy-start.37
  91.6 1.7 copy-start.38
  91.6 1.7 copy-start.39
  91.6 1.7 copy-start.40
  91.6 1.7 copy-start.41
  91.6 1.7 copy-start.42
  93.7 16.5 %copy-start.13 = (f32[1,6,48,1,512]{4,2,3,1,0:T(8,128)S(1)}, f32[1,6,48,1,512]{4,2,3,1,0:T(8,128)}, u32[]{:S(2)}) copy-start(f32[1,6,48,1,512]{4,2,3,1,0:T(8,128)} %subtract_multiply_fusion.1) | copy-start | bytes 1769476
  93.7 16.5 %copy-start.14 = (f32[1,6,48,1,512]{4,2,3,1,0:T(8,128)S(1)}, f32[1,6,48,1,512]{4,2,3,1,0:T(8,128)}, u32[]{:S(2)}) copy-start(f32[1,6,48,1,512]{4,2,3,1,0:T(8,128)} %subtract_multiply_fusion.2) | copy-start | bytes 1769476
  (21 other events, 31.0 us)
Sparse Core Ops, SparseCore 0:
  22.0 87.0 all-reduce.2
  119.6 512.0 all-reduce.4
where the time goes:
time: 642 us; the launch traced here: 640 us
  waiting for transfers between devices  527 us (82%)
  local copies, waits for them, and re-layouts  54.8 us (9%)
  other arithmetic  24.1 us (4%)
  between operations  14.9 us (2%)
  starting transfers between devices  10.7 us (2%)
  matrix products  8.55 us (1%)
    psum x1, waiting for transfers between devices, body(): lax.psum(jnp.stack([real_part, imag_part], 0).transpose(2, 0, 3, 1, 4), '...  512 us
    psum x1, waiting for transfers between devices, body(): gathered = lax.psum(picked.astype(jnp.bfloat16), 'vec').astype(jnp.float32)  14.3 us
  transfers between devices with their start and end apart: 4, of which 2 were waited for; matrix products, arithmetic and copies ran while one was open for 11% of the time, Pallas kernels for 0%

commit v1 on v0

v1 whole, which is shorter than its diff:
```python
import functools
import math

import jax
import jax.numpy as jnp
from jax import lax
from jax.experimental import pallas as pl
from jax.experimental.pallas import tpu as pltpu
from jax.sharding import PartitionSpec as P

LX = 32
LY = 16
CAP = 16
TILE = 16
LANES = 128
F32 = jnp.float32
BF16 = jnp.bfloat16
NT = (((1,), (1,)), ((), ()))


def iota(shape, dim):
    return lax.broadcasted_iota(jnp.int32, shape, dim)


def as_column(row):
    n = row.shape[1]
    return jnp.sum(jnp.where(iota((n, n), 0) == iota((n, n), 1), row, 0.0), axis=1, keepdims=True)


def select_kernel(cap, ids_ref, vec_ref, links_ref, pay_ref, up_ref):
    rows, held, sites = vec_ref.shape
    ids = ids_ref[...]
    npanel = ids.shape[1]
    local = ids - lax.axis_index("vec") * held
    inside = (local >= 0) & (local < held)
    mine = jnp.where(inside, 1.0, 0.0)
    before = iota((npanel, npanel), 0) < iota((npanel, npanel), 1)
    rank = jnp.sum(jnp.where(before, as_column(mine), 0.0), axis=0, keepdims=True)
    place = jnp.where(inside, rank, -1.0)
    to_slot = jnp.where(iota((cap, npanel), 0).astype(F32) == place, 1.0, 0.0)
    of_held = jnp.where(iota((held, npanel), 0) == local, 1.0, 0.0)
    pick = lax.dot_general(to_slot, of_held, NT, preferred_element_type=F32).astype(BF16)
    for row in range(rows):
        part = jnp.dot(pick, vec_ref[row], preferred_element_type=F32).astype(BF16)
        for peer in range(pay_ref.shape[0]):
            pay_ref[peer, row * cap:(row + 1) * cap, :] = part
    for row in range(rows):
        up_ref[row * held:(row + 1) * held, :] = vec_ref[row]
    zlink = links_ref[2].astype(F32)
    spare = up_ref.shape[0] - rows * held - zlink.shape[0]
    up_ref[rows * held:, :] = jnp.concatenate([zlink, jnp.zeros((spare, sites), F32)], axis=0).astype(BF16)


def link_terms(ahead, behind, fore, back):
    real, imag = [], []
    for row in range(3):
        re, im = 0.0, 0.0
        for col in range(3):
            ur, ui = fore(row * 3 + col), fore(9 + row * 3 + col)
            re = re + ur * ahead[col] - ui * ahead[3 + col]
            im = im + ur * ahead[3 + col] + ui * ahead[col]
        for col in range(3):
            ur, ui = back(col * 3 + row), back(9 + col * 3 + row)
            re = re - ur * behind[col] - ui * behind[3 + col]
            im = im - ur * behind[3 + col] + ui * behind[col]
        real.append(re)
        imag.append(im)
    return real + imag


def turn_x(value, ahead):
    inner = iota((value.shape[0], LANES), 1) % LX
    parts = []
    for at in range(0, value.shape[1], LANES):
        part = value[:, at:at + LANES]
        if ahead:
            part = jnp.where(inner == LX - 1, pltpu.roll(part, LX - 1, 1), pltpu.roll(part, LANES - 1, 1))
        else:
            part = jnp.where(inner == 0, pltpu.roll(part, LANES - LX + 1, 1), pltpu.roll(part, 1, 1))
        parts.append(part)
    return jnp.concatenate(parts, axis=1)


def turn_y(value, ahead):
    sites = value.shape[1]
    return pltpu.roll(value, sites - LX if ahead else LX, 1)


def planar_kernel(vec_ref, links_ref, out_ref, link_ref, turned_ref):
    rows, held, sites = vec_ref.shape
    for axis_id, turn in enumerate((turn_x, turn_y)):
        link = links_ref[axis_id].astype(F32) * 0.5
        link_ref[2 * axis_id] = link
        link_ref[2 * axis_id + 1] = turn(link, False)

    def step(at, carry):
        first = pl.multiple_of(at * TILE, TILE)
        for row in range(rows):
            value = vec_ref[row, pl.ds(first, TILE), :].astype(F32)
            for axis_id, turn in enumerate((turn_x, turn_y)):
                turned_ref[axis_id, 0, row] = turn(value, True)
                turned_ref[axis_id, 1, row] = turn(value, False)
        for axis_id in range(2):
            for lane in range(0, sites, LANES):
                span = slice(lane, lane + LANES)
                ahead = [turned_ref[axis_id, 0, row, :, span] for row in range(rows)]
                behind = [turned_ref[axis_id, 1, row, :, span] for row in range(rows)]
                shifted = link_terms(
                    ahead, behind,
                    lambda e: link_ref[2 * axis_id, e:e + 1, span],
                    lambda e: link_ref[2 * axis_id + 1, e:e + 1, span],
                )
                for row in range(rows):
                    out_ref[axis_id, pl.ds(first, TILE), row * sites + lane:row * sites + lane + LANES] = (
                        shifted[row].astype(BF16))
        return carry

    lax.fori_loop(0, held // TILE, step, 0)


def main_kernel(cap, momenta_ref, ids_ref, planar_ref, ahead_ref, behind_ref, links_ref, got_ref,
                keep_ref, send_ref, link_ref, field_ref, panel_ref, phase_ref, weight_ref):
    owners = got_ref.shape[0]
    npanel = ids_ref.shape[1]
    held = planar_ref.shape[1]
    sites = got_ref.shape[2]
    rows = got_ref.shape[1] // cap
    nmom = momenta_ref.shape[0]
    slab_id = lax.axis_index("slab")
    core = slab_id % 2

    field_ref[0:2 * held, :] = planar_ref[...].reshape(2 * held, rows * sites)
    link_ref[0] = links_ref[2].astype(F32) * 0.5
    link_ref[1] = behind_ref[rows * held:rows * held + 32, :].astype(F32)[:18] * 0.5

    def z_step(at, carry):
        first = pl.multiple_of(at * TILE, TILE)
        for lane in range(0, sites, LANES):
            span = slice(lane, lane + LANES)
            ahead = [ahead_ref[pl.ds(row * held + first, TILE), span].astype(F32) for row in range(rows)]
            behind = [behind_ref[pl.ds(row * held + first, TILE), span].astype(F32) for row in range(rows)]
            shifted = link_terms(
                ahead, behind,
                lambda e: link_ref[0, e:e + 1, span],
                lambda e: link_ref[1, e:e + 1, span],
            )
            for row in range(rows):
                field_ref[pl.ds(2 * held + first, TILE), row * sites + lane:row * sites + lane + LANES] = (
                    shifted[row].astype(BF16))
        return carry

    lax.fori_loop(0, held // TILE, z_step, 0)

    ids = ids_ref[...]
    owner = jnp.zeros(ids.shape, F32)
    for other in range(1, owners):
        owner = owner + jnp.where(ids >= other * held, 1.0, 0.0)
    owner_col = as_column(owner)
    before = iota((npanel, npanel), 0) < iota((npanel, npanel), 1)
    rank = jnp.sum(jnp.where(before & (owner_col == owner), 1.0, 0.0), axis=0, keepdims=True)
    slot = owner * cap + rank
    place = iota((npanel, npanel), 0)
    half = npanel // 2
    wanted = jnp.where(place < half, 2 * place + core, 2 * (place - half) + 1 - core)
    slot_col = jnp.sum(jnp.where(iota((npanel, npanel), 1) == wanted, slot, 0.0), axis=1, keepdims=True)
    order = jnp.where(iota((npanel, owners * cap), 1).astype(F32) == slot_col, 1.0, 0.0).astype(BF16)
    for row in range(rows):
        block = got_ref[:, row * cap:(row + 1) * cap, :].reshape(owners * cap, sites)
        panel_ref[row] = jnp.dot(order, block, preferred_element_type=F32)

    modulus = sites * lax.axis_size("slab")
    shape = (2 * nmom, sites)
    site, line = iota(shape, 1), iota(shape, 0)
    x_coord, y_coord = site % LX, site // LX
    turns = jnp.zeros(shape, jnp.int32)
    for mom in range(nmom):
        along = (momenta_ref[mom, 0] * (modulus // LX) * x_coord
                 + momenta_ref[mom, 1] * (modulus // LY) * y_coord
                 + momenta_ref[mom, 2] * sites * slab_id)
        turns = jnp.where(line % nmom == mom, along, turns)
    turns = jnp.where(line >= nmom, turns - modulus // 4, turns) & (modulus - 1)
    turns = jnp.where(turns >= modulus // 2, turns - modulus, turns)
    phase_ref[...] = jnp.cos(turns.astype(F32) * (2.0 * math.pi / modulus))

    def weigh(at, carry):
        first = pl.multiple_of(at * TILE, TILE)
        for colour in range(3):
            re = panel_ref[colour, pl.ds(first, TILE), :]
            im = panel_ref[3 + colour, pl.ds(first, TILE), :]
            for mom in range(nmom):
                cos = phase_ref[mom:mom + 1, :]
                sin = phase_ref[nmom + mom:nmom + mom + 1, :]
                wr = (re * cos - im * sin).astype(BF16)
                wi = re * sin + im * cos
                low = slice(colour * sites, (colour + 1) * sites)
                high = slice((3 + colour) * sites, (4 + colour) * sites)
                weight_ref[pl.ds(mom * npanel + first, TILE), low] = wr
                weight_ref[pl.ds(mom * npanel + first, TILE), high] = wi.astype(BF16)
                weight_ref[pl.ds((nmom + mom) * npanel + first, TILE), low] = (-wi).astype(BF16)
                weight_ref[pl.ds((nmom + mom) * npanel + first, TILE), high] = wr
        return carry

    lax.fori_loop(0, npanel // TILE, weigh, 0)
    whole = lax.dot_general(weight_ref[...], field_ref[...], NT, preferred_element_type=F32)
    for part in range(2 * nmom):
        block = whole[part * npanel:(part + 1) * npanel]
        keep_ref[:, part, :] = block[:half]
        send_ref[:, part, :] = block[half:]


def sum_kernel(nmom, directions_ref, parts_ref, out_ref):
    total = jnp.sum(parts_ref[...], axis=0)
    held = out_ref.shape[-1]
    for place in range(out_ref.shape[1]):
        chosen = total[:, 0:held]
        for axis_id in (1, 2):
            along = total[:, axis_id * held:(axis_id + 1) * held]
            chosen = jnp.where(directions_ref[place] == axis_id, along, chosen)
        out_ref[0, place] = chosen[:nmom]
        out_ref[1, place] = chosen[nmom:]


def specs(*spaces):
    return [pl.BlockSpec(memory_space=pltpu.SMEM if s == "s" else pltpu.VMEM) for s in spaces]


def run(cap, vectors, links, momenta, directions, panel_index):
    rows, held, planes, sites = vectors.shape
    npanel = panel_index.shape[0]
    nmom = momenta.shape[0]
    nslab, nvec = lax.axis_size("slab"), lax.axis_size("vec")
    vec = vectors.reshape(rows, held, sites)
    link = links.reshape(3, 18, sites)
    ids = panel_index.reshape(1, npanel)
    params = pltpu.CompilerParams(vmem_limit_bytes=40 * 1024 * 1024)
    shape = jax.ShapeDtypeStruct
    vm = pltpu.VMEM
    pay, up = pl.pallas_call(
        functools.partial(select_kernel, cap),
        out_shape=[shape((nvec, rows * cap, sites), BF16), shape((rows * held + 32, sites), BF16)],
        in_specs=specs("v", "v", "v"), out_specs=specs("v", "v"),
        compiler_params=params, name="select",
    )(ids, vec, link)
    upward = [(i, (i + 1) % nslab) for i in range(nslab)]
    downward = [(j, i) for i, j in upward]
    ahead = lax.ppermute(vec.reshape(rows * held, sites), "slab", downward)
    behind = lax.ppermute(up, "slab", upward)
    got = lax.all_to_all(pay, "vec", 0, 0, tiled=True)
    planar = pl.pallas_call(
        planar_kernel,
        out_shape=shape((2, held, rows * sites), BF16),
        in_specs=specs("v", "v"), out_specs=specs("v")[0],
        scratch_shapes=[vm((4, 18, sites), F32), vm((2, 2, rows, TILE, sites), F32)],
        compiler_params=params, name="planar",
    )(vec, link)
    half = npanel // 2
    part = shape((half, 2 * nmom, 3 * held), F32)
    keep, send = pl.pallas_call(
        functools.partial(main_kernel, cap),
        out_shape=[part, part],
        in_specs=specs("s", "v", "v", "v", "v", "v", "v"), out_specs=specs("v", "v"),
        scratch_shapes=[
            vm((2, 18, sites), F32),
            vm((3 * held, rows * sites), BF16),
            vm((rows, npanel, sites), F32),
            vm((2 * nmom, sites), F32),
            vm((2 * nmom * npanel, rows * sites), BF16),
        ],
        compiler_params=params, name="main",
    )(momenta, ids, planar, ahead, behind, link, got)
    pair = lax.ppermute(send, "slab", [(i, i ^ 1) for i in range(nslab)])
    groups = [[2 * k + c for k in range(nslab // 2)] for c in range(2)]
    parts = lax.all_to_all(keep + pair, "slab", 0, 0, axis_index_groups=groups, tiled=True)
    return pl.pallas_call(
        functools.partial(sum_kernel, nmom),
        out_shape=shape((2, 3, nmom, held), F32),
        in_specs=specs("s", "v"), out_specs=specs("v")[0],
        name="total",
    )(directions, parts)[None]


def body(vectors, links, momenta, directions, panel_index):
    held = vectors.shape[1]
    owner = panel_index // held
    counts = jnp.sum((owner[:, None] == jnp.arange(lax.axis_size("vec"))[None, :]).astype(jnp.int32), axis=0)
    args = (vectors, links, momenta, directions, panel_index)
    return lax.cond(jnp.max(counts) <= CAP, functools.partial(run, CAP), functools.partial(run, held), *args)


def solution(mesh):
    placed = (P(None, "vec", "slab", None), P(None, None, "slab", None), P(), P(), P())
    return jax.shard_map(
        body,
        mesh=mesh,
        in_specs=placed,
        out_specs=P("slab", None, None, None, "vec"),
        check_vma=False,
    )
```

time: 642 us -> 76.4 us (0.12)
  the two profiles are of different devices: /device:TPU:1 before, /device:TPU:24 now
where the time goes in v1:
time: 76.4 us; the launch traced here: 76 us
  blocking collectives  38.9 us (51%)
  starting transfers between devices  14.9 us (20%)
  waiting for transfers between devices  10 us (13%)
  Pallas kernels  9.4 us (12%)
  other arithmetic  1.46 us (2%)
    all_to_all x1, blocking collectives, run(): lax.all_to_all(keep + pair, 'slab', 0, 0, axis_index_groups=groups, tiled...  38.9 us
    ppermute x1, waiting for transfers between devices, run(): ahead = lax.ppermute(vec.reshape(rows * held, sites), 'slab', downward)  7.14 us
    all_to_all x1, starting transfers between devices, run(): got = lax.all_to_all(pay, 'vec', 0, 0, tiled=True)  5.76 us
    ppermute x1, starting transfers between devices, run(): ahead = lax.ppermute(vec.reshape(rows * held, sites), 'slab', downward)  5.15 us
    pallas_call x1, Pallas kernels, run(): pl.pallas_call(functools.partial(main_kernel, cap), out_shape=[part, part...  3.18 us
    pallas_call x1, Pallas kernels, run(): pl.pallas_call(planar_kernel, out_shape=shape((2, held, rows * sites), BF...  2.69 us
    pallas_call x1, Pallas kernels, run(): pl.pallas_call(functools.partial(select_kernel, cap), out_shape=[shape((n...  2.33 us
    ppermute x1, starting transfers between devices, run(): behind = lax.ppermute(up, 'slab', upward)  2.04 us
  transfers between devices with their start and end apart: 4, of which 3 were waited for; matrix products, arithmetic and copies ran while one was open for 0% of the time, Pallas kernels for 4%

profile of v1, /device:TPU:24, one launch (start us, length us, event | category | flops | bytes accessed | tf_op | source)
XLA Modules:
  0.0 76.0 jit_solution(2875796095560913985)
XLA Ops:
  0.0 0.7 and_select_fusion
  0.7 0.1 convert_reduce_fusion
  0.8 0.6 reduce_max.9
  2.1 73.3 %conditional.1 = (f32[1,2,3,4,48]{4,3,2,1,0:T(4,128)S(1)}) conditional(s32[]{:T(128)} %convert_element_type.7, (s32[64]{0:T(128)}, bf16[6,48,1,512]{3,1,2,0:T(8,128)(2,1)}, bf16[3,18,1,512]{3,1,2,0:T(8,128)(2,1)}, s32[4,3]{1,0:T(4,128)}, s32[3]{0:T(128)}) %tuple.11, (s32[64]{0:T(128)}, bf16[6,48,1,512]{3,1,2,0:T(8,128)(2,1)}, ...), branch_computations={%region_2.3_spmd, %region_3.4_spmd} | conditional | flops 36864 | bytes 22914644 | solution.py:287
  2.1 0.0 copy-start.4
  2.1 0.0 copy-start.7
  2.1 0.0 copy-start.9
  2.1 2.3 %select.3 = (bf16[8,96,512]{2,1,0:T(8,128)(2,1)}, bf16[320,512]{1,0:T(8,128)(2,1)S(1)}) custom-call(s32[1,64]{1,0:T(1,128)} %bitcast.26, bf16[6,48,512]{2,1,0:T(8,128)(2,1)} %bitcast.10.vec_ref, bf16[3,18,512]{2,1,0:T(8,128)(2,1)} %bitcast.19), custom_call_target="tpu_custom_call" | custom-call | tf_op jit(solution)/shard_map/cond/branch_1_fun/select/pallas_call | solution.py:238
  4.5 5.8 %all-to-all-start.2 = ((bf16[8,96,512]{2,1,0:T(8,128)(2,1)}), bf16[8,96,512]{2,1,0:T(8,128)(2,1)S(1)}, u32[]{:S(2)}, u32[]{:S(2)}) async-start(bf16[8,96,512]{2,1,0:T(8,128)(2,1)} %get-tuple-element.43), calls=%async_computation.2 | async-start | bytes 1572864 | tf_op jit(solution)/shard_map/cond/branch_1_fun/all_to_all | solution.py:248
  10.2 0.0 copy-start.11
  10.2 2.0 %collective-permute-start.4 = (bf16[320,512]{1,0:T(8,128)(2,1)S(1)}, bf16[320,512]{1,0:T(8,128)(2,1)S(1)}, u32[]{:S(2)}, u32[]{:S(2)}) collective-permute-start(bf16[320,512]{1,0:T(8,128)(2,1)S(1)} %get-tuple-element.42), channel_id=1, source_target_pairs={{0,8},{8,16},{16,24},{24,32},{32,40},{40,48},{48,56},{56,64},{64,7... | collective-permute-start | bytes 983048 | tf_op jit(solution)/shard_map/cond/branch_1_fun/ppermute | solution.py:247
  12.3 5.1 %collective-permute-start.3 = (bf16[288,512]{1,0:T(8,128)(2,1)}, bf16[288,512]{1,0:T(8,128)(2,1)S(1)}, u32[]{:S(2)}, u32[]{:S(2)}) collective-permute-start(bf16[288,512]{1,0:T(8,128)(2,1)} %bitcast.13), channel_id=1, source_target_pairs={{8,0},{16,8},{24,16},{32,24},{40,32},{48,40},{56,48},{64,56},{72,6... | collective-permute-start | bytes 884744 | tf_op jit(solution)/shard_map/cond/branch_1_fun/ppermute | solution.py:246
  17.4 2.7 %planar.3.planar_ref = bf16[2,48,3072]{2,1,0:T(8,128)(2,1)S(1)} custom-call(bf16[6,48,512]{2,1,0:T(8,128)(2,1)} %bitcast.10.vec_ref, bf16[3,18,512]{2,1,0:T(8,128)(2,1)} %bitcast.20), custom_call_target="tpu_custom_call" | custom-call | tf_op jit(solution)/shard_map/cond/branch_1_fun/planar/pallas_call | solution.py:249
  20.1 7.1 %collective-permute-done.3.ahead_ref = bf16[288,512]{1,0:T(8,128)(2,1)S(1)} collective-permute-done((bf16[288,512]{1,0:T(8,128)(2,1)}, bf16[288,512]{1,0:T(8,128)(2,1)S(1)}, u32[]{:S(2)}, u32[]{:S(2)}) %collective-permute-start.3) | collective-permute-done | bytes 294944 | tf_op jit(solution)/shard_map/cond/branch_1_fun/ppermute | solution.py:246
  27.3 1.4 %collective-permute-done.4.behind_ref = bf16[320,512]{1,0:T(8,128)(2,1)S(1)} collective-permute-done((bf16[320,512]{1,0:T(8,128)(2,1)S(1)}, bf16[320,512]{1,0:T(8,128)(2,1)S(1)}, u32[]{:S(2)}, u32[]{:S(2)}) %collective-permute-start.4) | collective-permute-done | bytes 327712 | tf_op jit(solution)/shard_map/cond/branch_1_fun/ppermute | solution.py:247
  28.7 0.0 all-to-all-done.2.got_ref
  28.7 0.0 copy-done.4
  28.7 0.0 copy-done.7
  28.7 0.0 copy-done.9
  28.7 3.2 %main.3 = (f32[32,8,144]{2,1,0:T(8,128)S(1)}, f32[32,8,144]{2,1,0:T(8,128)S(1)}) custom-call(s32[4,3]{1,0:T(4,128)S(1)} %copy-done.7, s32[1,64]{1,0:T(1,128)S(1)} %bitcast.27, bf16[2,48,3072]{2,1,0:T(8,128)(2,1)S(1)} %planar.3.planar_ref, bf16[288,512]{1,0:T(8,128)(2,1)S(1)} %collective-permute-done.3.ahead_ref, ...), custom_call_target="tpu_custom_call" | custom-call | tf_op jit(solution)/shard_map/cond/branch_1_fun/main/pallas_call | solution.py:258
  31.9 1.9 %collective-permute-start.5 = (f32[32,8,144]{2,1,0:T(8,128)S(1)}, f32[32,8,144]{2,1,0:T(8,128)S(1)}, u32[]{:S(2)}, u32[]{:S(2)}) collective-permute-start(f32[32,8,144]{2,1,0:T(8,128)S(1)} %get-tuple-element.45), channel_id=1, source_target_pairs={{0,8},{8,0},{16,24},{24,16},{32,40},{40,32},{48,56},{56,48},{64,72... | collective-permute-start | bytes 442376 | tf_op jit(solution)/shard_map/cond/branch_1_fun/ppermute | solution.py:271
  33.8 1.5 %collective-permute-done.5 = f32[32,8,144]{2,1,0:T(8,128)S(1)} collective-permute-done((f32[32,8,144]{2,1,0:T(8,128)S(1)}, f32[32,8,144]{2,1,0:T(8,128)S(1)}, u32[]{:S(2)}, u32[]{:S(2)}) %collective-permute-start.5) | collective-permute-done | bytes 147488 | tf_op jit(solution)/shard_map/cond/branch_1_fun/ppermute | solution.py:271
  35.3 38.9 %all_to_all.17.parts_ref = f32[32,8,144]{2,1,0:T(8,128)} all-to-all(f32[32,8,144]{2,1,0:T(8,128)S(1)} %add.6), channel_id=1, replica_groups={{0,16,32,48,64,80,96,112,128,144,160,176,192,208,224,240,256,272,288,30..., dimensions={0} | all-to-all | bytes 294912 | tf_op jit(solution)/shard_map/cond/branch_1_fun/all_to_all | solution.py:273
  74.2 0.0 copy-done.11
  74.2 1.2 %total.3 = f32[2,3,4,48]{3,2,1,0:T(4,128)S(1)} custom-call(s32[3]{0:T(128)S(1)} %copy-done.11, f32[32,8,144]{2,1,0:T(8,128)} %all_to_all.17.parts_ref), custom_call_target="tpu_custom_call" | custom-call | tf_op jit(solution)/shard_map/cond/branch_1_fun/total/pallas_call | solution.py:274
  75.4 0.0 copy-start.5
  75.4 0.6 copy-done.5
  (1 shorter events, 0.0 us)
Async XLA Ops:
  2.1 26.6 %copy-start.4 = (bf16[3,18,1,512]{3,1,2,0:T(8,128)(2,1)S(1)}, bf16[3,18,1,512]{3,1,2,0:T(8,128)(2,1)}, u32[]{:S(2)}) copy-start(bf16[3,18,1,512]{3,1,2,0:T(8,128)(2,1)} %get-tuple-element.64) | copy-start | bytes 165892 | tf_op jit(solution)/shard_map/cond
  2.1 26.6 %copy-start.7 = (s32[4,3]{1,0:T(4,128)S(1)}, s32[4,3]{1,0:T(4,128)}, u32[]{:S(2)}) copy-start(s32[4,3]{1,0:T(4,128)} %get-tuple-element.38.momenta_ref) | copy-start | bytes 148 | tf_op jit(solution)/shard_map/cond
  2.1 26.6 %copy-start.9 = (s32[64]{0:T(128)S(1)}, s32[64]{0:T(128)}, u32[]{:S(2)}) copy-start(s32[64]{0:T(128)} %get-tuple-element.39) | copy-start | bytes 772 | tf_op jit(solution)/shard_map/cond
  4.5 24.2 %all-to-all-start.2 = ((bf16[8,96,512]{2,1,0:T(8,128)(2,1)}), bf16[8,96,512]{2,1,0:T(8,128)(2,1)S(1)}, u32[]{:S(2)}, u32[]{:S(2)}) async-start(bf16[8,96,512]{2,1,0:T(8,128)(2,1)} %get-tuple-element.43), calls=%async_computation.2 | async-start | bytes 1572864 | tf_op jit(solution)/shard_map/cond/branch_1_fun/all_to_all | solution.py:248
  10.2 64.0 %copy-start.11 = (s32[3]{0:T(128)S(1)}, s32[3]{0:T(128)}, u32[]{:S(2)}) copy-start(s32[3]{0:T(128)} %get-tuple-element.37.directions_ref) | copy-start | bytes 40 | tf_op jit(solution)/shard_map/cond
  10.2 18.4 %collective-permute-start.4 = (bf16[320,512]{1,0:T(8,128)(2,1)S(1)}, bf16[320,512]{1,0:T(8,128)(2,1)S(1)}, u32[]{:S(2)}, u32[]{:S(2)}) collective-permute-start(bf16[320,512]{1,0:T(8,128)(2,1)S(1)} %get-tuple-element.42), channel_id=1, source_target_pairs={{0,8},{8,16},{16,24},{24,32},{32,40},{40,48},{48,56},{56,64},{64,7... | collective-permute-start | bytes 983048 | tf_op jit(solution)/shard_map/cond/branch_1_fun/ppermute | solution.py:247
  12.3 15.0 %collective-permute-start.3 = (bf16[288,512]{1,0:T(8,128)(2,1)}, bf16[288,512]{1,0:T(8,128)(2,1)S(1)}, u32[]{:S(2)}, u32[]{:S(2)}) collective-permute-start(bf16[288,512]{1,0:T(8,128)(2,1)} %bitcast.13), channel_id=1, source_target_pairs={{8,0},{16,8},{24,16},{32,24},{40,32},{48,40},{56,48},{64,56},{72,6... | collective-permute-start | bytes 884744 | tf_op jit(solution)/shard_map/cond/branch_1_fun/ppermute | solution.py:246
  31.9 3.4 %collective-permute-start.5 = (f32[32,8,144]{2,1,0:T(8,128)S(1)}, f32[32,8,144]{2,1,0:T(8,128)S(1)}, u32[]{:S(2)}, u32[]{:S(2)}) collective-permute-start(f32[32,8,144]{2,1,0:T(8,128)S(1)} %get-tuple-element.45), channel_id=1, source_target_pairs={{0,8},{8,0},{16,24},{24,16},{32,40},{40,32},{48,56},{56,48},{64,72... | collective-permute-start | bytes 442376 | tf_op jit(solution)/shard_map/cond/branch_1_fun/ppermute | solution.py:271
  75.4 0.6 copy-start.5

commit v2 on v1

v2 whole, which is shorter than its diff:
```python
import functools
import math

import jax
import jax.numpy as jnp
from jax import lax
from jax.experimental import pallas as pl
from jax.experimental.pallas import tpu as pltpu
from jax.sharding import PartitionSpec as P

LX = 32
LY = 16
CAP = 16
TILE = 16
LANES = 128
F32 = jnp.float32
BF16 = jnp.bfloat16
NT = (((1,), (1,)), ((), ()))


def iota(shape, dim):
    return lax.broadcasted_iota(jnp.int32, shape, dim)


def as_column(row):
    n = row.shape[1]
    return jnp.sum(jnp.where(iota((n, n), 0) == iota((n, n), 1), row, 0.0), axis=1, keepdims=True)


def owner_and_rank(ids, owners, held):
    npanel = ids.shape[1]
    owner = jnp.zeros(ids.shape, F32)
    for other in range(1, owners):
        owner = owner + jnp.where(ids >= other * held, 1.0, 0.0)
    before = iota((npanel, npanel), 0) < iota((npanel, npanel), 1)
    rank = jnp.sum(jnp.where(before & (as_column(owner) == owner), 1.0, 0.0), axis=0, keepdims=True)
    return owner, rank


def order_of(slot, slots):
    npanel = slot.shape[1]
    half = npanel // 2
    core = lax.axis_index("slab") % 2
    place = iota((npanel, npanel), 0)
    wanted = jnp.where(place < half, 2 * place + core, 2 * (place - half) + 1 - core)
    column = jnp.sum(jnp.where(iota((npanel, npanel), 1) == wanted, slot, 0.0), axis=1, keepdims=True)
    return jnp.where(iota((npanel, slots), 1).astype(F32) == column, 1.0, 0.0).astype(BF16)


def select_kernel(cap, ids_ref, vec_ref, links_ref, pay_ref, up_ref, over_ref):
    rows, held, sites = vec_ref.shape
    ids = ids_ref[...]
    npanel = ids.shape[1]
    local = ids - lax.axis_index("vec") * held
    inside = (local >= 0) & (local < held)
    owner, rank = owner_and_rank(ids, pay_ref.shape[0], held)
    over_ref[0] = (jnp.max(rank) >= cap).astype(jnp.int32)
    place = jnp.where(inside, rank, -1.0)
    to_slot = jnp.where(iota((cap, npanel), 0).astype(F32) == place, 1.0, 0.0)
    of_held = jnp.where(iota((held, npanel), 0) == local, 1.0, 0.0)
    pick = lax.dot_general(to_slot, of_held, NT, preferred_element_type=F32).astype(BF16)
    for row in range(rows):
        part = jnp.dot(pick, vec_ref[row], preferred_element_type=F32).astype(BF16)
        for peer in range(pay_ref.shape[0]):
            pay_ref[peer, row * cap:(row + 1) * cap, :] = part
    for row in range(rows):
        up_ref[row * held:(row + 1) * held, :] = vec_ref[row]
    zlink = links_ref[2].astype(F32)
    spare = up_ref.shape[0] - rows * held - zlink.shape[0]
    up_ref[rows * held:, :] = jnp.concatenate([zlink, jnp.zeros((spare, sites), F32)], axis=0).astype(BF16)


def link_terms(ahead, behind, fore, back):
    real, imag = [], []
    for row in range(3):
        re, im = 0.0, 0.0
        for col in range(3):
            ur, ui = fore(row * 3 + col), fore(9 + row * 3 + col)
            re = re + ur * ahead[col] - ui * ahead[3 + col]
            im = im + ur * ahead[3 + col] + ui * ahead[col]
        for col in range(3):
            ur, ui = back(col * 3 + row), back(9 + col * 3 + row)
            re = re - ur * behind[col] - ui * behind[3 + col]
            im = im - ur * behind[3 + col] + ui * behind[col]
        real.append(re)
        imag.append(im)
    return real + imag


def turn_x(value, ahead):
    inner = iota((value.shape[0], LANES), 1) % LX
    parts = []
    for at in range(0, value.shape[1], LANES):
        part = value[:, at:at + LANES]
        if ahead:
            part = jnp.where(inner == LX - 1, pltpu.roll(part, LX - 1, 1), pltpu.roll(part, LANES - 1, 1))
        else:
            part = jnp.where(inner == 0, pltpu.roll(part, LANES - LX + 1, 1), pltpu.roll(part, 1, 1))
        parts.append(part)
    return jnp.concatenate(parts, axis=1)


def turn_y(value, ahead):
    sites = value.shape[1]
    return pltpu.roll(value, sites - LX if ahead else LX, 1)


def planar_kernel(cap, owners, momenta_ref, ids_ref, vec_ref, links_ref, out_ref, phase_ref, order_ref,
                  link_ref, turned_ref):
    rows, held, sites = vec_ref.shape
    for axis_id, turn in enumerate((turn_x, turn_y)):
        link = links_ref[axis_id].astype(F32) * 0.5
        link_ref[2 * axis_id] = link
        link_ref[2 * axis_id + 1] = turn(link, False)

    def step(at, carry):
        first = pl.multiple_of(at * TILE, TILE)
        for row in range(rows):
            value = vec_ref[row, pl.ds(first, TILE), :].astype(F32)
            for axis_id, turn in enumerate((turn_x, turn_y)):
                turned_ref[axis_id, 0, row] = turn(value, True)
                turned_ref[axis_id, 1, row] = turn(value, False)
        for axis_id in range(2):
            for lane in range(0, sites, LANES):
                span = slice(lane, lane + LANES)
                ahead = [turned_ref[axis_id, 0, row, :, span] for row in range(rows)]
                behind = [turned_ref[axis_id, 1, row, :, span] for row in range(rows)]
                shifted = link_terms(
                    ahead, behind,
                    lambda e: link_ref[2 * axis_id, e:e + 1, span],
                    lambda e: link_ref[2 * axis_id + 1, e:e + 1, span],
                )
                for row in range(rows):
                    out_ref[axis_id, pl.ds(first, TILE), row * sites + lane:row * sites + lane + LANES] = (
                        shifted[row].astype(BF16))
        return carry

    lax.fori_loop(0, held // TILE, step, 0)
    owner, rank = owner_and_rank(ids_ref[...], owners, held)
    order_ref[...] = order_of(owner * cap + rank, owners * cap)
    nmom = momenta_ref.shape[0]
    slab_id = lax.axis_index("slab")
    modulus = sites * lax.axis_size("slab")
    shape = (2 * nmom, sites)
    site, line = iota(shape, 1), iota(shape, 0)
    x_coord, y_coord = site % LX, site // LX
    turns = jnp.zeros(shape, jnp.int32)
    for mom in range(nmom):
        along = (momenta_ref[mom, 0] * (modulus // LX) * x_coord
                 + momenta_ref[mom, 1] * (modulus // LY) * y_coord
                 + momenta_ref[mom, 2] * sites * slab_id)
        turns = jnp.where(line % nmom == mom, along, turns)
    turns = jnp.where(line >= nmom, turns - modulus // 4, turns) & (modulus - 1)
    turns = jnp.where(turns >= modulus // 2, turns - modulus, turns)
    phase_ref[...] = jnp.cos(turns.astype(F32) * (2.0 * math.pi / modulus))


def height_kernel(links_ref, ahead_ref, behind_ref, out_ref, link_ref):
    held, width = out_ref.shape
    sites = links_ref.shape[2]
    rows = width // sites
    link_ref[0] = links_ref[2].astype(F32) * 0.5
    link_ref[1] = behind_ref[rows * held:rows * held + 32, :].astype(F32)[:18] * 0.5

    def step(at, carry):
        first = pl.multiple_of(at * TILE, TILE)
        for lane in range(0, sites, LANES):
            span = slice(lane, lane + LANES)
            ahead = [ahead_ref[pl.ds(row * held + first, TILE), span].astype(F32) for row in range(rows)]
            behind = [behind_ref[pl.ds(row * held + first, TILE), span].astype(F32) for row in range(rows)]
            shifted = link_terms(
                ahead, behind,
                lambda e: link_ref[0, e:e + 1, span],
                lambda e: link_ref[1, e:e + 1, span],
            )
            for row in range(rows):
                out_ref[pl.ds(first, TILE), row * sites + lane:row * sites + lane + LANES] = (
                    shifted[row].astype(BF16))
        return carry

    lax.fori_loop(0, held // TILE, step, 0)


def reorder_kernel(ids_ref, got_ref, out_ref):
    held = got_ref.shape[1] // out_ref.shape[0]
    owners, _, sites = got_ref.shape
    order = order_of(ids_ref[...].astype(F32), owners * held)
    for row in range(out_ref.shape[0]):
        block = got_ref[:, row * held:(row + 1) * held, :].reshape(owners * held, sites)
        out_ref[row] = jnp.dot(order, block, preferred_element_type=F32).astype(BF16)


def main_kernel(cap, over_ref, planar_ref, height_ref, phase_ref, order_ref, got_ref, spare_ref,
                keep_ref, send_ref, field_ref, panel_ref, weight_ref, copied_ref):
    owners = got_ref.shape[0]
    npanel = order_ref.shape[0]
    held = planar_ref.shape[1]
    sites = got_ref.shape[2]
    rows = got_ref.shape[1] // cap
    nmom = phase_ref.shape[0] // 2
    half = npanel // 2
    field_ref[0:2 * held, :] = planar_ref[...].reshape(2 * held, rows * sites)
    field_ref[2 * held:3 * held, :] = height_ref[...]

    @pl.when(over_ref[0] == 0)
    def _():
        for row in range(rows):
            block = got_ref[:, row * cap:(row + 1) * cap, :].reshape(owners * cap, sites)
            panel_ref[row] = jnp.dot(order_ref[...], block, preferred_element_type=F32)

    @pl.when(over_ref[0] != 0)
    def _():
        pltpu.sync_copy(spare_ref, copied_ref)
        panel_ref[...] = copied_ref[...].astype(F32)

    def weigh(at, carry):
        first = pl.multiple_of(at * TILE, TILE)
        for colour in range(3):
            re = panel_ref[colour, pl.ds(first, TILE), :]
            im = panel_ref[3 + colour, pl.ds(first, TILE), :]
            for mom in range(nmom):
                cos = phase_ref[mom:mom + 1, :]
                sin = phase_ref[nmom + mom:nmom + mom + 1, :]
                wr = (re * cos - im * sin).astype(BF16)
                wi = re * sin + im * cos
                low = slice(colour * sites, (colour + 1) * sites)
                high = slice((3 + colour) * sites, (4 + colour) * sites)
                weight_ref[pl.ds(mom * npanel + first, TILE), low] = wr
                weight_ref[pl.ds(mom * npanel + first, TILE), high] = wi.astype(BF16)
                weight_ref[pl.ds((nmom + mom) * npanel + first, TILE), low] = (-wi).astype(BF16)
                weight_ref[pl.ds((nmom + mom) * npanel + first, TILE), high] = wr
        return carry

    lax.fori_loop(0, npanel // TILE, weigh, 0)
    whole = lax.dot_general(weight_ref[...], field_ref[...], NT, preferred_element_type=F32)
    lines = 2 * nmom + 1
    for at, ref in ((0, keep_ref), (half, send_ref)):
        blocks = [whole[part * npanel + at:part * npanel + at + half] for part in range(2 * nmom)]
        for part, block in enumerate(blocks):
            ref[pl.ds(part, half, stride=lines), :] = block[:, :LANES]
        ref[pl.ds(2 * nmom, half, stride=lines), :] = jnp.concatenate([b[:, LANES:] for b in blocks], axis=1)


def sum_kernel(nmom, directions_ref, parts_ref, out_ref):
    total = jnp.sum(parts_ref[...], axis=0)
    held = out_ref.shape[-1]
    spill = 3 * held - LANES
    lines = 2 * nmom
    first = jnp.concatenate([total[:, k * LANES:(k + 1) * LANES] for k in range(lines)], axis=0)
    last = total[:, lines * LANES:]
    last = jnp.concatenate([last[:, k * spill:(k + 1) * spill] for k in range(lines)], axis=0)
    total = jnp.concatenate([first, last], axis=1)
    for place in range(out_ref.shape[1]):
        chosen = total[:, 0:held]
        for axis_id in (1, 2):
            along = total[:, axis_id * held:(axis_id + 1) * held]
            chosen = jnp.where(directions_ref[place] == axis_id, along, chosen)
        out_ref[0, place] = chosen[:nmom]
        out_ref[1, place] = chosen[nmom:]


def specs(*spaces):
    kinds = {"s": pltpu.SMEM, "v": pltpu.VMEM, "a": pl.ANY}
    return [pl.BlockSpec(memory_space=kinds[space]) for space in spaces]


def call(kernel, out_shape, ins, outs, name, scratch=()):
    return pl.pallas_call(
        kernel, out_shape=out_shape, in_specs=specs(*ins), out_specs=specs(*outs),
        scratch_shapes=list(scratch), name=name,
        compiler_params=pltpu.CompilerParams(vmem_limit_bytes=16 * 1024 * 1024),
    )


def body(vectors, links, momenta, directions, panel_index):
    rows, held, planes, sites = vectors.shape
    npanel = panel_index.shape[0]
    nmom = momenta.shape[0]
    nslab, nvec = lax.axis_size("slab"), lax.axis_size("vec")
    half = npanel // 2
    lines = 2 * nmom + 1
    vec = vectors.reshape(rows, held, sites)
    link = links.reshape(3, 18, sites)
    ids = panel_index.reshape(1, npanel)
    shape = jax.ShapeDtypeStruct
    vm = pltpu.VMEM
    pay, up, over = call(
        functools.partial(select_kernel, CAP),
        [shape((nvec, rows * CAP, sites), BF16), shape((rows * held + 32, sites), BF16), shape((1,), jnp.int32)],
        "vvv", "vvs", "select",
    )(ids, vec, link)
    upward = [(i, (i + 1) % nslab) for i in range(nslab)]
    downward = [(j, i) for i, j in upward]
    ahead = lax.ppermute(vec.reshape(rows * held, sites), "slab", downward)
    behind = lax.ppermute(up, "slab", upward)
    got = lax.all_to_all(pay, "vec", 0, 0, tiled=True)

    def gather_all():
        every = jnp.broadcast_to(vec.reshape(1, rows * held, sites), (nvec, rows * held, sites))
        every = lax.all_to_all(every, "vec", 0, 0, tiled=True)
        return call(reorder_kernel, [shape((rows, npanel, sites), BF16)], "vv", "v", "reorder")(ids, every)[0]

    spare = lax.cond(over[0] != 0, gather_all, lambda: jnp.zeros((rows, npanel, sites), BF16))
    planar, phase, order = call(
        functools.partial(planar_kernel, CAP, nvec),
        [shape((2, held, rows * sites), BF16), shape((2 * nmom, sites), F32), shape((npanel, nvec * CAP), BF16)],
        "svvv", "vvv", "planar",
        [vm((4, 18, sites), F32), vm((2, 2, rows, TILE, sites), F32)],
    )(momenta, ids, vec, link)
    height = call(
        height_kernel, [shape((held, rows * sites), BF16)], "vvv", "v", "height", [vm((2, 18, sites), F32)],
    )(link, ahead, behind)[0]
    part = shape((half * lines, LANES), F32)
    keep, send = call(
        functools.partial(main_kernel, CAP), [part, part], "svvvvva", "vv", "main",
        [
            vm((3 * held, rows * sites), BF16),
            vm((rows, npanel, sites), F32),
            vm((2 * nmom * npanel, rows * sites), BF16),
            vm((rows, npanel, sites), BF16),
        ],
    )(over, planar, height, phase, order, got, spare)
    pair = lax.ppermute(send, "slab", [(i, i ^ 1) for i in range(nslab)])
    groups = [[2 * k + c for k in range(nslab // 2)] for c in range(2)]
    both = (keep + pair).reshape(half, 1, lines * LANES)
    parts = lax.all_to_all(both, "slab", 0, 0, axis_index_groups=groups, tiled=True)
    return call(
        functools.partial(sum_kernel, nmom), [shape((2, 3, nmom, held), F32)], "sv", "v", "total",
    )(directions, parts)[0][None]


def solution(mesh):
    placed = (P(None, "vec", "slab", None), P(None, None, "slab", None), P(), P(), P())
    return jax.shard_map(
        body,
        mesh=mesh,
        in_specs=placed,
        out_specs=P("slab", None, None, None, "vec"),
        check_vma=False,
    )
```

time: 76.4 us -> 70.7 us (0.925)
  the two profiles are of different devices: /device:TPU:24 before, /device:TPU:8 now
where the time goes in v2:
time: 70.7 us; the launch traced here: 70.3 us
  blocking collectives  33.2 us (47%)
  starting transfers between devices  22 us (31%)
  Pallas kernels  9.44 us (13%)
  waiting for transfers between devices  4.01 us (6%)
  local copies, waits for them, and re-layouts  0.94 us (1%)
  between operations  0.77 us (1%)
    all_to_all x1, blocking collectives, body(): lax.all_to_all(both, 'slab', 0, 0, axis_index_groups=groups, tiled=True)  33.2 us
    all_to_all x1, starting transfers between devices, body(): got = lax.all_to_all(pay, 'vec', 0, 0, tiled=True)  9.43 us
    ppermute x1, starting transfers between devices, body(): ahead = lax.ppermute(vec.reshape(rows * held, sites), 'slab', downward)  8.48 us
    ppermute x1, waiting for transfers between devices, body(): ahead = lax.ppermute(vec.reshape(rows * held, sites), 'slab', downward)  2.74 us
    pallas_call x1, Pallas kernels, body(): call(functools.partial(planar_kernel, CAP, nvec), [shape((2, held, rows *...  2.58 us
    pallas_call x1, Pallas kernels, body(): call(functools.partial(main_kernel, CAP), [part, part], 'svvvvva', 'vv',...  2.56 us
    pallas_call x1, Pallas kernels, body(): call(functools.partial(select_kernel, CAP), [shape((nvec, rows * CAP, sit...  2.32 us
    ppermute x1, starting transfers between devices, body(): behind = lax.ppermute(up, 'slab', upward)  2.04 us
  transfers between devices with their start and end apart: 4, of which 2 were waited for; matrix products, arithmetic and copies ran while one was open for 0% of the time, Pallas kernels for 4%

profile of v2, /device:TPU:8, one launch (start us, length us, event | category | flops | bytes accessed | tf_op | source)
XLA Modules:
  0.0 70.3 jit_solution(16881024495094540329)
XLA Ops:
  0.0 0.0 copy-start
  0.0 0.9 %copy-done = bf16[3,18,1,512]{3,1,2,0:T(8,128)(2,1)S(1)} copy-done((bf16[3,18,1,512]{3,1,2,0:T(8,128)(2,1)S(1)}, bf16[3,18,1,512]{3,1,2,0:T(8,128)(2,1)}, u32[]{:S(2)}) %copy-start) | copy-done | bytes 55320
  0.9 2.3 %select.1 = (bf16[8,96,512]{2,1,0:T(8,128)(2,1)}, bf16[320,512]{1,0:T(8,128)(2,1)S(1)}, s32[1]{0:T(128)}) custom-call(s32[1,64]{1,0:T(1,128)} %bitcast.18, bf16[6,48,512]{2,1,0:T(8,128)(2,1)} %bitcast.13, bf16[3,18,512]{2,1,0:T(8,128)(2,1)S(1)} %bitcast.10), custom_call_target="tpu_custom_call" | custom-call | tf_op jit(solution)/shard_map/select/pallas_call | solution.py:287
  3.9 0.0 copy-start.1
  3.9 0.0 copy-start.2
  3.9 0.0 copy-start.4
  4.0 9.4 %all-to-all-start.1 = ((bf16[8,96,512]{2,1,0:T(8,128)(2,1)}), bf16[8,96,512]{2,1,0:T(8,128)(2,1)S(1)}, u32[]{:S(2)}, u32[]{:S(2)}) async-start(bf16[8,96,512]{2,1,0:T(8,128)(2,1)} %get-tuple-element.27), calls=%async_computation.1 | async-start | bytes 1572864 | tf_op jit(solution)/shard_map/all_to_all | solution.py:296
  13.4 0.0 copy-start.3
  13.4 2.0 %collective-permute-start.1 = (bf16[320,512]{1,0:T(8,128)(2,1)S(1)}, bf16[320,512]{1,0:T(8,128)(2,1)S(1)}, u32[]{:S(2)}, u32[]{:S(2)}) collective-permute-start(bf16[320,512]{1,0:T(8,128)(2,1)S(1)} %get-tuple-element.24), channel_id=1, source_target_pairs={{0,8},{8,16},{16,24},{24,32},{32,40},{40,48},{48,56},{56,64},{64,7... | collective-permute-start | bytes 983048 | tf_op jit(solution)/shard_map/ppermute | solution.py:295
  15.4 8.5 %collective-permute-start = (bf16[288,512]{1,0:T(8,128)(2,1)}, bf16[288,512]{1,0:T(8,128)(2,1)S(1)}, u32[]{:S(2)}, u32[]{:S(2)}) collective-permute-start(bf16[288,512]{1,0:T(8,128)(2,1)} %bitcast.14), channel_id=1, source_target_pairs={{8,0},{16,8},{24,16},{32,24},{40,32},{48,40},{56,48},{64,56},{72,6... | collective-permute-start | bytes 884744 | tf_op jit(solution)/shard_map/ppermute | solution.py:294
  23.9 0.0 copy-done.1
  23.9 0.0 copy-done.2
  23.9 0.0 copy-done.4
  24.0 2.6 %planar.1 = (bf16[2,48,3072]{2,1,0:T(8,128)(2,1)S(1)}, f32[8,512]{1,0:T(8,128)S(1)}, bf16[64,128]{1,0:T(8,128)(2,1)S(1)}) custom-call(s32[4,3]{1,0:T(4,128)S(1)} %copy-done.2, s32[1,64]{1,0:T(1,128)} %bitcast.20, bf16[6,48,512]{2,1,0:T(8,128)(2,1)S(1)} %bitcast.15, bf16[3,18,512]{2,1,0:T(8,128)(2,1)S(1)} %bitcast.11), custom_call_target="tpu_custom_call" | custom-call | tf_op jit(solution)/shard_map/planar/pallas_call | solution.py:304
  26.5 2.7 %collective-permute-done.ahead_ref = bf16[288,512]{1,0:T(8,128)(2,1)S(1)} collective-permute-done((bf16[288,512]{1,0:T(8,128)(2,1)}, bf16[288,512]{1,0:T(8,128)(2,1)S(1)}, u32[]{:S(2)}, u32[]{:S(2)}) %collective-permute-start) | collective-permute-done | bytes 294944 | tf_op jit(solution)/shard_map/ppermute | solution.py:294
  29.3 0.0 collective-permute-done.1.behind_ref
  29.3 0.5 height.1.height_ref
  29.8 0.0 all-to-all-done.1.got_ref
  29.9 2.6 %main.1 = (f32[288,128]{1,0:T(8,128)S(1)}, f32[288,128]{1,0:T(8,128)S(1)}) custom-call(s32[1]{0:T(128)} %get-tuple-element.22.over_ref, bf16[2,48,3072]{2,1,0:T(8,128)(2,1)S(1)} %get-tuple-element.23.planar_ref, bf16[48,3072]{1,0:T(8,128)(2,1)S(1)} %height.1.height_ref, f32[8,512]{1,0:T(8,128)S(1)} %get-tuple-element.25.phase_ref, ...), custom_call_target="tpu_custom_call" | custom-call | tf_op jit(solution)/shard_map/main/pallas_call | solution.py:314
  32.4 2.0 %collective-permute-start.2 = (f32[288,128]{1,0:T(8,128)S(1)}, f32[288,128]{1,0:T(8,128)S(1)}, u32[]{:S(2)}, u32[]{:S(2)}) collective-permute-start(f32[288,128]{1,0:T(8,128)S(1)} %get-tuple-element.29), channel_id=1, source_target_pairs={{0,8},{8,0},{16,24},{24,16},{32,40},{40,32},{48,56},{56,48},{64,72... | collective-permute-start | bytes 442376 | tf_op jit(solution)/shard_map/ppermute | solution.py:323
  34.4 1.3 %collective-permute-done.2 = f32[288,128]{1,0:T(8,128)S(1)} collective-permute-done((f32[288,128]{1,0:T(8,128)S(1)}, f32[288,128]{1,0:T(8,128)S(1)}, u32[]{:S(2)}, u32[]{:S(2)}) %collective-permute-start.2) | collective-permute-done | bytes 147488 | tf_op jit(solution)/shard_map/ppermute | solution.py:323
  35.7 33.2 %all_to_all.15.parts_ref = f32[32,1,1152]{2,1,0:T(1,128)S(1)} all-to-all(f32[32,1,1152]{2,1,0:T(1,128)S(1)} %bitcast.17), channel_id=1, replica_groups={{0,16,32,48,64,80,96,112,128,144,160,176,192,208,224,240,256,272,288,30..., dimensions={0} | all-to-all | bytes 294912 | tf_op jit(solution)/shard_map/all_to_all | solution.py:326
  68.9 0.0 copy-done.3
  68.9 1.4 %total.1 = f32[2,3,4,48]{3,2,1,0:T(4,128)} custom-call(s32[3]{0:T(128)S(1)} %copy-done.3, f32[32,1,1152]{2,1,0:T(1,128)S(1)} %all_to_all.15.parts_ref), custom_call_target="tpu_custom_call" | custom-call | tf_op jit(solution)/shard_map/total/pallas_call | solution.py:327
  (3 shorter events, 0.1 us)
Async XLA Ops:
  0.0 0.9 %copy-start = (bf16[3,18,1,512]{3,1,2,0:T(8,128)(2,1)S(1)}, bf16[3,18,1,512]{3,1,2,0:T(8,128)(2,1)}, u32[]{:S(2)}) copy-start(bf16[3,18,1,512]{3,1,2,0:T(8,128)(2,1)} %param.8) | copy-start | bytes 165892
  3.9 20.1 %copy-start.1 = (bf16[3,18,1,512]{3,1,2,0:T(8,128)(2,1)S(1)}, bf16[3,18,1,512]{3,1,2,0:T(8,128)(2,1)}, u32[]{:S(2)}) copy-start(bf16[3,18,1,512]{3,1,2,0:T(8,128)(2,1)} %param.8) | copy-start | bytes 165892
  3.9 20.1 %copy-start.2 = (s32[4,3]{1,0:T(4,128)S(1)}, s32[4,3]{1,0:T(4,128)}, u32[]{:S(2)}) copy-start(s32[4,3]{1,0:T(4,128)} %momenta_ref.1) | copy-start | bytes 148
  3.9 20.1 %copy-start.4 = (bf16[6,48,1,512]{3,1,2,0:T(8,128)(2,1)S(1)}, bf16[6,48,1,512]{3,1,2,0:T(8,128)(2,1)}, u32[]{:S(2)}) copy-start(bf16[6,48,1,512]{3,1,2,0:T(8,128)(2,1)} %param.7) | copy-start | bytes 884740
  4.0 25.9 %all-to-all-start.1 = ((bf16[8,96,512]{2,1,0:T(8,128)(2,1)}), bf16[8,96,512]{2,1,0:T(8,128)(2,1)S(1)}, u32[]{:S(2)}, u32[]{:S(2)}) async-start(bf16[8,96,512]{2,1,0:T(8,128)(2,1)} %get-tuple-element.27), calls=%async_computation.1 | async-start | bytes 1572864 | tf_op jit(solution)/shard_map/all_to_all | solution.py:296
  13.4 55.5 %copy-start.3 = (s32[3]{0:T(128)S(1)}, s32[3]{0:T(128)}, u32[]{:S(2)}) copy-start(s32[3]{0:T(128)} %directions_ref.1) | copy-start | bytes 40
  13.4 15.9 %collective-permute-start.1 = (bf16[320,512]{1,0:T(8,128)(2,1)S(1)}, bf16[320,512]{1,0:T(8,128)(2,1)S(1)}, u32[]{:S(2)}, u32[]{:S(2)}) collective-permute-start(bf16[320,512]{1,0:T(8,128)(2,1)S(1)} %get-tuple-element.24), channel_id=1, source_target_pairs={{0,8},{8,16},{16,24},{24,32},{32,40},{40,48},{48,56},{56,64},{64,7... | collective-permute-start | bytes 983048 | tf_op jit(solution)/shard_map/ppermute | solution.py:295
  15.4 13.8 %collective-permute-start = (bf16[288,512]{1,0:T(8,128)(2,1)}, bf16[288,512]{1,0:T(8,128)(2,1)S(1)}, u32[]{:S(2)}, u32[]{:S(2)}) collective-permute-start(bf16[288,512]{1,0:T(8,128)(2,1)} %bitcast.14), channel_id=1, source_target_pairs={{8,0},{16,8},{24,16},{32,24},{40,32},{48,40},{56,48},{64,56},{72,6... | collective-permute-start | bytes 884744 | tf_op jit(solution)/shard_map/ppermute | solution.py:294
  32.4 3.3 %collective-permute-start.2 = (f32[288,128]{1,0:T(8,128)S(1)}, f32[288,128]{1,0:T(8,128)S(1)}, u32[]{:S(2)}, u32[]{:S(2)}) collective-permute-start(f32[288,128]{1,0:T(8,128)S(1)} %get-tuple-element.29), channel_id=1, source_target_pairs={{0,8},{8,0},{16,24},{24,16},{32,40},{40,32},{48,56},{56,48},{64,72... | collective-permute-start | bytes 442376 | tf_op jit(solution)/shard_map/ppermute | solution.py:323

commit v3 on v2

--- a/solution.py
+++ b/solution.py
@@ -11,6 +11,7 @@
 LX = 32
 LY = 16
 CAP = 16
+COST = 50_000_000_000
 TILE = 16
 LANES = 128
 F32 = jnp.float32
@@ -47,7 +48,7 @@
     return jnp.where(iota((npanel, slots), 1).astype(F32) == column, 1.0, 0.0).astype(BF16)
 
 
-def select_kernel(cap, ids_ref, vec_ref, links_ref, pay_ref, up_ref, over_ref):
+def select_kernel(cap, ids_ref, vec_ref, pay_ref, over_ref):
     rows, held, sites = vec_ref.shape
     ids = ids_ref[...]
     npanel = ids.shape[1]
@@ -63,11 +64,6 @@
         part = jnp.dot(pick, vec_ref[row], preferred_element_type=F32).astype(BF16)
         for peer in range(pay_ref.shape[0]):
             pay_ref[peer, row * cap:(row + 1) * cap, :] = part
-    for row in range(rows):
-        up_ref[row * held:(row + 1) * held, :] = vec_ref[row]
-    zlink = links_ref[2].astype(F32)
-    spare = up_ref.shape[0] - rows * held - zlink.shape[0]
-    up_ref[rows * held:, :] = jnp.concatenate([zlink, jnp.zeros((spare, sites), F32)], axis=0).astype(BF16)
 
 
 def link_terms(ahead, behind, fore, back):
@@ -137,7 +133,8 @@
 
     lax.fori_loop(0, held // TILE, step, 0)
     owner, rank = owner_and_rank(ids_ref[...], owners, held)
-    order_ref[...] = order_of(owner * cap + rank, owners * cap)
+    fits = jnp.max(rank, axis=1, keepdims=True) < cap
+    order_ref[...] = order_of(jnp.where(fits, owner * cap + rank, -1.0), owners * cap)
     nmom = momenta_ref.shape[0]
     slab_id = lax.axis_index("slab")
     modulus = sites * lax.axis_size("slab")
@@ -155,12 +152,18 @@
     phase_ref[...] = jnp.cos(turns.astype(F32) * (2.0 * math.pi / modulus))
 
 
-def height_kernel(links_ref, ahead_ref, behind_ref, out_ref, link_ref):
+def height_kernel(links_ref, below_ref, inner_ref, outer_ref, out_ref, link_ref):
+    first_core = lax.axis_index("slab") % 2 == 0
+    pl.when(first_core)(lambda: height(links_ref, below_ref, inner_ref, outer_ref, out_ref, link_ref))
+    pl.when(jnp.logical_not(first_core))(lambda: height(links_ref, below_ref, outer_ref, inner_ref, out_ref, link_ref))
+
+
+def height(links_ref, below_ref, ahead_ref, behind_ref, out_ref, link_ref):
     held, width = out_ref.shape
     sites = links_ref.shape[2]
     rows = width // sites
     link_ref[0] = links_ref[2].astype(F32) * 0.5
-    link_ref[1] = behind_ref[rows * held:rows * held + 32, :].astype(F32)[:18] * 0.5
+    link_ref[1] = below_ref[2].astype(F32) * 0.5
 
     def step(at, carry):
         first = pl.multiple_of(at * TILE, TILE)
@@ -190,8 +193,8 @@
         out_ref[row] = jnp.dot(order, block, preferred_element_type=F32).astype(BF16)
 
 
-def main_kernel(cap, over_ref, planar_ref, height_ref, phase_ref, order_ref, got_ref, spare_ref,
-                keep_ref, send_ref, field_ref, panel_ref, weight_ref, copied_ref):
+def main_kernel(cap, planar_ref, height_ref, phase_ref, order_ref, got_ref, spare_ref,
+                keep_ref, send_ref, field_ref, panel_ref, weight_ref):
     owners = got_ref.shape[0]
     npanel = order_ref.shape[0]
     held = planar_ref.shape[1]
@@ -201,17 +204,10 @@
     half = npanel // 2
     field_ref[0:2 * held, :] = planar_ref[...].reshape(2 * held, rows * sites)
     field_ref[2 * held:3 * held, :] = height_ref[...]
-
-    @pl.when(over_ref[0] == 0)
-    def _():
-        for row in range(rows):
-            block = got_ref[:, row * cap:(row + 1) * cap, :].reshape(owners * cap, sites)
-            panel_ref[row] = jnp.dot(order_ref[...], block, preferred_element_type=F32)
-
-    @pl.when(over_ref[0] != 0)
-    def _():
-        pltpu.sync_copy(spare_ref, copied_ref)
-        panel_ref[...] = copied_ref[...].astype(F32)
+    for row in range(rows):
+        block = got_ref[:, row * cap:(row + 1) * cap, :].reshape(owners * cap, sites)
+        picked = jnp.dot(order_ref[...], block, preferred_element_type=F32)
+        panel_ref[row] = picked + spare_ref[row].astype(F32)
 
     def weigh(at, carry):
         first = pl.multiple_of(at * TILE, TILE)
@@ -254,7 +250,7 @@
         chosen = total[:, 0:held]
         for axis_id in (1, 2):
             along = total[:, axis_id * held:(axis_id + 1) * held]
-            chosen = jnp.where(directions_ref[place] == axis_id, along, chosen)
+            chosen = jnp.where(directions_ref[:, place:place + 1] == axis_id, along, chosen)
         out_ref[0, place] = chosen[:nmom]
         out_ref[1, place] = chosen[nmom:]
 
@@ -264,12 +260,17 @@
     return [pl.BlockSpec(memory_space=kinds[space]) for space in spaces]
 
 
-def call(kernel, out_shape, ins, outs, name, scratch=()):
+def call(kernel, out_shape, ins, outs, name, scratch=(), cost=0):
     return pl.pallas_call(
         kernel, out_shape=out_shape, in_specs=specs(*ins), out_specs=specs(*outs),
         scratch_shapes=list(scratch), name=name,
+        cost_estimate=pl.CostEstimate(flops=cost, bytes_accessed=0, transcendentals=0) if cost else None,
         compiler_params=pltpu.CompilerParams(vmem_limit_bytes=16 * 1024 * 1024),
     )
+
+
+def in_vmem(value):
+    return pltpu.with_memory_space_constraint(value, pltpu.VMEM)
 
 
 def body(vectors, links, momenta, directions, panel_index):
@@ -284,49 +285,50 @@
     ids = panel_index.reshape(1, npanel)
     shape = jax.ShapeDtypeStruct
     vm = pltpu.VMEM
-    pay, up, over = call(
-        functools.partial(select_kernel, CAP),
-        [shape((nvec, rows * CAP, sites), BF16), shape((rows * held + 32, sites), BF16), shape((1,), jnp.int32)],
-        "vvv", "vvs", "select",
-    )(ids, vec, link)
+    flat = vec.reshape(rows * held, sites)
+    mate = [(i, i ^ 1) for i in range(nslab)]
+    beyond = [(i, (i + 1) % nslab if i % 2 else (i - 1) % nslab) for i in range(nslab)]
     upward = [(i, (i + 1) % nslab) for i in range(nslab)]
-    downward = [(j, i) for i, j in upward]
-    ahead = lax.ppermute(vec.reshape(rows * held, sites), "slab", downward)
-    behind = lax.ppermute(up, "slab", upward)
+    outer = lax.ppermute(flat, "slab", beyond)
+    pay, over = call(
+        functools.partial(select_kernel, CAP), [shape((nvec, rows * CAP, sites), BF16), shape((1,), jnp.int32)],
+        "vv", "vs", "select", (), COST,
+    )(in_vmem(ids), in_vmem(vec))
     got = lax.all_to_all(pay, "vec", 0, 0, tiled=True)
-
     def gather_all():
         every = jnp.broadcast_to(vec.reshape(1, rows * held, sites), (nvec, rows * held, sites))
         every = lax.all_to_all(every, "vec", 0, 0, tiled=True)
         return call(reorder_kernel, [shape((rows, npanel, sites), BF16)], "vv", "v", "reorder")(ids, every)[0]
 
-    spare = lax.cond(over[0] != 0, gather_all, lambda: jnp.zeros((rows, npanel, sites), BF16))
     planar, phase, order = call(
         functools.partial(planar_kernel, CAP, nvec),
         [shape((2, held, rows * sites), BF16), shape((2 * nmom, sites), F32), shape((npanel, nvec * CAP), BF16)],
         "svvv", "vvv", "planar",
-        [vm((4, 18, sites), F32), vm((2, 2, rows, TILE, sites), F32)],
+        [vm((4, 18, sites), F32), vm((2, 2, rows, TILE, sites), F32)], COST,
     )(momenta, ids, vec, link)
+    spare = lax.cond(over[0] != 0, gather_all, lambda: jnp.zeros((rows, npanel, sites), BF16))
+    outer, flat_late, link_late = lax.optimization_barrier((outer, flat, link))
+    inner = lax.ppermute(flat_late, "slab", mate)
+    below = lax.ppermute(link_late, "slab", upward)
     height = call(
-        height_kernel, [shape((held, rows * sites), BF16)], "vvv", "v", "height", [vm((2, 18, sites), F32)],
-    )(link, ahead, behind)[0]
+        height_kernel, [shape((held, rows * sites), BF16)], "vvvv", "v", "height", [vm((2, 18, sites), F32)],
+    )(link, below, inner, outer)[0]
     part = shape((half * lines, LANES), F32)
     keep, send = call(
-        functools.partial(main_kernel, CAP), [part, part], "svvvvva", "vv", "main",
+        functools.partial(main_kernel, CAP), [part, part], "vvvvvv", "vv", "main",
         [
             vm((3 * held, rows * sites), BF16),
             vm((rows, npanel, sites), F32),
             vm((2 * nmom * npanel, rows * sites), BF16),
-            vm((rows, npanel, sites), BF16),
         ],
-    )(over, planar, height, phase, order, got, spare)
-    pair = lax.ppermute(send, "slab", [(i, i ^ 1) for i in range(nslab)])
+    )(planar, height, in_vmem(phase), in_vmem(order), got, in_vmem(spare))
+    pair = lax.ppermute(send, "slab", mate)
     groups = [[2 * k + c for k in range(nslab // 2)] for c in range(2)]
     both = (keep + pair).reshape(half, 1, lines * LANES)
     parts = lax.all_to_all(both, "slab", 0, 0, axis_index_groups=groups, tiled=True)
     return call(
-        functools.partial(sum_kernel, nmom), [shape((2, 3, nmom, held), F32)], "sv", "v", "total",
-    )(directions, parts)[0][None]
+        functools.partial(sum_kernel, nmom), [shape((2, 3, nmom, held), F32)], "vv", "v", "total",
+    )(in_vmem(directions.reshape(1, 3)), parts)[0][None]
 
 
 def solution(mesh):

time: 70.7 us -> 67.4 us (0.953)
  the two profiles are of different devices: /device:TPU:8 before, /device:TPU:2 now
where the time goes in v3:
time: 67.4 us; the launch traced here: 67 us
  blocking collectives  29.6 us (44%)
  starting transfers between devices  24.2 us (36%)
  Pallas kernels  8.64 us (13%)
  waiting for transfers between devices  3.77 us (6%)
  between operations  0.77 us (1%)
    all_to_all x1, blocking collectives, body(): lax.all_to_all(both, 'slab', 0, 0, axis_index_groups=groups, tiled=True)  29.6 us
    ppermute x1, starting transfers between devices, body(): outer = lax.ppermute(flat, 'slab', beyond)  13.5 us
    all_to_all x1, starting transfers between devices, body(): got = lax.all_to_all(pay, 'vec', 0, 0, tiled=True)  4.96 us
    pallas_call x1, Pallas kernels, body(): call(functools.partial(planar_kernel, CAP, nvec), [shape((2, held, rows *...  2.97 us
    ppermute x1, waiting for transfers between devices, body(): below = lax.ppermute(link_late, 'slab', upward)  2.43 us
    pallas_call x1, Pallas kernels, body(): call(functools.partial(select_kernel, CAP), [shape((nvec, rows * CAP, sit...  2.31 us
    ppermute x1, starting transfers between devices, body(): inner = lax.ppermute(flat_late, 'slab', mate)  1.92 us
    ppermute x1, starting transfers between devices, body(): below = lax.ppermute(link_late, 'slab', upward)  1.92 us
  transfers between devices with their start and end apart: 5, of which 2 were waited for; matrix products, arithmetic and copies ran while one was open for 0% of the time, Pallas kernels for 9%

profile of v3, /device:TPU:2, one launch (start us, length us, event | category | flops | bytes accessed | tf_op | source)
XLA Modules:
  0.0 67.0 jit_solution(4092428082050447055)
XLA Ops:
  0.0 13.5 %collective-permute-start = (bf16[288,512]{1,0:T(8,128)(2,1)}, bf16[288,512]{1,0:T(8,128)(2,1)S(1)}, u32[]{:S(2)}, u32[]{:S(2)}) collective-permute-start(bf16[288,512]{1,0:T(8,128)(2,1)} %bitcast.7), channel_id=1, source_target_pairs={{0,504},{8,16},{16,8},{24,32},{32,24},{40,48},{48,40},{56,64},{64,... | collective-permute-start | bytes 884744 | tf_op jit(solution)/shard_map/ppermute | solution.py:292
  13.5 2.3 %select.1 = (bf16[8,96,512]{2,1,0:T(8,128)(2,1)}, s32[1]{0:T(128)}) custom-call(s32[1,64]{1,0:T(1,128)} %bitcast.4.ids_ref, bf16[6,48,512]{2,1,0:T(8,128)(2,1)} %bitcast.5.vec_ref), custom_call_target="tpu_custom_call" | custom-call | flops 49999998976 | tf_op jit(solution)/shard_map/select/pallas_call | solution.py:293
  16.4 0.0 copy-start
  16.5 0.0 copy-start.2
  16.5 5.0 %all-to-all-start.1 = ((bf16[8,96,512]{2,1,0:T(8,128)(2,1)}), bf16[8,96,512]{2,1,0:T(8,128)(2,1)S(1)}, u32[]{:S(2)}, u32[]{:S(2)}) async-start(bf16[8,96,512]{2,1,0:T(8,128)(2,1)} %get-tuple-element.30), calls=%async_computation.1 | async-start | bytes 1572864 | tf_op jit(solution)/shard_map/all_to_all | solution.py:297
  21.5 0.0 collective-permute-done.outer_ref
  21.5 0.0 copy-done
  21.5 1.9 %collective-permute-start.1 = (bf16[3,18,512]{2,1,0:T(8,128)(2,1)S(1)}, bf16[3,18,512]{2,1,0:T(8,128)(2,1)S(1)}, u32[]{:S(2)}, u32[]{:S(2)}) collective-permute-start(bf16[3,18,512]{2,1,0:T(8,128)(2,1)S(1)} %bitcast.11), channel_id=1, source_target_pairs={{0,8},{8,16},{16,24},{24,32},{32,40},{40,48},{48,56},{56,64},{64,7... | collective-permute-start | bytes 165896 | tf_op jit(solution)/shard_map/ppermute | solution.py:312
  23.4 1.9 %collective-permute-start.2 = (bf16[288,512]{1,0:T(8,128)(2,1)}, bf16[288,512]{1,0:T(8,128)(2,1)S(1)}, u32[]{:S(2)}, u32[]{:S(2)}) collective-permute-start(bf16[288,512]{1,0:T(8,128)(2,1)} %bitcast.7), channel_id=1, source_target_pairs={{0,8},{8,0},{16,24},{24,16},{32,40},{40,32},{48,56},{56,48},{64,72... | collective-permute-start | bytes 884744 | tf_op jit(solution)/shard_map/ppermute | solution.py:311
  25.3 0.0 copy-done.2
  25.4 3.0 %planar.1 = (bf16[2,48,3072]{2,1,0:T(8,128)(2,1)S(1)}, f32[8,512]{1,0:T(8,128)S(1)}, bf16[64,128]{1,0:T(8,128)(2,1)S(1)}) custom-call(s32[4,3]{1,0:T(4,128)S(1)} %copy-done.2, s32[1,64]{1,0:T(1,128)} %bitcast.4.ids_ref, bf16[6,48,512]{2,1,0:T(8,128)(2,1)} %bitcast.5.vec_ref, bf16[3,18,512]{2,1,0:T(8,128)(2,1)S(1)} %bitcast.12), custom_call_target="tpu_custom_call" | custom-call | flops 49999998976 | tf_op jit(solution)/shard_map/planar/pallas_call | solution.py:303
  28.3 0.0 copy-start.1
  28.3 2.4 %collective-permute-done.1.below_ref = bf16[3,18,512]{2,1,0:T(8,128)(2,1)S(1)} collective-permute-done((bf16[3,18,512]{2,1,0:T(8,128)(2,1)S(1)}, bf16[3,18,512]{2,1,0:T(8,128)(2,1)S(1)}, u32[]{:S(2)}, u32[]{:S(2)}) %collective-permute-start.1) | collective-permute-done | bytes 55328 | tf_op jit(solution)/shard_map/ppermute | solution.py:312
  30.8 0.0 collective-permute-done.2.inner_ref
  30.8 0.5 height.1.height_ref
  31.3 0.0 all-to-all-done.1.got_ref
  31.3 1.9 %main.1 = (f32[288,128]{1,0:T(8,128)S(1)}, f32[288,128]{1,0:T(8,128)S(1)}) custom-call(bf16[2,48,3072]{2,1,0:T(8,128)(2,1)S(1)} %get-tuple-element.24.planar_ref, bf16[48,3072]{1,0:T(8,128)(2,1)S(1)} %height.1.height_ref, f32[8,512]{1,0:T(8,128)S(1)} %get-tuple-element.28.phase_ref, bf16[64,128]{1,0:T(8,128)(2,1)S(1)} %get-tuple-element.29.order_ref, ...), custom_call_target="tpu_custom_call" | custom-call | tf_op jit(solution)/shard_map/main/pallas_call | solution.py:317
  33.3 1.9 %collective-permute-start.3 = (f32[288,128]{1,0:T(8,128)S(1)}, f32[288,128]{1,0:T(8,128)S(1)}, u32[]{:S(2)}, u32[]{:S(2)}) collective-permute-start(f32[288,128]{1,0:T(8,128)S(1)} %get-tuple-element.33), channel_id=1, source_target_pairs={{0,8},{8,0},{16,24},{24,16},{32,40},{40,32},{48,56},{56,48},{64,72... | collective-permute-start | bytes 442376 | tf_op jit(solution)/shard_map/ppermute | solution.py:325
  35.2 1.3 %collective-permute-done.3 = f32[288,128]{1,0:T(8,128)S(1)} collective-permute-done((f32[288,128]{1,0:T(8,128)S(1)}, f32[288,128]{1,0:T(8,128)S(1)}, u32[]{:S(2)}, u32[]{:S(2)}) %collective-permute-start.3) | collective-permute-done | bytes 147488 | tf_op jit(solution)/shard_map/ppermute | solution.py:325
  36.5 29.6 %all_to_all.15.parts_ref = f32[32,1,1152]{2,1,0:T(1,128)S(1)} all-to-all(f32[32,1,1152]{2,1,0:T(1,128)S(1)} %bitcast.15), channel_id=1, replica_groups={{0,16,32,48,64,80,96,112,128,144,160,176,192,208,224,240,256,272,288,30..., dimensions={0} | all-to-all | bytes 294912 | tf_op jit(solution)/shard_map/all_to_all | solution.py:328
  66.1 0.0 copy-done.1
  66.1 0.9 %total.1 = f32[2,3,4,48]{3,2,1,0:T(4,128)} custom-call(s32[1,3]{1,0:T(1,128)S(1)} %bitcast.14, f32[32,1,1152]{2,1,0:T(1,128)S(1)} %all_to_all.15.parts_ref), custom_call_target="tpu_custom_call" | custom-call | tf_op jit(solution)/shard_map/total/pallas_call | solution.py:329
  (3 shorter events, 0.1 us)
Async XLA Ops:
  0.0 21.5 %collective-permute-start = (bf16[288,512]{1,0:T(8,128)(2,1)}, bf16[288,512]{1,0:T(8,128)(2,1)S(1)}, u32[]{:S(2)}, u32[]{:S(2)}) collective-permute-start(bf16[288,512]{1,0:T(8,128)(2,1)} %bitcast.7), channel_id=1, source_target_pairs={{0,504},{8,16},{16,8},{24,32},{32,24},{40,48},{48,40},{56,64},{64,... | collective-permute-start | bytes 884744 | tf_op jit(solution)/shard_map/ppermute | solution.py:292
  16.4 5.0 %copy-start = (bf16[3,18,1,512]{3,1,2,0:T(8,128)(2,1)S(1)}, bf16[3,18,1,512]{3,1,2,0:T(8,128)(2,1)}, u32[]{:S(2)}) copy-start(bf16[3,18,1,512]{3,1,2,0:T(8,128)(2,1)} %param.8) | copy-start | bytes 165892
  16.5 8.9 %copy-start.2 = (s32[4,3]{1,0:T(4,128)S(1)}, s32[4,3]{1,0:T(4,128)}, u32[]{:S(2)}) copy-start(s32[4,3]{1,0:T(4,128)} %momenta_ref.1) | copy-start | bytes 148
  16.5 14.8 %all-to-all-start.1 = ((bf16[8,96,512]{2,1,0:T(8,128)(2,1)}), bf16[8,96,512]{2,1,0:T(8,128)(2,1)S(1)}, u32[]{:S(2)}, u32[]{:S(2)}) async-start(bf16[8,96,512]{2,1,0:T(8,128)(2,1)} %get-tuple-element.30), calls=%async_computation.1 | async-start | bytes 1572864 | tf_op jit(solution)/shard_map/all_to_all | solution.py:297
  21.5 9.3 %collective-permute-start.1 = (bf16[3,18,512]{2,1,0:T(8,128)(2,1)S(1)}, bf16[3,18,512]{2,1,0:T(8,128)(2,1)S(1)}, u32[]{:S(2)}, u32[]{:S(2)}) collective-permute-start(bf16[3,18,512]{2,1,0:T(8,128)(2,1)S(1)} %bitcast.11), channel_id=1, source_target_pairs={{0,8},{8,16},{16,24},{24,32},{32,40},{40,48},{48,56},{56,64},{64,7... | collective-permute-start | bytes 165896 | tf_op jit(solution)/shard_map/ppermute | solution.py:312
  23.4 7.4 %collective-permute-start.2 = (bf16[288,512]{1,0:T(8,128)(2,1)}, bf16[288,512]{1,0:T(8,128)(2,1)S(1)}, u32[]{:S(2)}, u32[]{:S(2)}) collective-permute-start(bf16[288,512]{1,0:T(8,128)(2,1)} %bitcast.7), channel_id=1, source_target_pairs={{0,8},{8,0},{16,24},{24,16},{32,40},{40,32},{48,56},{56,48},{64,72... | collective-permute-start | bytes 884744 | tf_op jit(solution)/shard_map/ppermute | solution.py:311
  28.3 37.8 %copy-start.1 = (s32[3]{0:T(128)S(1)}, s32[3]{0:T(128)}, u32[]{:S(2)}) copy-start(s32[3]{0:T(128)} %param.10) | copy-start | bytes 40
  33.3 3.3 %collective-permute-start.3 = (f32[288,128]{1,0:T(8,128)S(1)}, f32[288,128]{1,0:T(8,128)S(1)}, u32[]{:S(2)}, u32[]{:S(2)}) collective-permute-start(f32[288,128]{1,0:T(8,128)S(1)} %get-tuple-element.33), channel_id=1, source_target_pairs={{0,8},{8,0},{16,24},{24,16},{32,40},{40,32},{48,56},{56,48},{64,72... | collective-permute-start | bytes 442376 | tf_op jit(solution)/shard_map/ppermute | solution.py:325

commit v4 on v3

--- a/solution.py
+++ b/solution.py
@@ -48,9 +48,14 @@
     return jnp.where(iota((npanel, slots), 1).astype(F32) == column, 1.0, 0.0).astype(BF16)
 
 
-def select_kernel(cap, ids_ref, vec_ref, pay_ref, over_ref):
+def select_kernel(cap, ids_ref, vec_ref, pay_ref, over_ref, here_ref, held_ref, block_ref, in_sem, out_sem):
+    ids_load = pltpu.make_async_copy(ids_ref, here_ref, in_sem.at[0])
+    load = pltpu.make_async_copy(vec_ref, held_ref, in_sem.at[1])
+    ids_load.start()
+    load.start()
     rows, held, sites = vec_ref.shape
-    ids = ids_ref[...]
+    ids_load.wait()
+    ids = here_ref[...]
     npanel = ids.shape[1]
     local = ids - lax.axis_index("vec") * held
     inside = (local >= 0) & (local < held)
@@ -60,10 +65,15 @@
     to_slot = jnp.where(iota((cap, npanel), 0).astype(F32) == place, 1.0, 0.0)
     of_held = jnp.where(iota((held, npanel), 0) == local, 1.0, 0.0)
     pick = lax.dot_general(to_slot, of_held, NT, preferred_element_type=F32).astype(BF16)
+    load.wait()
     for row in range(rows):
-        part = jnp.dot(pick, vec_ref[row], preferred_element_type=F32).astype(BF16)
-        for peer in range(pay_ref.shape[0]):
-            pay_ref[peer, row * cap:(row + 1) * cap, :] = part
+        block_ref[row * cap:(row + 1) * cap, :] = jnp.dot(
+            pick, held_ref[row], preferred_element_type=F32).astype(BF16)
+    copies = [pltpu.make_async_copy(block_ref, pay_ref.at[peer], out_sem.at[peer]) for peer in range(pay_ref.shape[0])]
+    for copy in copies:
+        copy.start()
+    for copy in copies:
+        copy.wait()
 
 
 def link_terms(ahead, behind, fore, back):
@@ -193,21 +203,21 @@
         out_ref[row] = jnp.dot(order, block, preferred_element_type=F32).astype(BF16)
 
 
-def main_kernel(cap, planar_ref, height_ref, phase_ref, order_ref, got_ref, spare_ref,
-                keep_ref, send_ref, field_ref, panel_ref, weight_ref):
+def main_kernel(cap, half_at, planar_ref, height_ref, phase_ref, order_ref, got_ref, spare_ref,
+                out_ref, field_ref, panel_ref, weight_ref):
     owners = got_ref.shape[0]
-    npanel = order_ref.shape[0]
+    npanel = order_ref.shape[0] // 2
     held = planar_ref.shape[1]
     sites = got_ref.shape[2]
     rows = got_ref.shape[1] // cap
     nmom = phase_ref.shape[0] // 2
-    half = npanel // 2
+    chosen = slice(half_at * npanel, (half_at + 1) * npanel)
     field_ref[0:2 * held, :] = planar_ref[...].reshape(2 * held, rows * sites)
     field_ref[2 * held:3 * held, :] = height_ref[...]
     for row in range(rows):
         block = got_ref[:, row * cap:(row + 1) * cap, :].reshape(owners * cap, sites)
-        picked = jnp.dot(order_ref[...], block, preferred_element_type=F32)
-        panel_ref[row] = picked + spare_ref[row].astype(F32)
+        picked = jnp.dot(order_ref[chosen, :], block, preferred_element_type=F32)
+        panel_ref[row] = picked + spare_ref[row, chosen, :].astype(F32)
 
     def weigh(at, carry):
         first = pl.multiple_of(at * TILE, TILE)
@@ -230,11 +240,10 @@
     lax.fori_loop(0, npanel // TILE, weigh, 0)
     whole = lax.dot_general(weight_ref[...], field_ref[...], NT, preferred_element_type=F32)
     lines = 2 * nmom + 1
-    for at, ref in ((0, keep_ref), (half, send_ref)):
-        blocks = [whole[part * npanel + at:part * npanel + at + half] for part in range(2 * nmom)]
-        for part, block in enumerate(blocks):
-            ref[pl.ds(part, half, stride=lines), :] = block[:, :LANES]
-        ref[pl.ds(2 * nmom, half, stride=lines), :] = jnp.concatenate([b[:, LANES:] for b in blocks], axis=1)
+    blocks = [whole[part * npanel:(part + 1) * npanel] for part in range(2 * nmom)]
+    for part, block in enumerate(blocks):
+        out_ref[pl.ds(part, npanel, stride=lines), :] = block[:, :LANES]
+    out_ref[pl.ds(2 * nmom, npanel, stride=lines), :] = jnp.concatenate([b[:, LANES:] for b in blocks], axis=1)
 
 
 def sum_kernel(nmom, directions_ref, parts_ref, out_ref):
@@ -256,7 +265,7 @@
 
 
 def specs(*spaces):
-    kinds = {"s": pltpu.SMEM, "v": pltpu.VMEM, "a": pl.ANY}
+    kinds = {"s": pltpu.SMEM, "v": pltpu.VMEM, "a": pl.ANY, "h": pltpu.HBM}
     return [pl.BlockSpec(memory_space=kinds[space]) for space in spaces]
 
 
@@ -291,9 +300,12 @@
     upward = [(i, (i + 1) % nslab) for i in range(nslab)]
     outer = lax.ppermute(flat, "slab", beyond)
     pay, over = call(
-        functools.partial(select_kernel, CAP), [shape((nvec, rows * CAP, sites), BF16), shape((1,), jnp.int32)],
-        "vv", "vs", "select", (), COST,
-    )(in_vmem(ids), in_vmem(vec))
+        functools.partial(select_kernel, CAP), [shape((nvec, rows * CAP, sites), BF16), pltpu.SMEM((1,), jnp.int32)],
+        "hh", "as", "select",
+        [vm(ids.shape, jnp.int32), vm(vec.shape, BF16), vm((rows * CAP, sites), BF16), pltpu.SemaphoreType.DMA((2,)),
+         pltpu.SemaphoreType.DMA((nvec,))],
+        COST,
+    )(ids, vec)
     got = lax.all_to_all(pay, "vec", 0, 0, tiled=True)
     def gather_all():
         every = jnp.broadcast_to(vec.reshape(1, rows * held, sites), (nvec, rows * held, sites))
@@ -314,14 +326,16 @@
         height_kernel, [shape((held, rows * sites), BF16)], "vvvv", "v", "height", [vm((2, 18, sites), F32)],
     )(link, below, inner, outer)[0]
     part = shape((half * lines, LANES), F32)
-    keep, send = call(
-        functools.partial(main_kernel, CAP), [part, part], "vvvvvv", "vv", "main",
-        [
-            vm((3 * held, rows * sites), BF16),
-            vm((rows, npanel, sites), F32),
-            vm((2 * nmom * npanel, rows * sites), BF16),
-        ],
-    )(planar, height, in_vmem(phase), in_vmem(order), got, in_vmem(spare))
+    inputs = (planar, height, in_vmem(phase), in_vmem(order), got, in_vmem(spare))
+    send, keep = [
+        call(
+            functools.partial(main_kernel, CAP, half_at), [part], "vvvvvv", "v", name,
+            [vm((3 * held, rows * sites), BF16), vm((rows, half, sites), F32),
+             vm((2 * nmom * half, rows * sites), BF16)],
+            cost,
+        )(*inputs)[0]
+        for half_at, name, cost in ((1, "send", 0), (0, "keep", COST))
+    ]
     pair = lax.ppermute(send, "slab", mate)
     groups = [[2 * k + c for k in range(nslab // 2)] for c in range(2)]
     both = (keep + pair).reshape(half, 1, lines * LANES)

time: 67.4 us -> 66.2 us (0.982)
  waiting for transfers between devices: 3.77 us -> 3 us
    ppermute x1, waiting for transfers between devices: 1.34 us -> 0.13 us  [body(): pair = lax.ppermute(send, 'slab', mate)]
    pallas_call x1 -> x2, Pallas kernels: 1.91 us -> 2.42 us  [body(): call(functools.partial(main_kernel, CAP, half_at), [part], 'vvvvvv', 'v',...]
  transfers between devices with their start and end apart: 5 -> 5, of which waited for: 2 -> 2; matrix products, arithmetic and copies ran while one was open for 0% -> 0% of each run, Pallas kernels for 9% -> 10%
where the time goes in v4:
time: 66.2 us; the launch traced here: 65.8 us
  blocking collectives  29.8 us (45%)
  starting transfers between devices  24.2 us (37%)
  Pallas kernels  8.62 us (13%)
  waiting for transfers between devices  3 us (5%)
    all_to_all x1, blocking collectives, body(): lax.all_to_all(both, 'slab', 0, 0, axis_index_groups=groups, tiled=True)  29.8 us
    ppermute x1, starting transfers between devices, body(): outer = lax.ppermute(flat, 'slab', beyond)  13.5 us
    all_to_all x1, starting transfers between devices, body(): got = lax.all_to_all(pay, 'vec', 0, 0, tiled=True)  4.96 us
    ppermute x1, waiting for transfers between devices, body(): below = lax.ppermute(link_late, 'slab', upward)  2.87 us
    pallas_call x1, Pallas kernels, body(): call(functools.partial(planar_kernel, CAP, nvec), [shape((2, held, rows *...  2.55 us
    pallas_call x2, Pallas kernels, body(): call(functools.partial(main_kernel, CAP, half_at), [part], 'vvvvvv', 'v',...  2.42 us
    pallas_call x1, Pallas kernels, body(): call(functools.partial(select_kernel, CAP), [shape((nvec, rows * CAP, sit...  2.2 us
    ppermute x1, starting transfers between devices, body(): below = lax.ppermute(link_late, 'slab', upward)  1.92 us
  transfers between devices with their start and end apart: 5, of which 2 were waited for; matrix products, arithmetic and copies ran while one was open for 0% of the time, Pallas kernels for 10%

profile of v4, /device:TPU:2, one launch (start us, length us, event | category | flops | bytes accessed | tf_op | source)
XLA Modules:
  0.0 65.8 jit_solution(781890811129462537)
XLA Ops:
  0.0 13.5 %collective-permute-start = (bf16[288,512]{1,0:T(8,128)(2,1)}, bf16[288,512]{1,0:T(8,128)(2,1)S(1)}, u32[]{:S(2)}, u32[]{:S(2)}) collective-permute-start(bf16[288,512]{1,0:T(8,128)(2,1)} %bitcast.16), channel_id=1, source_target_pairs={{0,504},{8,16},{16,8},{24,32},{32,24},{40,48},{48,40},{56,64},{64,... | collective-permute-start | bytes 884744 | tf_op jit(solution)/shard_map/ppermute | solution.py:301
  13.5 0.0 copy-start.3
  13.5 0.0 copy-start.4
  13.5 2.2 %select.1 = (bf16[8,96,512]{2,1,0:T(8,128)(2,1)}, s32[1]{0:T(128)S(4)}) custom-call(s32[1,64]{1,0:T(1,128)} %bitcast.21, bf16[6,48,512]{2,1,0:T(8,128)(2,1)} %bitcast.17), custom_call_target="tpu_custom_call" | custom-call | flops 49999998976 | tf_op jit(solution)/shard_map/select/pallas_call | solution.py:302
  15.7 0.0 copy-done.3
  15.7 0.0 copy-done.4
  15.7 0.0 copy-start
  15.7 0.0 copy-start.2
  15.8 5.0 %all-to-all-start.1 = ((bf16[8,96,512]{2,1,0:T(8,128)(2,1)}), bf16[8,96,512]{2,1,0:T(8,128)(2,1)S(1)}, u32[]{:S(2)}, u32[]{:S(2)}) async-start(bf16[8,96,512]{2,1,0:T(8,128)(2,1)} %get-tuple-element.28), calls=%async_computation.1 | async-start | bytes 1572864 | tf_op jit(solution)/shard_map/all_to_all | solution.py:309
  20.8 0.0 collective-permute-done.outer_ref
  20.8 0.0 copy-done
  20.8 1.9 %collective-permute-start.1 = (bf16[3,18,512]{2,1,0:T(8,128)(2,1)S(1)}, bf16[3,18,512]{2,1,0:T(8,128)(2,1)S(1)}, u32[]{:S(2)}, u32[]{:S(2)}) collective-permute-start(bf16[3,18,512]{2,1,0:T(8,128)(2,1)S(1)} %bitcast.11), channel_id=1, source_target_pairs={{0,8},{8,16},{16,24},{24,32},{32,40},{40,48},{48,56},{56,64},{64,7... | collective-permute-start | bytes 165896 | tf_op jit(solution)/shard_map/ppermute | solution.py:324
  22.7 1.9 %collective-permute-start.2 = (bf16[288,512]{1,0:T(8,128)(2,1)S(1)}, bf16[288,512]{1,0:T(8,128)(2,1)S(1)}, u32[]{:S(2)}, u32[]{:S(2)}) collective-permute-start(bf16[288,512]{1,0:T(8,128)(2,1)S(1)} %bitcast.18), channel_id=1, source_target_pairs={{0,8},{8,0},{16,24},{24,16},{32,40},{40,32},{48,56},{56,48},{64,72... | collective-permute-start | bytes 884744 | tf_op jit(solution)/shard_map/ppermute | solution.py:323
  24.6 0.0 copy-done.2
  24.6 2.5 %planar.1 = (bf16[2,48,3072]{2,1,0:T(8,128)(2,1)S(1)}, f32[8,512]{1,0:T(8,128)S(1)}, bf16[64,128]{1,0:T(8,128)(2,1)S(1)}) custom-call(s32[4,3]{1,0:T(4,128)S(1)} %copy-done.2, s32[1,64]{1,0:T(1,128)S(1)} %bitcast.23, bf16[6,48,512]{2,1,0:T(8,128)(2,1)S(1)} %bitcast.19, bf16[3,18,512]{2,1,0:T(8,128)(2,1)S(1)} %bitcast.12), custom_call_target="tpu_custom_call" | custom-call | flops 49999998976 | tf_op jit(solution)/shard_map/planar/pallas_call | solution.py:315
  27.2 2.9 %collective-permute-done.1.below_ref = bf16[3,18,512]{2,1,0:T(8,128)(2,1)S(1)} collective-permute-done((bf16[3,18,512]{2,1,0:T(8,128)(2,1)S(1)}, bf16[3,18,512]{2,1,0:T(8,128)(2,1)S(1)}, u32[]{:S(2)}, u32[]{:S(2)}) %collective-permute-start.1) | collective-permute-done | bytes 55328 | tf_op jit(solution)/shard_map/ppermute | solution.py:324
  30.0 0.0 collective-permute-done.2.inner_ref
  30.1 0.5 height.1.height_ref
  30.6 0.0 all-to-all-done.1.got_ref
  30.6 1.2 %send.1 = f32[288,128]{1,0:T(8,128)S(1)} custom-call(bf16[2,48,3072]{2,1,0:T(8,128)(2,1)S(1)} %get-tuple-element.22.planar_ref, bf16[48,3072]{1,0:T(8,128)(2,1)S(1)} %height.1.height_ref, f32[8,512]{1,0:T(8,128)S(1)} %get-tuple-element.26.phase_ref, bf16[64,128]{1,0:T(8,128)(2,1)S(1)} %get-tuple-element.27.order_ref, ...), custom_call_target="tpu_custom_call" | custom-call | tf_op jit(solution)/shard_map/send/pallas_call | solution.py:331
  31.8 0.0 copy-start.1
  31.8 1.9 %collective-permute-start.3 = (f32[288,128]{1,0:T(8,128)S(1)}, f32[288,128]{1,0:T(8,128)S(1)}, u32[]{:S(2)}, u32[]{:S(2)}) collective-permute-start(f32[288,128]{1,0:T(8,128)S(1)} %send.1), channel_id=1, source_target_pairs={{0,8},{8,0},{16,24},{24,16},{32,40},{40,32},{48,56},{56,48},{64,72... | collective-permute-start | bytes 442376 | tf_op jit(solution)/shard_map/ppermute | solution.py:339
  33.8 1.2 %keep.1 = f32[288,128]{1,0:T(8,128)S(1)} custom-call(bf16[2,48,3072]{2,1,0:T(8,128)(2,1)S(1)} %get-tuple-element.22.planar_ref, bf16[48,3072]{1,0:T(8,128)(2,1)S(1)} %height.1.height_ref, f32[8,512]{1,0:T(8,128)S(1)} %get-tuple-element.26.phase_ref, bf16[64,128]{1,0:T(8,128)(2,1)S(1)} %get-tuple-element.27.order_ref, ...), custom_call_target="tpu_custom_call" | custom-call | flops 49999998976 | tf_op jit(solution)/shard_map/keep/pallas_call | solution.py:331
  35.0 0.1 collective-permute-done.3
  35.1 29.8 %all_to_all.15.parts_ref = f32[32,1,1152]{2,1,0:T(1,128)S(1)} all-to-all(f32[32,1,1152]{2,1,0:T(1,128)S(1)} %bitcast.15), channel_id=1, replica_groups={{0,16,32,48,64,80,96,112,128,144,160,176,192,208,224,240,256,272,288,30..., dimensions={0} | all-to-all | bytes 294912 | tf_op jit(solution)/shard_map/all_to_all | solution.py:342
  64.9 0.0 copy-done.1
  64.9 0.9 %total.1 = f32[2,3,4,48]{3,2,1,0:T(4,128)} custom-call(s32[1,3]{1,0:T(1,128)S(1)} %bitcast.14, f32[32,1,1152]{2,1,0:T(1,128)S(1)} %all_to_all.15.parts_ref), custom_call_target="tpu_custom_call" | custom-call | tf_op jit(solution)/shard_map/total/pallas_call | solution.py:343
  (3 shorter events, 0.1 us)
Async XLA Ops:
  0.0 20.8 %collective-permute-start = (bf16[288,512]{1,0:T(8,128)(2,1)}, bf16[288,512]{1,0:T(8,128)(2,1)S(1)}, u32[]{:S(2)}, u32[]{:S(2)}) collective-permute-start(bf16[288,512]{1,0:T(8,128)(2,1)} %bitcast.16), channel_id=1, source_target_pairs={{0,504},{8,16},{16,8},{24,32},{32,24},{40,48},{48,40},{56,64},{64,... | collective-permute-start | bytes 884744 | tf_op jit(solution)/shard_map/ppermute | solution.py:301
  13.5 2.2 %copy-start.3 = (bf16[6,48,1,512]{3,1,2,0:T(8,128)(2,1)S(1)}, bf16[6,48,1,512]{3,1,2,0:T(8,128)(2,1)}, u32[]{:S(2)}) copy-start(bf16[6,48,1,512]{3,1,2,0:T(8,128)(2,1)} %param.7) | copy-start | bytes 884740
  13.5 2.2 %copy-start.4 = (s32[64]{0:T(128)S(1)}, s32[64]{0:T(128)}, u32[]{:S(2)}) copy-start(s32[64]{0:T(128)} %param.11) | copy-start | bytes 772
  15.7 5.0 %copy-start = (bf16[3,18,1,512]{3,1,2,0:T(8,128)(2,1)S(1)}, bf16[3,18,1,512]{3,1,2,0:T(8,128)(2,1)}, u32[]{:S(2)}) copy-start(bf16[3,18,1,512]{3,1,2,0:T(8,128)(2,1)} %param.8) | copy-start | bytes 165892
  15.7 8.9 %copy-start.2 = (s32[4,3]{1,0:T(4,128)S(1)}, s32[4,3]{1,0:T(4,128)}, u32[]{:S(2)}) copy-start(s32[4,3]{1,0:T(4,128)} %momenta_ref.1) | copy-start | bytes 148
  15.8 14.8 %all-to-all-start.1 = ((bf16[8,96,512]{2,1,0:T(8,128)(2,1)}), bf16[8,96,512]{2,1,0:T(8,128)(2,1)S(1)}, u32[]{:S(2)}, u32[]{:S(2)}) async-start(bf16[8,96,512]{2,1,0:T(8,128)(2,1)} %get-tuple-element.28), calls=%async_computation.1 | async-start | bytes 1572864 | tf_op jit(solution)/shard_map/all_to_all | solution.py:309
  20.8 9.3 %collective-permute-start.1 = (bf16[3,18,512]{2,1,0:T(8,128)(2,1)S(1)}, bf16[3,18,512]{2,1,0:T(8,128)(2,1)S(1)}, u32[]{:S(2)}, u32[]{:S(2)}) collective-permute-start(bf16[3,18,512]{2,1,0:T(8,128)(2,1)S(1)} %bitcast.11), channel_id=1, source_target_pairs={{0,8},{8,16},{16,24},{24,32},{32,40},{40,48},{48,56},{56,64},{64,7... | collective-permute-start | bytes 165896 | tf_op jit(solution)/shard_map/ppermute | solution.py:324
  22.7 7.4 %collective-permute-start.2 = (bf16[288,512]{1,0:T(8,128)(2,1)S(1)}, bf16[288,512]{1,0:T(8,128)(2,1)S(1)}, u32[]{:S(2)}, u32[]{:S(2)}) collective-permute-start(bf16[288,512]{1,0:T(8,128)(2,1)S(1)} %bitcast.18), channel_id=1, source_target_pairs={{0,8},{8,0},{16,24},{24,16},{32,40},{40,32},{48,56},{56,48},{64,72... | collective-permute-start | bytes 884744 | tf_op jit(solution)/shard_map/ppermute | solution.py:323
  31.8 33.1 %copy-start.1 = (s32[3]{0:T(128)S(1)}, s32[3]{0:T(128)}, u32[]{:S(2)}) copy-start(s32[3]{0:T(128)} %param.10) | copy-start | bytes 40
  31.8 3.3 %collective-permute-start.3 = (f32[288,128]{1,0:T(8,128)S(1)}, f32[288,128]{1,0:T(8,128)S(1)}, u32[]{:S(2)}, u32[]{:S(2)}) collective-permute-start(f32[288,128]{1,0:T(8,128)S(1)} %send.1), channel_id=1, source_target_pairs={{0,8},{8,0},{16,24},{24,16},{32,40},{40,32},{48,56},{56,48},{64,72... | collective-permute-start | bytes 442376 | tf_op jit(solution)/shard_map/ppermute | solution.py:339

commit v5 on v4

--- a/solution.py
+++ b/solution.py
@@ -162,16 +162,18 @@
     phase_ref[...] = jnp.cos(turns.astype(F32) * (2.0 * math.pi / modulus))
 
 
-def height_kernel(links_ref, below_ref, inner_ref, outer_ref, out_ref, link_ref):
+def height_kernel(planar_ref, links_ref, below_ref, inner_ref, outer_ref, out_ref, link_ref):
+    planes, held, width = planar_ref.shape
+    out_ref[0:planes * held, :] = planar_ref[...].reshape(planes * held, width)
     first_core = lax.axis_index("slab") % 2 == 0
     pl.when(first_core)(lambda: height(links_ref, below_ref, inner_ref, outer_ref, out_ref, link_ref))
     pl.when(jnp.logical_not(first_core))(lambda: height(links_ref, below_ref, outer_ref, inner_ref, out_ref, link_ref))
 
 
 def height(links_ref, below_ref, ahead_ref, behind_ref, out_ref, link_ref):
-    held, width = out_ref.shape
+    held = out_ref.shape[0] // 3
     sites = links_ref.shape[2]
-    rows = width // sites
+    rows = out_ref.shape[1] // sites
     link_ref[0] = links_ref[2].astype(F32) * 0.5
     link_ref[1] = below_ref[2].astype(F32) * 0.5
 
@@ -187,7 +189,7 @@
                 lambda e: link_ref[1, e:e + 1, span],
             )
             for row in range(rows):
-                out_ref[pl.ds(first, TILE), row * sites + lane:row * sites + lane + LANES] = (
+                out_ref[pl.ds(2 * held + first, TILE), row * sites + lane:row * sites + lane + LANES] = (
                     shifted[row].astype(BF16))
         return carry
 
@@ -203,27 +205,23 @@
         out_ref[row] = jnp.dot(order, block, preferred_element_type=F32).astype(BF16)
 
 
-def main_kernel(cap, half_at, planar_ref, height_ref, phase_ref, order_ref, got_ref, spare_ref,
-                out_ref, field_ref, panel_ref, weight_ref):
+def main_kernel(cap, half_at, field_ref, phase_ref, order_ref, got_ref, spare_ref,
+                out_ref, panel_ref, weight_ref):
     owners = got_ref.shape[0]
     npanel = order_ref.shape[0] // 2
-    held = planar_ref.shape[1]
     sites = got_ref.shape[2]
     rows = got_ref.shape[1] // cap
     nmom = phase_ref.shape[0] // 2
     chosen = slice(half_at * npanel, (half_at + 1) * npanel)
-    field_ref[0:2 * held, :] = planar_ref[...].reshape(2 * held, rows * sites)
-    field_ref[2 * held:3 * held, :] = height_ref[...]
     for row in range(rows):
         block = got_ref[:, row * cap:(row + 1) * cap, :].reshape(owners * cap, sites)
         picked = jnp.dot(order_ref[chosen, :], block, preferred_element_type=F32)
         panel_ref[row] = picked + spare_ref[row, chosen, :].astype(F32)
 
-    def weigh(at, carry):
-        first = pl.multiple_of(at * TILE, TILE)
+    for first in range(0, npanel, TILE):
         for colour in range(3):
-            re = panel_ref[colour, pl.ds(first, TILE), :]
-            im = panel_ref[3 + colour, pl.ds(first, TILE), :]
+            re = panel_ref[colour, first:first + TILE, :]
+            im = panel_ref[3 + colour, first:first + TILE, :]
             for mom in range(nmom):
                 cos = phase_ref[mom:mom + 1, :]
                 sin = phase_ref[nmom + mom:nmom + mom + 1, :]
@@ -231,13 +229,11 @@
                 wi = re * sin + im * cos
                 low = slice(colour * sites, (colour + 1) * sites)
                 high = slice((3 + colour) * sites, (4 + colour) * sites)
-                weight_ref[pl.ds(mom * npanel + first, TILE), low] = wr
-                weight_ref[pl.ds(mom * npanel + first, TILE), high] = wi.astype(BF16)
-                weight_ref[pl.ds((nmom + mom) * npanel + first, TILE), low] = (-wi).astype(BF16)
-                weight_ref[pl.ds((nmom + mom) * npanel + first, TILE), high] = wr
-        return carry
-
-    lax.fori_loop(0, npanel // TILE, weigh, 0)
+                at, after = mom * npanel + first, (nmom + mom) * npanel + first
+                weight_ref[at:at + TILE, low] = wr
+                weight_ref[at:at + TILE, high] = wi.astype(BF16)
+                weight_ref[after:after + TILE, low] = (-wi).astype(BF16)
+                weight_ref[after:after + TILE, high] = wr
     whole = lax.dot_general(weight_ref[...], field_ref[...], NT, preferred_element_type=F32)
     lines = 2 * nmom + 1
     blocks = [whole[part * npanel:(part + 1) * npanel] for part in range(2 * nmom)]
@@ -322,15 +318,15 @@
     outer, flat_late, link_late = lax.optimization_barrier((outer, flat, link))
     inner = lax.ppermute(flat_late, "slab", mate)
     below = lax.ppermute(link_late, "slab", upward)
-    height = call(
-        height_kernel, [shape((held, rows * sites), BF16)], "vvvv", "v", "height", [vm((2, 18, sites), F32)],
-    )(link, below, inner, outer)[0]
+    field = call(
+        height_kernel, [shape((3 * held, rows * sites), BF16)], "vvvvv", "v", "height", [vm((2, 18, sites), F32)],
+    )(planar, link, below, inner, outer)[0]
     part = shape((half * lines, LANES), F32)
-    inputs = (planar, height, in_vmem(phase), in_vmem(order), got, in_vmem(spare))
+    inputs = (field, in_vmem(phase), in_vmem(order), got, in_vmem(spare))
     send, keep = [
         call(
-            functools.partial(main_kernel, CAP, half_at), [part], "vvvvvv", "v", name,
-            [vm((3 * held, rows * sites), BF16), vm((rows, half, sites), F32),
+            functools.partial(main_kernel, CAP, half_at), [part], "vvvvv", "v", name,
+            [vm((rows, half, sites), F32),
              vm((2 * nmom * half, rows * sites), BF16)],
             cost,
         )(*inputs)[0]

time: 66.2 us -> 65.6 us (level)
  transfers between devices with their start and end apart: 5 -> 5, of which waited for: 2 -> 2; matrix products, arithmetic and copies ran while one was open for 0% -> 0% of each run, Pallas kernels for 10% -> 9%
where the time goes in v5:
time: 65.6 us; the launch traced here: 65.3 us
  blocking collectives  29.6 us (45%)
  starting transfers between devices  24.2 us (37%)
  Pallas kernels  7.96 us (12%)
  waiting for transfers between devices  3.34 us (5%)
    all_to_all x1, blocking collectives, body(): lax.all_to_all(both, 'slab', 0, 0, axis_index_groups=groups, tiled=True)  29.6 us
    ppermute x1, starting transfers between devices, body(): outer = lax.ppermute(flat, 'slab', beyond)  13.5 us
    all_to_all x1, starting transfers between devices, body(): got = lax.all_to_all(pay, 'vec', 0, 0, tiled=True)  4.96 us
    ppermute x1, waiting for transfers between devices, body(): below = lax.ppermute(link_late, 'slab', upward)  2.87 us
    pallas_call x1, Pallas kernels, body(): call(functools.partial(planar_kernel, CAP, nvec), [shape((2, held, rows *...  2.55 us
    pallas_call x1, Pallas kernels, body(): call(functools.partial(select_kernel, CAP), [shape((nvec, rows * CAP, sit...  2.2 us
    ppermute x1, starting transfers between devices, body(): below = lax.ppermute(link_late, 'slab', upward)  1.92 us
    ppermute x1, starting transfers between devices, body(): inner = lax.ppermute(flat_late, 'slab', mate)  1.92 us
  transfers between devices with their start and end apart: 5, of which 2 were waited for; matrix products, arithmetic and copies ran while one was open for 0% of the time, Pallas kernels for 9%

profile of v5, /device:TPU:2, one launch (start us, length us, event | category | flops | bytes accessed | tf_op | source)
XLA Modules:
  0.0 65.3 jit_solution(13839194957723450553)
XLA Ops:
  0.0 13.5 %collective-permute-start = (bf16[288,512]{1,0:T(8,128)(2,1)}, bf16[288,512]{1,0:T(8,128)(2,1)S(1)}, u32[]{:S(2)}, u32[]{:S(2)}) collective-permute-start(bf16[288,512]{1,0:T(8,128)(2,1)} %bitcast.16), channel_id=1, source_target_pairs={{0,504},{8,16},{16,8},{24,32},{32,24},{40,48},{48,40},{56,64},{64,... | collective-permute-start | bytes 884744 | tf_op jit(solution)/shard_map/ppermute | solution.py:297
  13.5 0.0 copy-start.3
  13.5 0.0 copy-start.4
  13.5 2.2 %select.1 = (bf16[8,96,512]{2,1,0:T(8,128)(2,1)}, s32[1]{0:T(128)S(4)}) custom-call(s32[1,64]{1,0:T(1,128)} %bitcast.21, bf16[6,48,512]{2,1,0:T(8,128)(2,1)} %bitcast.17), custom_call_target="tpu_custom_call" | custom-call | flops 49999998976 | tf_op jit(solution)/shard_map/select/pallas_call | solution.py:298
  15.7 0.0 copy-done.3
  15.7 0.0 copy-done.4
  15.7 0.0 copy-start
  15.7 0.0 copy-start.2
  15.8 5.0 %all-to-all-start.1 = ((bf16[8,96,512]{2,1,0:T(8,128)(2,1)}), bf16[8,96,512]{2,1,0:T(8,128)(2,1)S(1)}, u32[]{:S(2)}, u32[]{:S(2)}) async-start(bf16[8,96,512]{2,1,0:T(8,128)(2,1)} %get-tuple-element.28), calls=%async_computation.1 | async-start | bytes 1572864 | tf_op jit(solution)/shard_map/all_to_all | solution.py:305
  20.8 0.0 collective-permute-done.outer_ref
  20.8 0.0 copy-done
  20.8 1.9 %collective-permute-start.1 = (bf16[3,18,512]{2,1,0:T(8,128)(2,1)S(1)}, bf16[3,18,512]{2,1,0:T(8,128)(2,1)S(1)}, u32[]{:S(2)}, u32[]{:S(2)}) collective-permute-start(bf16[3,18,512]{2,1,0:T(8,128)(2,1)S(1)} %bitcast.11), channel_id=1, source_target_pairs={{0,8},{8,16},{16,24},{24,32},{32,40},{40,48},{48,56},{56,64},{64,7... | collective-permute-start | bytes 165896 | tf_op jit(solution)/shard_map/ppermute | solution.py:320
  22.7 1.9 %collective-permute-start.2 = (bf16[288,512]{1,0:T(8,128)(2,1)S(1)}, bf16[288,512]{1,0:T(8,128)(2,1)S(1)}, u32[]{:S(2)}, u32[]{:S(2)}) collective-permute-start(bf16[288,512]{1,0:T(8,128)(2,1)S(1)} %bitcast.18), channel_id=1, source_target_pairs={{0,8},{8,0},{16,24},{24,16},{32,40},{40,32},{48,56},{56,48},{64,72... | collective-permute-start | bytes 884744 | tf_op jit(solution)/shard_map/ppermute | solution.py:319
  24.6 0.0 copy-done.2
  24.6 2.5 %planar.1 = (bf16[2,48,3072]{2,1,0:T(8,128)(2,1)S(1)}, f32[8,512]{1,0:T(8,128)S(1)}, bf16[64,128]{1,0:T(8,128)(2,1)S(1)}) custom-call(s32[4,3]{1,0:T(4,128)S(1)} %copy-done.2, s32[1,64]{1,0:T(1,128)S(1)} %bitcast.23, bf16[6,48,512]{2,1,0:T(8,128)(2,1)S(1)} %bitcast.19, bf16[3,18,512]{2,1,0:T(8,128)(2,1)S(1)} %bitcast.12), custom_call_target="tpu_custom_call" | custom-call | flops 49999998976 | tf_op jit(solution)/shard_map/planar/pallas_call | solution.py:311
  27.2 2.9 %collective-permute-done.1.below_ref = bf16[3,18,512]{2,1,0:T(8,128)(2,1)S(1)} collective-permute-done((bf16[3,18,512]{2,1,0:T(8,128)(2,1)S(1)}, bf16[3,18,512]{2,1,0:T(8,128)(2,1)S(1)}, u32[]{:S(2)}, u32[]{:S(2)}) %collective-permute-start.1) | collective-permute-done | bytes 55328 | tf_op jit(solution)/shard_map/ppermute | solution.py:320
  30.0 0.0 collective-permute-done.2.inner_ref
  30.1 0.6 height.1.field_ref
  30.6 0.0 all-to-all-done.1.got_ref
  30.6 0.9 %send.1 = f32[288,128]{1,0:T(8,128)S(1)} custom-call(bf16[144,3072]{1,0:T(8,128)(2,1)S(1)} %height.1.field_ref, f32[8,512]{1,0:T(8,128)S(1)} %get-tuple-element.26.phase_ref, bf16[64,128]{1,0:T(8,128)(2,1)S(1)} %get-tuple-element.27.order_ref, bf16[8,96,512]{2,1,0:T(8,128)(2,1)S(1)} %all-to-all-done.1.got_ref, ...), custom_call_target="tpu_custom_call" | custom-call | tf_op jit(solution)/shard_map/send/pallas_call | solution.py:327
  31.5 0.0 copy-start.1
  31.5 1.9 %collective-permute-start.3 = (f32[288,128]{1,0:T(8,128)S(1)}, f32[288,128]{1,0:T(8,128)S(1)}, u32[]{:S(2)}, u32[]{:S(2)}) collective-permute-start(f32[288,128]{1,0:T(8,128)S(1)} %send.1), channel_id=1, source_target_pairs={{0,8},{8,0},{16,24},{24,16},{32,40},{40,32},{48,56},{56,48},{64,72... | collective-permute-start | bytes 442376 | tf_op jit(solution)/shard_map/ppermute | solution.py:335
  33.5 0.9 %keep.1 = f32[288,128]{1,0:T(8,128)S(1)} custom-call(bf16[144,3072]{1,0:T(8,128)(2,1)S(1)} %height.1.field_ref, f32[8,512]{1,0:T(8,128)S(1)} %get-tuple-element.26.phase_ref, bf16[64,128]{1,0:T(8,128)(2,1)S(1)} %get-tuple-element.27.order_ref, bf16[8,96,512]{2,1,0:T(8,128)(2,1)S(1)} %all-to-all-done.1.got_ref, ...), custom_call_target="tpu_custom_call" | custom-call | flops 49999998976 | tf_op jit(solution)/shard_map/keep/pallas_call | solution.py:327
  34.3 0.5 collective-permute-done.3
  34.8 29.6 %all_to_all.15.parts_ref = f32[32,1,1152]{2,1,0:T(1,128)S(1)} all-to-all(f32[32,1,1152]{2,1,0:T(1,128)S(1)} %bitcast.15), channel_id=1, replica_groups={{0,16,32,48,64,80,96,112,128,144,160,176,192,208,224,240,256,272,288,30..., dimensions={0} | all-to-all | bytes 294912 | tf_op jit(solution)/shard_map/all_to_all | solution.py:338
  64.4 0.0 copy-done.1
  64.4 0.9 %total.1 = f32[2,3,4,48]{3,2,1,0:T(4,128)} custom-call(s32[1,3]{1,0:T(1,128)S(1)} %bitcast.14, f32[32,1,1152]{2,1,0:T(1,128)S(1)} %all_to_all.15.parts_ref), custom_call_target="tpu_custom_call" | custom-call | tf_op jit(solution)/shard_map/total/pallas_call | solution.py:339
  (3 shorter events, 0.1 us)
Async XLA Ops:
  0.0 20.8 %collective-permute-start = (bf16[288,512]{1,0:T(8,128)(2,1)}, bf16[288,512]{1,0:T(8,128)(2,1)S(1)}, u32[]{:S(2)}, u32[]{:S(2)}) collective-permute-start(bf16[288,512]{1,0:T(8,128)(2,1)} %bitcast.16), channel_id=1, source_target_pairs={{0,504},{8,16},{16,8},{24,32},{32,24},{40,48},{48,40},{56,64},{64,... | collective-permute-start | bytes 884744 | tf_op jit(solution)/shard_map/ppermute | solution.py:297
  13.5 2.2 %copy-start.3 = (bf16[6,48,1,512]{3,1,2,0:T(8,128)(2,1)S(1)}, bf16[6,48,1,512]{3,1,2,0:T(8,128)(2,1)}, u32[]{:S(2)}) copy-start(bf16[6,48,1,512]{3,1,2,0:T(8,128)(2,1)} %param.7) | copy-start | bytes 884740
  13.5 2.2 %copy-start.4 = (s32[64]{0:T(128)S(1)}, s32[64]{0:T(128)}, u32[]{:S(2)}) copy-start(s32[64]{0:T(128)} %param.11) | copy-start | bytes 772
  15.7 5.0 %copy-start = (bf16[3,18,1,512]{3,1,2,0:T(8,128)(2,1)S(1)}, bf16[3,18,1,512]{3,1,2,0:T(8,128)(2,1)}, u32[]{:S(2)}) copy-start(bf16[3,18,1,512]{3,1,2,0:T(8,128)(2,1)} %param.8) | copy-start | bytes 165892
  15.7 8.9 %copy-start.2 = (s32[4,3]{1,0:T(4,128)S(1)}, s32[4,3]{1,0:T(4,128)}, u32[]{:S(2)}) copy-start(s32[4,3]{1,0:T(4,128)} %momenta_ref.1) | copy-start | bytes 148
  15.8 14.8 %all-to-all-start.1 = ((bf16[8,96,512]{2,1,0:T(8,128)(2,1)}), bf16[8,96,512]{2,1,0:T(8,128)(2,1)S(1)}, u32[]{:S(2)}, u32[]{:S(2)}) async-start(bf16[8,96,512]{2,1,0:T(8,128)(2,1)} %get-tuple-element.28), calls=%async_computation.1 | async-start | bytes 1572864 | tf_op jit(solution)/shard_map/all_to_all | solution.py:305
  20.8 9.3 %collective-permute-start.1 = (bf16[3,18,512]{2,1,0:T(8,128)(2,1)S(1)}, bf16[3,18,512]{2,1,0:T(8,128)(2,1)S(1)}, u32[]{:S(2)}, u32[]{:S(2)}) collective-permute-start(bf16[3,18,512]{2,1,0:T(8,128)(2,1)S(1)} %bitcast.11), channel_id=1, source_target_pairs={{0,8},{8,16},{16,24},{24,32},{32,40},{40,48},{48,56},{56,64},{64,7... | collective-permute-start | bytes 165896 | tf_op jit(solution)/shard_map/ppermute | solution.py:320
  22.7 7.4 %collective-permute-start.2 = (bf16[288,512]{1,0:T(8,128)(2,1)S(1)}, bf16[288,512]{1,0:T(8,128)(2,1)S(1)}, u32[]{:S(2)}, u32[]{:S(2)}) collective-permute-start(bf16[288,512]{1,0:T(8,128)(2,1)S(1)} %bitcast.18), channel_id=1, source_target_pairs={{0,8},{8,0},{16,24},{24,16},{32,40},{40,32},{48,56},{56,48},{64,72... | collective-permute-start | bytes 884744 | tf_op jit(solution)/shard_map/ppermute | solution.py:319
  31.5 32.9 %copy-start.1 = (s32[3]{0:T(128)S(1)}, s32[3]{0:T(128)}, u32[]{:S(2)}) copy-start(s32[3]{0:T(128)} %param.10) | copy-start | bytes 40
  31.5 3.3 %collective-permute-start.3 = (f32[288,128]{1,0:T(8,128)S(1)}, f32[288,128]{1,0:T(8,128)S(1)}, u32[]{:S(2)}, u32[]{:S(2)}) collective-permute-start(f32[288,128]{1,0:T(8,128)S(1)} %send.1), channel_id=1, source_target_pairs={{0,8},{8,0},{16,24},{24,16},{32,40},{40,32},{48,56},{56,48},{64,72... | collective-permute-start | bytes 442376 | tf_op jit(solution)/shard_map/ppermute | solution.py:335

commit v6 on v5

--- a/solution.py
+++ b/solution.py
@@ -175,7 +175,7 @@
     sites = links_ref.shape[2]
     rows = out_ref.shape[1] // sites
     link_ref[0] = links_ref[2].astype(F32) * 0.5
-    link_ref[1] = below_ref[2].astype(F32) * 0.5
+    link_ref[1] = below_ref[...].astype(F32) * 0.5
 
     def step(at, carry):
         first = pl.multiple_of(at * TILE, TILE)
@@ -317,7 +317,7 @@
     spare = lax.cond(over[0] != 0, gather_all, lambda: jnp.zeros((rows, npanel, sites), BF16))
     outer, flat_late, link_late = lax.optimization_barrier((outer, flat, link))
     inner = lax.ppermute(flat_late, "slab", mate)
-    below = lax.ppermute(link_late, "slab", upward)
+    below = lax.ppermute(link_late[2], "slab", upward)
     field = call(
         height_kernel, [shape((3 * held, rows * sites), BF16)], "vvvvv", "v", "height", [vm((2, 18, sites), F32)],
     )(planar, link, below, inner, outer)[0]

time: 65.6 us -> 65.1 us (level)
  transfers between devices with their start and end apart: 5 -> 5, of which waited for: 2 -> 2; matrix products, arithmetic and copies ran while one was open for 0% -> 0% of each run, Pallas kernels for 9% -> 10%
where the time goes in v6:
time: 65.1 us; the launch traced here: 64.7 us
  blocking collectives  29.5 us (45%)
  starting transfers between devices  24.2 us (37%)
  Pallas kernels  7.96 us (12%)
  waiting for transfers between devices  2.81 us (4%)
    all_to_all x1, blocking collectives, body(): lax.all_to_all(both, 'slab', 0, 0, axis_index_groups=groups, tiled=True)  29.5 us
    ppermute x1, starting transfers between devices, body(): outer = lax.ppermute(flat, 'slab', beyond)  13.5 us
    all_to_all x1, starting transfers between devices, body(): got = lax.all_to_all(pay, 'vec', 0, 0, tiled=True)  4.96 us
    pallas_call x1, Pallas kernels, body(): call(functools.partial(planar_kernel, CAP, nvec), [shape((2, held, rows *...  2.55 us
    ppermute x1, waiting for transfers between devices, body(): below = lax.ppermute(link_late[2], 'slab', upward)  2.34 us
    pallas_call x1, Pallas kernels, body(): call(functools.partial(select_kernel, CAP), [shape((nvec, rows * CAP, sit...  2.2 us
    ppermute x1, starting transfers between devices, body(): below = lax.ppermute(link_late[2], 'slab', upward)  1.92 us
    ppermute x1, starting transfers between devices, body(): inner = lax.ppermute(flat_late, 'slab', mate)  1.92 us
  transfers between devices with their start and end apart: 5, of which 2 were waited for; matrix products, arithmetic and copies ran while one was open for 0% of the time, Pallas kernels for 10%

profile of v6, /device:TPU:2, one launch (start us, length us, event | category | flops | bytes accessed | tf_op | source)
XLA Modules:
  0.0 64.7 jit_solution(11474614191617219024)
XLA Ops:
  0.0 13.5 %collective-permute-start = (bf16[288,512]{1,0:T(8,128)(2,1)}, bf16[288,512]{1,0:T(8,128)(2,1)S(1)}, u32[]{:S(2)}, u32[]{:S(2)}) collective-permute-start(bf16[288,512]{1,0:T(8,128)(2,1)} %bitcast.18), channel_id=1, source_target_pairs={{0,504},{8,16},{16,8},{24,32},{32,24},{40,48},{48,40},{56,64},{64,... | collective-permute-start | bytes 884744 | tf_op jit(solution)/shard_map/ppermute | solution.py:297
  13.5 0.0 copy-start.3
  13.5 0.0 copy-start.4
  13.5 2.2 %select.1 = (bf16[8,96,512]{2,1,0:T(8,128)(2,1)}, s32[1]{0:T(128)S(4)}) custom-call(s32[1,64]{1,0:T(1,128)} %bitcast.23, bf16[6,48,512]{2,1,0:T(8,128)(2,1)} %bitcast.19), custom_call_target="tpu_custom_call" | custom-call | flops 49999998976 | tf_op jit(solution)/shard_map/select/pallas_call | solution.py:298
  15.7 0.0 copy-done.3
  15.7 0.0 copy-done.4
  15.7 0.0 copy-start
  15.7 0.0 copy-start.2
  15.8 5.0 %all-to-all-start.1 = ((bf16[8,96,512]{2,1,0:T(8,128)(2,1)}), bf16[8,96,512]{2,1,0:T(8,128)(2,1)S(1)}, u32[]{:S(2)}, u32[]{:S(2)}) async-start(bf16[8,96,512]{2,1,0:T(8,128)(2,1)} %get-tuple-element.28), calls=%async_computation.1 | async-start | bytes 1572864 | tf_op jit(solution)/shard_map/all_to_all | solution.py:305
  20.8 0.0 collective-permute-done.outer_ref
  20.8 0.0 copy-done
  20.8 1.9 %collective-permute-start.1 = (bf16[18,512]{1,0:T(8,128)(2,1)S(1)}, bf16[18,512]{1,0:T(8,128)(2,1)S(1)}, u32[]{:S(2)}, u32[]{:S(2)}) collective-permute-start(bf16[18,512]{1,0:T(8,128)(2,1)S(1)} %slice_bitcast_fusion), channel_id=1, source_target_pairs={{0,8},{8,16},{16,24},{24,32},{32,40},{40,48},{48,56},{56,64},{64,7... | collective-permute-start | bytes 55304 | tf_op jit(solution)/shard_map/ppermute | solution.py:320
  22.7 1.9 %collective-permute-start.2 = (bf16[288,512]{1,0:T(8,128)(2,1)S(1)}, bf16[288,512]{1,0:T(8,128)(2,1)S(1)}, u32[]{:S(2)}, u32[]{:S(2)}) collective-permute-start(bf16[288,512]{1,0:T(8,128)(2,1)S(1)} %bitcast.20), channel_id=1, source_target_pairs={{0,8},{8,0},{16,24},{24,16},{32,40},{40,32},{48,56},{56,48},{64,72... | collective-permute-start | bytes 884744 | tf_op jit(solution)/shard_map/ppermute | solution.py:319
  24.6 0.0 copy-done.2
  24.6 2.5 %planar.1 = (bf16[2,48,3072]{2,1,0:T(8,128)(2,1)S(1)}, f32[8,512]{1,0:T(8,128)S(1)}, bf16[64,128]{1,0:T(8,128)(2,1)S(1)}) custom-call(s32[4,3]{1,0:T(4,128)S(1)} %copy-done.2, s32[1,64]{1,0:T(1,128)S(1)} %bitcast.25, bf16[6,48,512]{2,1,0:T(8,128)(2,1)S(1)} %bitcast.21, bf16[3,18,512]{2,1,0:T(8,128)(2,1)S(1)} %bitcast.14), custom_call_target="tpu_custom_call" | custom-call | flops 49999998976 | tf_op jit(solution)/shard_map/planar/pallas_call | solution.py:311
  27.2 2.3 %collective-permute-done.1.below_ref = bf16[18,512]{1,0:T(8,128)(2,1)S(1)} collective-permute-done((bf16[18,512]{1,0:T(8,128)(2,1)S(1)}, bf16[18,512]{1,0:T(8,128)(2,1)S(1)}, u32[]{:S(2)}, u32[]{:S(2)}) %collective-permute-start.1) | collective-permute-done | bytes 18464 | tf_op jit(solution)/shard_map/ppermute | solution.py:320
  29.5 0.0 collective-permute-done.2.inner_ref
  29.5 0.6 height.1.field_ref
  30.1 0.0 all-to-all-done.1.got_ref
  30.1 0.9 %send.1 = f32[288,128]{1,0:T(8,128)S(1)} custom-call(bf16[144,3072]{1,0:T(8,128)(2,1)S(1)} %height.1.field_ref, f32[8,512]{1,0:T(8,128)S(1)} %get-tuple-element.26.phase_ref, bf16[64,128]{1,0:T(8,128)(2,1)S(1)} %get-tuple-element.27.order_ref, bf16[8,96,512]{2,1,0:T(8,128)(2,1)S(1)} %all-to-all-done.1.got_ref, ...), custom_call_target="tpu_custom_call" | custom-call | tf_op jit(solution)/shard_map/send/pallas_call | solution.py:327
  31.0 0.0 copy-start.1
  31.0 1.9 %collective-permute-start.3 = (f32[288,128]{1,0:T(8,128)S(1)}, f32[288,128]{1,0:T(8,128)S(1)}, u32[]{:S(2)}, u32[]{:S(2)}) collective-permute-start(f32[288,128]{1,0:T(8,128)S(1)} %send.1), channel_id=1, source_target_pairs={{0,8},{8,0},{16,24},{24,16},{32,40},{40,32},{48,56},{56,48},{64,72... | collective-permute-start | bytes 442376 | tf_op jit(solution)/shard_map/ppermute | solution.py:335
  32.9 0.9 %keep.1 = f32[288,128]{1,0:T(8,128)S(1)} custom-call(bf16[144,3072]{1,0:T(8,128)(2,1)S(1)} %height.1.field_ref, f32[8,512]{1,0:T(8,128)S(1)} %get-tuple-element.26.phase_ref, bf16[64,128]{1,0:T(8,128)(2,1)S(1)} %get-tuple-element.27.order_ref, bf16[8,96,512]{2,1,0:T(8,128)(2,1)S(1)} %all-to-all-done.1.got_ref, ...), custom_call_target="tpu_custom_call" | custom-call | flops 49999998976 | tf_op jit(solution)/shard_map/keep/pallas_call | solution.py:327
  33.8 0.5 collective-permute-done.3
  34.3 29.5 %all_to_all.15.parts_ref = f32[32,1,1152]{2,1,0:T(1,128)S(1)} all-to-all(f32[32,1,1152]{2,1,0:T(1,128)S(1)} %bitcast.17), channel_id=1, replica_groups={{0,16,32,48,64,80,96,112,128,144,160,176,192,208,224,240,256,272,288,30..., dimensions={0} | all-to-all | bytes 294912 | tf_op jit(solution)/shard_map/all_to_all | solution.py:338
  63.8 0.0 copy-done.1
  63.8 0.9 %total.1 = f32[2,3,4,48]{3,2,1,0:T(4,128)} custom-call(s32[1,3]{1,0:T(1,128)S(1)} %bitcast.16, f32[32,1,1152]{2,1,0:T(1,128)S(1)} %all_to_all.15.parts_ref), custom_call_target="tpu_custom_call" | custom-call | tf_op jit(solution)/shard_map/total/pallas_call | solution.py:339
  (4 shorter events, 0.1 us)
Async XLA Ops:
  0.0 20.8 %collective-permute-start = (bf16[288,512]{1,0:T(8,128)(2,1)}, bf16[288,512]{1,0:T(8,128)(2,1)S(1)}, u32[]{:S(2)}, u32[]{:S(2)}) collective-permute-start(bf16[288,512]{1,0:T(8,128)(2,1)} %bitcast.18), channel_id=1, source_target_pairs={{0,504},{8,16},{16,8},{24,32},{32,24},{40,48},{48,40},{56,64},{64,... | collective-permute-start | bytes 884744 | tf_op jit(solution)/shard_map/ppermute | solution.py:297
  13.5 2.2 %copy-start.3 = (bf16[6,48,1,512]{3,1,2,0:T(8,128)(2,1)S(1)}, bf16[6,48,1,512]{3,1,2,0:T(8,128)(2,1)}, u32[]{:S(2)}) copy-start(bf16[6,48,1,512]{3,1,2,0:T(8,128)(2,1)} %param.7) | copy-start | bytes 884740
  13.5 2.2 %copy-start.4 = (s32[64]{0:T(128)S(1)}, s32[64]{0:T(128)}, u32[]{:S(2)}) copy-start(s32[64]{0:T(128)} %param.11) | copy-start | bytes 772
  15.7 5.0 %copy-start = (bf16[3,18,1,512]{3,1,2,0:T(8,128)(2,1)S(1)}, bf16[3,18,1,512]{3,1,2,0:T(8,128)(2,1)}, u32[]{:S(2)}) copy-start(bf16[3,18,1,512]{3,1,2,0:T(8,128)(2,1)} %param.8) | copy-start | bytes 165892
  15.7 8.9 %copy-start.2 = (s32[4,3]{1,0:T(4,128)S(1)}, s32[4,3]{1,0:T(4,128)}, u32[]{:S(2)}) copy-start(s32[4,3]{1,0:T(4,128)} %momenta_ref.1) | copy-start | bytes 148
  15.8 14.3 %all-to-all-start.1 = ((bf16[8,96,512]{2,1,0:T(8,128)(2,1)}), bf16[8,96,512]{2,1,0:T(8,128)(2,1)S(1)}, u32[]{:S(2)}, u32[]{:S(2)}) async-start(bf16[8,96,512]{2,1,0:T(8,128)(2,1)} %get-tuple-element.28), calls=%async_computation.1 | async-start | bytes 1572864 | tf_op jit(solution)/shard_map/all_to_all | solution.py:305
  20.8 8.8 %collective-permute-start.1 = (bf16[18,512]{1,0:T(8,128)(2,1)S(1)}, bf16[18,512]{1,0:T(8,128)(2,1)S(1)}, u32[]{:S(2)}, u32[]{:S(2)}) collective-permute-start(bf16[18,512]{1,0:T(8,128)(2,1)S(1)} %slice_bitcast_fusion), channel_id=1, source_target_pairs={{0,8},{8,16},{16,24},{24,32},{32,40},{40,48},{48,56},{56,64},{64,7... | collective-permute-start | bytes 55304 | tf_op jit(solution)/shard_map/ppermute | solution.py:320
  22.7 6.8 %collective-permute-start.2 = (bf16[288,512]{1,0:T(8,128)(2,1)S(1)}, bf16[288,512]{1,0:T(8,128)(2,1)S(1)}, u32[]{:S(2)}, u32[]{:S(2)}) collective-permute-start(bf16[288,512]{1,0:T(8,128)(2,1)S(1)} %bitcast.20), channel_id=1, source_target_pairs={{0,8},{8,0},{16,24},{24,16},{32,40},{40,32},{48,56},{56,48},{64,72... | collective-permute-start | bytes 884744 | tf_op jit(solution)/shard_map/ppermute | solution.py:319
  31.0 32.8 %copy-start.1 = (s32[3]{0:T(128)S(1)}, s32[3]{0:T(128)}, u32[]{:S(2)}) copy-start(s32[3]{0:T(128)} %param.10) | copy-start | bytes 40
  31.0 3.3 %collective-permute-start.3 = (f32[288,128]{1,0:T(8,128)S(1)}, f32[288,128]{1,0:T(8,128)S(1)}, u32[]{:S(2)}, u32[]{:S(2)}) collective-permute-start(f32[288,128]{1,0:T(8,128)S(1)} %send.1), channel_id=1, source_target_pairs={{0,8},{8,0},{16,24},{24,16},{32,40},{40,32},{48,56},{56,48},{64,72... | collective-permute-start | bytes 442376 | tf_op jit(solution)/shard_map/ppermute | solution.py:335

commit v7 on v6

--- a/solution.py
+++ b/solution.py
@@ -48,7 +48,7 @@
     return jnp.where(iota((npanel, slots), 1).astype(F32) == column, 1.0, 0.0).astype(BF16)
 
 
-def select_kernel(cap, ids_ref, vec_ref, pay_ref, over_ref, here_ref, held_ref, block_ref, in_sem, out_sem):
+def select_kernel(cap, ids_ref, vec_ref, pay_ref, over_ref, here_ref, held_ref, in_sem):
     ids_load = pltpu.make_async_copy(ids_ref, here_ref, in_sem.at[0])
     load = pltpu.make_async_copy(vec_ref, held_ref, in_sem.at[1])
     ids_load.start()
@@ -67,13 +67,9 @@
     pick = lax.dot_general(to_slot, of_held, NT, preferred_element_type=F32).astype(BF16)
     load.wait()
     for row in range(rows):
-        block_ref[row * cap:(row + 1) * cap, :] = jnp.dot(
-            pick, held_ref[row], preferred_element_type=F32).astype(BF16)
-    copies = [pltpu.make_async_copy(block_ref, pay_ref.at[peer], out_sem.at[peer]) for peer in range(pay_ref.shape[0])]
-    for copy in copies:
-        copy.start()
-    for copy in copies:
-        copy.wait()
+        part = jnp.dot(pick, held_ref[row], preferred_element_type=F32).astype(BF16)
+        for peer in range(pay_ref.shape[0]):
+            pay_ref[peer, row * cap:(row + 1) * cap, :] = part
 
 
 def link_terms(ahead, behind, fore, back):
@@ -243,12 +239,15 @@
 
 
 def sum_kernel(nmom, directions_ref, parts_ref, out_ref):
-    total = jnp.sum(parts_ref[...], axis=0)
     held = out_ref.shape[-1]
     spill = 3 * held - LANES
     lines = 2 * nmom
-    first = jnp.concatenate([total[:, k * LANES:(k + 1) * LANES] for k in range(lines)], axis=0)
-    last = total[:, lines * LANES:]
+    count = parts_ref.shape[0] // (lines + 1)
+    summed = [
+        jnp.sum(parts_ref[pl.ds(k, count, stride=lines + 1), :], axis=0, keepdims=True) for k in range(lines + 1)
+    ]
+    first = jnp.concatenate(summed[:lines], axis=0)
+    last = summed[lines]
     last = jnp.concatenate([last[:, k * spill:(k + 1) * spill] for k in range(lines)], axis=0)
     total = jnp.concatenate([first, last], axis=1)
     for place in range(out_ref.shape[1]):
@@ -297,9 +296,8 @@
     outer = lax.ppermute(flat, "slab", beyond)
     pay, over = call(
         functools.partial(select_kernel, CAP), [shape((nvec, rows * CAP, sites), BF16), pltpu.SMEM((1,), jnp.int32)],
-        "hh", "as", "select",
-        [vm(ids.shape, jnp.int32), vm(vec.shape, BF16), vm((rows * CAP, sites), BF16), pltpu.SemaphoreType.DMA((2,)),
-         pltpu.SemaphoreType.DMA((nvec,))],
+        "hh", "vs", "select",
+        [vm(ids.shape, jnp.int32), vm(vec.shape, BF16), pltpu.SemaphoreType.DMA((2,))],
         COST,
     )(ids, vec)
     got = lax.all_to_all(pay, "vec", 0, 0, tiled=True)
@@ -336,6 +334,7 @@
     groups = [[2 * k + c for k in range(nslab // 2)] for c in range(2)]
     both = (keep + pair).reshape(half, 1, lines * LANES)
     parts = lax.all_to_all(both, "slab", 0, 0, axis_index_groups=groups, tiled=True)
+    parts = parts.reshape(half * lines, LANES)
     return call(
         functools.partial(sum_kernel, nmom), [shape((2, 3, nmom, held), F32)], "vv", "v", "total",
     )(in_vmem(directions.reshape(1, 3)), parts)[0][None]

time: 65.1 us -> 64.9 us (level)
  transfers between devices with their start and end apart: 5 -> 5, of which waited for: 2 -> 2; matrix products, arithmetic and copies ran while one was open for 0% -> 0% of each run, Pallas kernels for 10% -> 9%
where the time goes in v7:
time: 64.9 us; the launch traced here: 64.6 us
  blocking collectives  29.5 us (45%)
  starting transfers between devices  24.2 us (37%)
  Pallas kernels  7.83 us (12%)
  waiting for transfers between devices  2.81 us (4%)
    all_to_all x1, blocking collectives, body(): lax.all_to_all(both, 'slab', 0, 0, axis_index_groups=groups, tiled=True)  29.5 us
    ppermute x1, starting transfers between devices, body(): outer = lax.ppermute(flat, 'slab', beyond)  13.5 us
    all_to_all x1, starting transfers between devices, body(): got = lax.all_to_all(pay, 'vec', 0, 0, tiled=True)  4.96 us
    pallas_call x1, Pallas kernels, body(): call(functools.partial(planar_kernel, CAP, nvec), [shape((2, held, rows *...  2.55 us
    ppermute x1, waiting for transfers between devices, body(): below = lax.ppermute(link_late[2], 'slab', upward)  2.34 us
    pallas_call x1, Pallas kernels, body(): call(functools.partial(select_kernel, CAP), [shape((nvec, rows * CAP, sit...  2.14 us
    ppermute x1, starting transfers between devices, body(): below = lax.ppermute(link_late[2], 'slab', upward)  1.92 us
    ppermute x1, starting transfers between devices, body(): inner = lax.ppermute(flat_late, 'slab', mate)  1.92 us
  transfers between devices with their start and end apart: 5, of which 2 were waited for; matrix products, arithmetic and copies ran while one was open for 0% of the time, Pallas kernels for 9%

profile of v7, /device:TPU:2, one launch (start us, length us, event | category | flops | bytes accessed | tf_op | source)
XLA Modules:
  0.0 64.6 jit_solution(5439879330018404698)
XLA Ops:
  0.0 13.5 %collective-permute-start = (bf16[288,512]{1,0:T(8,128)(2,1)}, bf16[288,512]{1,0:T(8,128)(2,1)S(1)}, u32[]{:S(2)}, u32[]{:S(2)}) collective-permute-start(bf16[288,512]{1,0:T(8,128)(2,1)} %bitcast.20), channel_id=1, source_target_pairs={{0,504},{8,16},{16,8},{24,32},{32,24},{40,48},{48,40},{56,64},{64,... | collective-permute-start | bytes 884744 | tf_op jit(solution)/shard_map/ppermute | solution.py:296
  13.5 0.0 copy-start.3
  13.5 0.0 copy-start.4
  13.5 2.1 %select.1 = (bf16[8,96,512]{2,1,0:T(8,128)(2,1)}, s32[1]{0:T(128)S(4)}) custom-call(s32[1,64]{1,0:T(1,128)} %bitcast.25, bf16[6,48,512]{2,1,0:T(8,128)(2,1)} %bitcast.21), custom_call_target="tpu_custom_call" | custom-call | flops 49999998976 | tf_op jit(solution)/shard_map/select/pallas_call | solution.py:297
  15.6 0.0 copy-done.3
  15.7 0.0 copy-done.4
  15.7 0.0 copy-start
  15.7 0.0 copy-start.2
  15.7 5.0 %all-to-all-start.1 = ((bf16[8,96,512]{2,1,0:T(8,128)(2,1)}), bf16[8,96,512]{2,1,0:T(8,128)(2,1)S(1)}, u32[]{:S(2)}, u32[]{:S(2)}) async-start(bf16[8,96,512]{2,1,0:T(8,128)(2,1)} %get-tuple-element.28), calls=%async_computation.1 | async-start | bytes 1572864 | tf_op jit(solution)/shard_map/all_to_all | solution.py:303
  20.7 0.0 collective-permute-done.outer_ref
  20.7 0.0 copy-done
  20.7 1.9 %collective-permute-start.1 = (bf16[18,512]{1,0:T(8,128)(2,1)S(1)}, bf16[18,512]{1,0:T(8,128)(2,1)S(1)}, u32[]{:S(2)}, u32[]{:S(2)}) collective-permute-start(bf16[18,512]{1,0:T(8,128)(2,1)S(1)} %slice_bitcast_fusion), channel_id=1, source_target_pairs={{0,8},{8,16},{16,24},{24,32},{32,40},{40,48},{48,56},{56,64},{64,7... | collective-permute-start | bytes 55304 | tf_op jit(solution)/shard_map/ppermute | solution.py:318
  22.6 1.9 %collective-permute-start.2 = (bf16[288,512]{1,0:T(8,128)(2,1)S(1)}, bf16[288,512]{1,0:T(8,128)(2,1)S(1)}, u32[]{:S(2)}, u32[]{:S(2)}) collective-permute-start(bf16[288,512]{1,0:T(8,128)(2,1)S(1)} %bitcast.22), channel_id=1, source_target_pairs={{0,8},{8,0},{16,24},{24,16},{32,40},{40,32},{48,56},{56,48},{64,72... | collective-permute-start | bytes 884744 | tf_op jit(solution)/shard_map/ppermute | solution.py:317
  24.6 0.0 copy-done.2
  24.6 2.5 %planar.1 = (bf16[2,48,3072]{2,1,0:T(8,128)(2,1)S(1)}, f32[8,512]{1,0:T(8,128)S(1)}, bf16[64,128]{1,0:T(8,128)(2,1)S(1)}) custom-call(s32[4,3]{1,0:T(4,128)S(1)} %copy-done.2, s32[1,64]{1,0:T(1,128)S(1)} %bitcast.27, bf16[6,48,512]{2,1,0:T(8,128)(2,1)S(1)} %bitcast.23, bf16[3,18,512]{2,1,0:T(8,128)(2,1)S(1)} %bitcast.16), custom_call_target="tpu_custom_call" | custom-call | flops 49999998976 | tf_op jit(solution)/shard_map/planar/pallas_call | solution.py:309
  27.1 2.3 %collective-permute-done.1.below_ref = bf16[18,512]{1,0:T(8,128)(2,1)S(1)} collective-permute-done((bf16[18,512]{1,0:T(8,128)(2,1)S(1)}, bf16[18,512]{1,0:T(8,128)(2,1)S(1)}, u32[]{:S(2)}, u32[]{:S(2)}) %collective-permute-start.1) | collective-permute-done | bytes 18464 | tf_op jit(solution)/shard_map/ppermute | solution.py:318
  29.5 0.0 collective-permute-done.2.inner_ref
  29.5 0.6 height.1.field_ref
  30.1 0.0 all-to-all-done.1.got_ref
  30.1 0.9 %send.1 = f32[288,128]{1,0:T(8,128)S(1)} custom-call(bf16[144,3072]{1,0:T(8,128)(2,1)S(1)} %height.1.field_ref, f32[8,512]{1,0:T(8,128)S(1)} %get-tuple-element.26.phase_ref, bf16[64,128]{1,0:T(8,128)(2,1)S(1)} %get-tuple-element.27.order_ref, bf16[8,96,512]{2,1,0:T(8,128)(2,1)S(1)} %all-to-all-done.1.got_ref, ...), custom_call_target="tpu_custom_call" | custom-call | tf_op jit(solution)/shard_map/send/pallas_call | solution.py:325
  30.9 0.0 copy-start.1
  31.0 1.9 %collective-permute-start.3 = (f32[288,128]{1,0:T(8,128)S(1)}, f32[288,128]{1,0:T(8,128)S(1)}, u32[]{:S(2)}, u32[]{:S(2)}) collective-permute-start(f32[288,128]{1,0:T(8,128)S(1)} %send.1), channel_id=1, source_target_pairs={{0,8},{8,0},{16,24},{24,16},{32,40},{40,32},{48,56},{56,48},{64,72... | collective-permute-start | bytes 442376 | tf_op jit(solution)/shard_map/ppermute | solution.py:333
  32.9 0.9 %keep.1 = f32[288,128]{1,0:T(8,128)S(1)} custom-call(bf16[144,3072]{1,0:T(8,128)(2,1)S(1)} %height.1.field_ref, f32[8,512]{1,0:T(8,128)S(1)} %get-tuple-element.26.phase_ref, bf16[64,128]{1,0:T(8,128)(2,1)S(1)} %get-tuple-element.27.order_ref, bf16[8,96,512]{2,1,0:T(8,128)(2,1)S(1)} %all-to-all-done.1.got_ref, ...), custom_call_target="tpu_custom_call" | custom-call | flops 49999998976 | tf_op jit(solution)/shard_map/keep/pallas_call | solution.py:325
  33.8 0.5 collective-permute-done.3
  34.2 29.5 %all_to_all.15 = f32[32,1,1152]{2,1,0:T(1,128)S(1)} all-to-all(f32[32,1,1152]{2,1,0:T(1,128)S(1)} %bitcast.19), channel_id=1, replica_groups={{0,16,32,48,64,80,96,112,128,144,160,176,192,208,224,240,256,272,288,30..., dimensions={0} | all-to-all | bytes 294912 | tf_op jit(solution)/shard_map/all_to_all | solution.py:336
  63.8 0.0 copy-done.1
  63.8 0.8 %total.1 = f32[2,3,4,48]{3,2,1,0:T(4,128)} custom-call(s32[1,3]{1,0:T(1,128)S(1)} %bitcast.18, f32[288,128]{1,0:T(8,128)S(1)} %bitcast.14), custom_call_target="tpu_custom_call" | custom-call | tf_op jit(solution)/shard_map/total/pallas_call | solution.py:338
  (4 shorter events, 0.1 us)
Async XLA Ops:
  0.0 20.7 %collective-permute-start = (bf16[288,512]{1,0:T(8,128)(2,1)}, bf16[288,512]{1,0:T(8,128)(2,1)S(1)}, u32[]{:S(2)}, u32[]{:S(2)}) collective-permute-start(bf16[288,512]{1,0:T(8,128)(2,1)} %bitcast.20), channel_id=1, source_target_pairs={{0,504},{8,16},{16,8},{24,32},{32,24},{40,48},{48,40},{56,64},{64,... | collective-permute-start | bytes 884744 | tf_op jit(solution)/shard_map/ppermute | solution.py:296
  13.5 2.2 %copy-start.3 = (bf16[6,48,1,512]{3,1,2,0:T(8,128)(2,1)S(1)}, bf16[6,48,1,512]{3,1,2,0:T(8,128)(2,1)}, u32[]{:S(2)}) copy-start(bf16[6,48,1,512]{3,1,2,0:T(8,128)(2,1)} %param.7) | copy-start | bytes 884740
  13.5 2.2 %copy-start.4 = (s32[64]{0:T(128)S(1)}, s32[64]{0:T(128)}, u32[]{:S(2)}) copy-start(s32[64]{0:T(128)} %param.11) | copy-start | bytes 772
  15.7 5.0 %copy-start = (bf16[3,18,1,512]{3,1,2,0:T(8,128)(2,1)S(1)}, bf16[3,18,1,512]{3,1,2,0:T(8,128)(2,1)}, u32[]{:S(2)}) copy-start(bf16[3,18,1,512]{3,1,2,0:T(8,128)(2,1)} %param.8) | copy-start | bytes 165892
  15.7 8.9 %copy-start.2 = (s32[4,3]{1,0:T(4,128)S(1)}, s32[4,3]{1,0:T(4,128)}, u32[]{:S(2)}) copy-start(s32[4,3]{1,0:T(4,128)} %momenta_ref.1) | copy-start | bytes 148
  15.7 14.3 %all-to-all-start.1 = ((bf16[8,96,512]{2,1,0:T(8,128)(2,1)}), bf16[8,96,512]{2,1,0:T(8,128)(2,1)S(1)}, u32[]{:S(2)}, u32[]{:S(2)}) async-start(bf16[8,96,512]{2,1,0:T(8,128)(2,1)} %get-tuple-element.28), calls=%async_computation.1 | async-start | bytes 1572864 | tf_op jit(solution)/shard_map/all_to_all | solution.py:303
  20.7 8.8 %collective-permute-start.1 = (bf16[18,512]{1,0:T(8,128)(2,1)S(1)}, bf16[18,512]{1,0:T(8,128)(2,1)S(1)}, u32[]{:S(2)}, u32[]{:S(2)}) collective-permute-start(bf16[18,512]{1,0:T(8,128)(2,1)S(1)} %slice_bitcast_fusion), channel_id=1, source_target_pairs={{0,8},{8,16},{16,24},{24,32},{32,40},{40,48},{48,56},{56,64},{64,7... | collective-permute-start | bytes 55304 | tf_op jit(solution)/shard_map/ppermute | solution.py:318
  22.6 6.8 %collective-permute-start.2 = (bf16[288,512]{1,0:T(8,128)(2,1)S(1)}, bf16[288,512]{1,0:T(8,128)(2,1)S(1)}, u32[]{:S(2)}, u32[]{:S(2)}) collective-permute-start(bf16[288,512]{1,0:T(8,128)(2,1)S(1)} %bitcast.22), channel_id=1, source_target_pairs={{0,8},{8,0},{16,24},{24,16},{32,40},{40,32},{48,56},{56,48},{64,72... | collective-permute-start | bytes 884744 | tf_op jit(solution)/shard_map/ppermute | solution.py:317
  30.9 32.8 %copy-start.1 = (s32[3]{0:T(128)S(1)}, s32[3]{0:T(128)}, u32[]{:S(2)}) copy-start(s32[3]{0:T(128)} %param.10) | copy-start | bytes 40
  31.0 3.3 %collective-permute-start.3 = (f32[288,128]{1,0:T(8,128)S(1)}, f32[288,128]{1,0:T(8,128)S(1)}, u32[]{:S(2)}, u32[]{:S(2)}) collective-permute-start(f32[288,128]{1,0:T(8,128)S(1)} %send.1), channel_id=1, source_target_pairs={{0,8},{8,0},{16,24},{24,16},{32,40},{40,32},{48,56},{56,48},{64,72... | collective-permute-start | bytes 442376 | tf_op jit(solution)/shard_map/ppermute | solution.py:333

commit v8 on v7

--- a/solution.py
+++ b/solution.py
@@ -50,10 +50,11 @@
 
 def select_kernel(cap, ids_ref, vec_ref, pay_ref, over_ref, here_ref, held_ref, in_sem):
     ids_load = pltpu.make_async_copy(ids_ref, here_ref, in_sem.at[0])
-    load = pltpu.make_async_copy(vec_ref, held_ref, in_sem.at[1])
+    rows, held, sites = vec_ref.shape
+    loads = [pltpu.make_async_copy(vec_ref.at[row], held_ref.at[row], in_sem.at[1 + row]) for row in range(rows)]
     ids_load.start()
-    load.start()
-    rows, held, sites = vec_ref.shape
+    for load in loads:
+        load.start()
     ids_load.wait()
     ids = here_ref[...]
     npanel = ids.shape[1]
@@ -65,8 +66,8 @@
     to_slot = jnp.where(iota((cap, npanel), 0).astype(F32) == place, 1.0, 0.0)
     of_held = jnp.where(iota((held, npanel), 0) == local, 1.0, 0.0)
     pick = lax.dot_general(to_slot, of_held, NT, preferred_element_type=F32).astype(BF16)
-    load.wait()
     for row in range(rows):
+        loads[row].wait()
         part = jnp.dot(pick, held_ref[row], preferred_element_type=F32).astype(BF16)
         for peer in range(pay_ref.shape[0]):
             pay_ref[peer, row * cap:(row + 1) * cap, :] = part
@@ -297,7 +298,7 @@
     pay, over = call(
         functools.partial(select_kernel, CAP), [shape((nvec, rows * CAP, sites), BF16), pltpu.SMEM((1,), jnp.int32)],
         "hh", "vs", "select",
-        [vm(ids.shape, jnp.int32), vm(vec.shape, BF16), pltpu.SemaphoreType.DMA((2,))],
+        [vm(ids.shape, jnp.int32), vm(vec.shape, BF16), pltpu.SemaphoreType.DMA((1 + rows,))],
         COST,
     )(ids, vec)
     got = lax.all_to_all(pay, "vec", 0, 0, tiled=True)

time: 64.9 us -> 65.5 us (level)
  transfers between devices with their start and end apart: 5 -> 5, of which waited for: 2 -> 2; matrix products, arithmetic and copies ran while one was open for 0% -> 0% of each run, Pallas kernels for 9% -> 10%
where the time goes in v8:
time: 65.5 us; the launch traced here: 65.2 us
  blocking collectives  29.5 us (45%)
  starting transfers between devices  24.2 us (37%)
  Pallas kernels  8.4 us (13%)
  waiting for transfers between devices  2.81 us (4%)
    all_to_all x1, blocking collectives, body(): lax.all_to_all(both, 'slab', 0, 0, axis_index_groups=groups, tiled=True)  29.5 us
    ppermute x1, starting transfers between devices, body(): outer = lax.ppermute(flat, 'slab', beyond)  13.5 us
    all_to_all x1, starting transfers between devices, body(): got = lax.all_to_all(pay, 'vec', 0, 0, tiled=True)  4.96 us
    pallas_call x1, Pallas kernels, body(): call(functools.partial(select_kernel, CAP), [shape((nvec, rows * CAP, sit...  2.7 us
    pallas_call x1, Pallas kernels, body(): call(functools.partial(planar_kernel, CAP, nvec), [shape((2, held, rows *...  2.55 us
    ppermute x1, waiting for transfers between devices, body(): below = lax.ppermute(link_late[2], 'slab', upward)  2.34 us
    ppermute x1, starting transfers between devices, body(): inner = lax.ppermute(flat_late, 'slab', mate)  1.92 us
    ppermute x1, starting transfers between devices, body(): pair = lax.ppermute(send, 'slab', mate)  1.92 us
  transfers between devices with their start and end apart: 5, of which 2 were waited for; matrix products, arithmetic and copies ran while one was open for 0% of the time, Pallas kernels for 10%

profile of v8, /device:TPU:2, one launch (start us, length us, event | category | flops | bytes accessed | tf_op | source)
XLA Modules:
  0.0 65.2 jit_solution(14887651686540680095)
XLA Ops:
  0.0 13.5 %collective-permute-start = (bf16[288,512]{1,0:T(8,128)(2,1)}, bf16[288,512]{1,0:T(8,128)(2,1)S(1)}, u32[]{:S(2)}, u32[]{:S(2)}) collective-permute-start(bf16[288,512]{1,0:T(8,128)(2,1)} %bitcast.20), channel_id=1, source_target_pairs={{0,504},{8,16},{16,8},{24,32},{32,24},{40,48},{48,40},{56,64},{64,... | collective-permute-start | bytes 884744 | tf_op jit(solution)/shard_map/ppermute | solution.py:297
  13.5 0.0 copy-start.3
  13.5 0.0 copy-start.4
  13.5 2.7 %select.1 = (bf16[8,96,512]{2,1,0:T(8,128)(2,1)}, s32[1]{0:T(128)S(4)}) custom-call(s32[1,64]{1,0:T(1,128)} %bitcast.25, bf16[6,48,512]{2,1,0:T(8,128)(2,1)} %bitcast.21), custom_call_target="tpu_custom_call" | custom-call | flops 49999998976 | tf_op jit(solution)/shard_map/select/pallas_call | solution.py:298
  16.2 0.0 copy-done.3
  16.2 0.0 copy-done.4
  16.2 0.0 copy-start
  16.2 0.0 copy-start.2
  16.3 5.0 %all-to-all-start.1 = ((bf16[8,96,512]{2,1,0:T(8,128)(2,1)}), bf16[8,96,512]{2,1,0:T(8,128)(2,1)S(1)}, u32[]{:S(2)}, u32[]{:S(2)}) async-start(bf16[8,96,512]{2,1,0:T(8,128)(2,1)} %get-tuple-element.28), calls=%async_computation.1 | async-start | bytes 1572864 | tf_op jit(solution)/shard_map/all_to_all | solution.py:304
  21.3 0.0 collective-permute-done.outer_ref
  21.3 0.0 copy-done
  21.3 1.9 %collective-permute-start.1 = (bf16[18,512]{1,0:T(8,128)(2,1)S(1)}, bf16[18,512]{1,0:T(8,128)(2,1)S(1)}, u32[]{:S(2)}, u32[]{:S(2)}) collective-permute-start(bf16[18,512]{1,0:T(8,128)(2,1)S(1)} %slice_bitcast_fusion), channel_id=1, source_target_pairs={{0,8},{8,16},{16,24},{24,32},{32,40},{40,48},{48,56},{56,64},{64,7... | collective-permute-start | bytes 55304 | tf_op jit(solution)/shard_map/ppermute | solution.py:319
  23.2 1.9 %collective-permute-start.2 = (bf16[288,512]{1,0:T(8,128)(2,1)S(1)}, bf16[288,512]{1,0:T(8,128)(2,1)S(1)}, u32[]{:S(2)}, u32[]{:S(2)}) collective-permute-start(bf16[288,512]{1,0:T(8,128)(2,1)S(1)} %bitcast.22), channel_id=1, source_target_pairs={{0,8},{8,0},{16,24},{24,16},{32,40},{40,32},{48,56},{56,48},{64,72... | collective-permute-start | bytes 884744 | tf_op jit(solution)/shard_map/ppermute | solution.py:318
  25.1 0.0 copy-done.2
  25.1 2.5 %planar.1 = (bf16[2,48,3072]{2,1,0:T(8,128)(2,1)S(1)}, f32[8,512]{1,0:T(8,128)S(1)}, bf16[64,128]{1,0:T(8,128)(2,1)S(1)}) custom-call(s32[4,3]{1,0:T(4,128)S(1)} %copy-done.2, s32[1,64]{1,0:T(1,128)S(1)} %bitcast.27, bf16[6,48,512]{2,1,0:T(8,128)(2,1)S(1)} %bitcast.23, bf16[3,18,512]{2,1,0:T(8,128)(2,1)S(1)} %bitcast.16), custom_call_target="tpu_custom_call" | custom-call | flops 49999998976 | tf_op jit(solution)/shard_map/planar/pallas_call | solution.py:310
  27.7 2.3 %collective-permute-done.1.below_ref = bf16[18,512]{1,0:T(8,128)(2,1)S(1)} collective-permute-done((bf16[18,512]{1,0:T(8,128)(2,1)S(1)}, bf16[18,512]{1,0:T(8,128)(2,1)S(1)}, u32[]{:S(2)}, u32[]{:S(2)}) %collective-permute-start.1) | collective-permute-done | bytes 18464 | tf_op jit(solution)/shard_map/ppermute | solution.py:319
  30.0 0.0 collective-permute-done.2.inner_ref
  30.0 0.6 height.1.field_ref
  30.6 0.0 all-to-all-done.1.got_ref
  30.6 0.9 %send.1 = f32[288,128]{1,0:T(8,128)S(1)} custom-call(bf16[144,3072]{1,0:T(8,128)(2,1)S(1)} %height.1.field_ref, f32[8,512]{1,0:T(8,128)S(1)} %get-tuple-element.26.phase_ref, bf16[64,128]{1,0:T(8,128)(2,1)S(1)} %get-tuple-element.27.order_ref, bf16[8,96,512]{2,1,0:T(8,128)(2,1)S(1)} %all-to-all-done.1.got_ref, ...), custom_call_target="tpu_custom_call" | custom-call | tf_op jit(solution)/shard_map/send/pallas_call | solution.py:326
  31.5 0.0 copy-start.1
  31.5 1.9 %collective-permute-start.3 = (f32[288,128]{1,0:T(8,128)S(1)}, f32[288,128]{1,0:T(8,128)S(1)}, u32[]{:S(2)}, u32[]{:S(2)}) collective-permute-start(f32[288,128]{1,0:T(8,128)S(1)} %send.1), channel_id=1, source_target_pairs={{0,8},{8,0},{16,24},{24,16},{32,40},{40,32},{48,56},{56,48},{64,72... | collective-permute-start | bytes 442376 | tf_op jit(solution)/shard_map/ppermute | solution.py:334
  33.5 0.9 %keep.1 = f32[288,128]{1,0:T(8,128)S(1)} custom-call(bf16[144,3072]{1,0:T(8,128)(2,1)S(1)} %height.1.field_ref, f32[8,512]{1,0:T(8,128)S(1)} %get-tuple-element.26.phase_ref, bf16[64,128]{1,0:T(8,128)(2,1)S(1)} %get-tuple-element.27.order_ref, bf16[8,96,512]{2,1,0:T(8,128)(2,1)S(1)} %all-to-all-done.1.got_ref, ...), custom_call_target="tpu_custom_call" | custom-call | flops 49999998976 | tf_op jit(solution)/shard_map/keep/pallas_call | solution.py:326
  34.3 0.5 collective-permute-done.3
  34.8 29.5 %all_to_all.15 = f32[32,1,1152]{2,1,0:T(1,128)S(1)} all-to-all(f32[32,1,1152]{2,1,0:T(1,128)S(1)} %bitcast.19), channel_id=1, replica_groups={{0,16,32,48,64,80,96,112,128,144,160,176,192,208,224,240,256,272,288,30..., dimensions={0} | all-to-all | bytes 294912 | tf_op jit(solution)/shard_map/all_to_all | solution.py:337
  64.3 0.0 copy-done.1
  64.3 0.8 %total.1 = f32[2,3,4,48]{3,2,1,0:T(4,128)} custom-call(s32[1,3]{1,0:T(1,128)S(1)} %bitcast.18, f32[288,128]{1,0:T(8,128)S(1)} %bitcast.14), custom_call_target="tpu_custom_call" | custom-call | tf_op jit(solution)/shard_map/total/pallas_call | solution.py:339
  (4 shorter events, 0.1 us)
Async XLA Ops:
  0.0 21.3 %collective-permute-start = (bf16[288,512]{1,0:T(8,128)(2,1)}, bf16[288,512]{1,0:T(8,128)(2,1)S(1)}, u32[]{:S(2)}, u32[]{:S(2)}) collective-permute-start(bf16[288,512]{1,0:T(8,128)(2,1)} %bitcast.20), channel_id=1, source_target_pairs={{0,504},{8,16},{16,8},{24,32},{32,24},{40,48},{48,40},{56,64},{64,... | collective-permute-start | bytes 884744 | tf_op jit(solution)/shard_map/ppermute | solution.py:297
  13.5 2.7 %copy-start.3 = (bf16[6,48,1,512]{3,1,2,0:T(8,128)(2,1)S(1)}, bf16[6,48,1,512]{3,1,2,0:T(8,128)(2,1)}, u32[]{:S(2)}) copy-start(bf16[6,48,1,512]{3,1,2,0:T(8,128)(2,1)} %param.7) | copy-start | bytes 884740
  13.5 2.7 %copy-start.4 = (s32[64]{0:T(128)S(1)}, s32[64]{0:T(128)}, u32[]{:S(2)}) copy-start(s32[64]{0:T(128)} %param.11) | copy-start | bytes 772
  16.2 5.0 %copy-start = (bf16[3,18,1,512]{3,1,2,0:T(8,128)(2,1)S(1)}, bf16[3,18,1,512]{3,1,2,0:T(8,128)(2,1)}, u32[]{:S(2)}) copy-start(bf16[3,18,1,512]{3,1,2,0:T(8,128)(2,1)} %param.8) | copy-start | bytes 165892
  16.2 8.9 %copy-start.2 = (s32[4,3]{1,0:T(4,128)S(1)}, s32[4,3]{1,0:T(4,128)}, u32[]{:S(2)}) copy-start(s32[4,3]{1,0:T(4,128)} %momenta_ref.1) | copy-start | bytes 148
  16.3 14.3 %all-to-all-start.1 = ((bf16[8,96,512]{2,1,0:T(8,128)(2,1)}), bf16[8,96,512]{2,1,0:T(8,128)(2,1)S(1)}, u32[]{:S(2)}, u32[]{:S(2)}) async-start(bf16[8,96,512]{2,1,0:T(8,128)(2,1)} %get-tuple-element.28), calls=%async_computation.1 | async-start | bytes 1572864 | tf_op jit(solution)/shard_map/all_to_all | solution.py:304
  21.3 8.8 %collective-permute-start.1 = (bf16[18,512]{1,0:T(8,128)(2,1)S(1)}, bf16[18,512]{1,0:T(8,128)(2,1)S(1)}, u32[]{:S(2)}, u32[]{:S(2)}) collective-permute-start(bf16[18,512]{1,0:T(8,128)(2,1)S(1)} %slice_bitcast_fusion), channel_id=1, source_target_pairs={{0,8},{8,16},{16,24},{24,32},{32,40},{40,48},{48,56},{56,64},{64,7... | collective-permute-start | bytes 55304 | tf_op jit(solution)/shard_map/ppermute | solution.py:319
  23.2 6.8 %collective-permute-start.2 = (bf16[288,512]{1,0:T(8,128)(2,1)S(1)}, bf16[288,512]{1,0:T(8,128)(2,1)S(1)}, u32[]{:S(2)}, u32[]{:S(2)}) collective-permute-start(bf16[288,512]{1,0:T(8,128)(2,1)S(1)} %bitcast.22), channel_id=1, source_target_pairs={{0,8},{8,0},{16,24},{24,16},{32,40},{40,32},{48,56},{56,48},{64,72... | collective-permute-start | bytes 884744 | tf_op jit(solution)/shard_map/ppermute | solution.py:318
  31.5 32.8 %copy-start.1 = (s32[3]{0:T(128)S(1)}, s32[3]{0:T(128)}, u32[]{:S(2)}) copy-start(s32[3]{0:T(128)} %param.10) | copy-start | bytes 40
  31.5 3.3 %collective-permute-start.3 = (f32[288,128]{1,0:T(8,128)S(1)}, f32[288,128]{1,0:T(8,128)S(1)}, u32[]{:S(2)}, u32[]{:S(2)}) collective-permute-start(f32[288,128]{1,0:T(8,128)S(1)} %send.1), channel_id=1, source_target_pairs={{0,8},{8,0},{16,24},{24,16},{32,40},{40,32},{48,56},{56,48},{64,72... | collective-permute-start | bytes 442376 | tf_op jit(solution)/shard_map/ppermute | solution.py:334

commit v9 on v6

--- a/solution.py
+++ b/solution.py
@@ -243,12 +243,15 @@
 
 
 def sum_kernel(nmom, directions_ref, parts_ref, out_ref):
-    total = jnp.sum(parts_ref[...], axis=0)
     held = out_ref.shape[-1]
     spill = 3 * held - LANES
     lines = 2 * nmom
-    first = jnp.concatenate([total[:, k * LANES:(k + 1) * LANES] for k in range(lines)], axis=0)
-    last = total[:, lines * LANES:]
+    count = parts_ref.shape[0] // (lines + 1)
+    summed = [
+        jnp.sum(parts_ref[pl.ds(k, count, stride=lines + 1), :], axis=0, keepdims=True) for k in range(lines + 1)
+    ]
+    first = jnp.concatenate(summed[:lines], axis=0)
+    last = summed[lines]
     last = jnp.concatenate([last[:, k * spill:(k + 1) * spill] for k in range(lines)], axis=0)
     total = jnp.concatenate([first, last], axis=1)
     for place in range(out_ref.shape[1]):
@@ -336,6 +339,7 @@
     groups = [[2 * k + c for k in range(nslab // 2)] for c in range(2)]
     both = (keep + pair).reshape(half, 1, lines * LANES)
     parts = lax.all_to_all(both, "slab", 0, 0, axis_index_groups=groups, tiled=True)
+    parts = parts.reshape(half * lines, LANES)
     return call(
         functools.partial(sum_kernel, nmom), [shape((2, 3, nmom, held), F32)], "vv", "v", "total",
     )(in_vmem(directions.reshape(1, 3)), parts)[0][None]

time: 65.1 us -> 65 us (level)
  no operation moved by 1% of the time
where the time goes in v9:
time: 65 us; the launch traced here: 64.7 us
  blocking collectives  29.5 us (45%)
  starting transfers between devices  24.2 us (37%)
  Pallas kernels  7.89 us (12%)
  waiting for transfers between devices  2.81 us (4%)
    all_to_all x1, blocking collectives, body(): lax.all_to_all(both, 'slab', 0, 0, axis_index_groups=groups, tiled=True)  29.5 us
    ppermute x1, starting transfers between devices, body(): outer = lax.ppermute(flat, 'slab', beyond)  13.5 us
    all_to_all x1, starting transfers between devices, body(): got = lax.all_to_all(pay, 'vec', 0, 0, tiled=True)  4.96 us
    pallas_call x1, Pallas kernels, body(): call(functools.partial(planar_kernel, CAP, nvec), [shape((2, held, rows *...  2.55 us
    ppermute x1, waiting for transfers between devices, body(): below = lax.ppermute(link_late[2], 'slab', upward)  2.34 us
    pallas_call x1, Pallas kernels, body(): call(functools.partial(select_kernel, CAP), [shape((nvec, rows * CAP, sit...  2.2 us
    ppermute x1, starting transfers between devices, body(): below = lax.ppermute(link_late[2], 'slab', upward)  1.92 us
    ppermute x1, starting transfers between devices, body(): inner = lax.ppermute(flat_late, 'slab', mate)  1.92 us
  transfers between devices with their start and end apart: 5, of which 2 were waited for; matrix products, arithmetic and copies ran while one was open for 0% of the time, Pallas kernels for 10%

profile of v9, /device:TPU:2, one launch (start us, length us, event | category | flops | bytes accessed | tf_op | source)
XLA Modules:
  0.0 64.7 jit_solution(5815773016757153274)
XLA Ops:
  0.0 13.5 %collective-permute-start = (bf16[288,512]{1,0:T(8,128)(2,1)}, bf16[288,512]{1,0:T(8,128)(2,1)S(1)}, u32[]{:S(2)}, u32[]{:S(2)}) collective-permute-start(bf16[288,512]{1,0:T(8,128)(2,1)} %bitcast.20), channel_id=1, source_target_pairs={{0,504},{8,16},{16,8},{24,32},{32,24},{40,48},{48,40},{56,64},{64,... | collective-permute-start | bytes 884744 | tf_op jit(solution)/shard_map/ppermute | solution.py:300
  13.5 0.0 copy-start.3
  13.5 0.0 copy-start.4
  13.5 2.2 %select.1 = (bf16[8,96,512]{2,1,0:T(8,128)(2,1)}, s32[1]{0:T(128)S(4)}) custom-call(s32[1,64]{1,0:T(1,128)} %bitcast.25, bf16[6,48,512]{2,1,0:T(8,128)(2,1)} %bitcast.21), custom_call_target="tpu_custom_call" | custom-call | flops 49999998976 | tf_op jit(solution)/shard_map/select/pallas_call | solution.py:301
  15.7 0.0 copy-done.3
  15.7 0.0 copy-done.4
  15.7 0.0 copy-start
  15.7 0.0 copy-start.2
  15.8 5.0 %all-to-all-start.1 = ((bf16[8,96,512]{2,1,0:T(8,128)(2,1)}), bf16[8,96,512]{2,1,0:T(8,128)(2,1)S(1)}, u32[]{:S(2)}, u32[]{:S(2)}) async-start(bf16[8,96,512]{2,1,0:T(8,128)(2,1)} %get-tuple-element.28), calls=%async_computation.1 | async-start | bytes 1572864 | tf_op jit(solution)/shard_map/all_to_all | solution.py:308
  20.8 0.0 collective-permute-done.outer_ref
  20.8 0.0 copy-done
  20.8 1.9 %collective-permute-start.1 = (bf16[18,512]{1,0:T(8,128)(2,1)S(1)}, bf16[18,512]{1,0:T(8,128)(2,1)S(1)}, u32[]{:S(2)}, u32[]{:S(2)}) collective-permute-start(bf16[18,512]{1,0:T(8,128)(2,1)S(1)} %slice_bitcast_fusion), channel_id=1, source_target_pairs={{0,8},{8,16},{16,24},{24,32},{32,40},{40,48},{48,56},{56,64},{64,7... | collective-permute-start | bytes 55304 | tf_op jit(solution)/shard_map/ppermute | solution.py:323
  22.7 1.9 %collective-permute-start.2 = (bf16[288,512]{1,0:T(8,128)(2,1)S(1)}, bf16[288,512]{1,0:T(8,128)(2,1)S(1)}, u32[]{:S(2)}, u32[]{:S(2)}) collective-permute-start(bf16[288,512]{1,0:T(8,128)(2,1)S(1)} %bitcast.22), channel_id=1, source_target_pairs={{0,8},{8,0},{16,24},{24,16},{32,40},{40,32},{48,56},{56,48},{64,72... | collective-permute-start | bytes 884744 | tf_op jit(solution)/shard_map/ppermute | solution.py:322
  24.6 0.0 copy-done.2
  24.6 2.5 %planar.1 = (bf16[2,48,3072]{2,1,0:T(8,128)(2,1)S(1)}, f32[8,512]{1,0:T(8,128)S(1)}, bf16[64,128]{1,0:T(8,128)(2,1)S(1)}) custom-call(s32[4,3]{1,0:T(4,128)S(1)} %copy-done.2, s32[1,64]{1,0:T(1,128)S(1)} %bitcast.27, bf16[6,48,512]{2,1,0:T(8,128)(2,1)S(1)} %bitcast.23, bf16[3,18,512]{2,1,0:T(8,128)(2,1)S(1)} %bitcast.16), custom_call_target="tpu_custom_call" | custom-call | flops 49999998976 | tf_op jit(solution)/shard_map/planar/pallas_call | solution.py:314
  27.2 2.3 %collective-permute-done.1.below_ref = bf16[18,512]{1,0:T(8,128)(2,1)S(1)} collective-permute-done((bf16[18,512]{1,0:T(8,128)(2,1)S(1)}, bf16[18,512]{1,0:T(8,128)(2,1)S(1)}, u32[]{:S(2)}, u32[]{:S(2)}) %collective-permute-start.1) | collective-permute-done | bytes 18464 | tf_op jit(solution)/shard_map/ppermute | solution.py:323
  29.5 0.0 collective-permute-done.2.inner_ref
  29.5 0.6 height.1.field_ref
  30.1 0.0 all-to-all-done.1.got_ref
  30.1 0.9 %send.1 = f32[288,128]{1,0:T(8,128)S(1)} custom-call(bf16[144,3072]{1,0:T(8,128)(2,1)S(1)} %height.1.field_ref, f32[8,512]{1,0:T(8,128)S(1)} %get-tuple-element.26.phase_ref, bf16[64,128]{1,0:T(8,128)(2,1)S(1)} %get-tuple-element.27.order_ref, bf16[8,96,512]{2,1,0:T(8,128)(2,1)S(1)} %all-to-all-done.1.got_ref, ...), custom_call_target="tpu_custom_call" | custom-call | tf_op jit(solution)/shard_map/send/pallas_call | solution.py:330
  31.0 0.0 copy-start.1
  31.0 1.9 %collective-permute-start.3 = (f32[288,128]{1,0:T(8,128)S(1)}, f32[288,128]{1,0:T(8,128)S(1)}, u32[]{:S(2)}, u32[]{:S(2)}) collective-permute-start(f32[288,128]{1,0:T(8,128)S(1)} %send.1), channel_id=1, source_target_pairs={{0,8},{8,0},{16,24},{24,16},{32,40},{40,32},{48,56},{56,48},{64,72... | collective-permute-start | bytes 442376 | tf_op jit(solution)/shard_map/ppermute | solution.py:338
  32.9 0.9 %keep.1 = f32[288,128]{1,0:T(8,128)S(1)} custom-call(bf16[144,3072]{1,0:T(8,128)(2,1)S(1)} %height.1.field_ref, f32[8,512]{1,0:T(8,128)S(1)} %get-tuple-element.26.phase_ref, bf16[64,128]{1,0:T(8,128)(2,1)S(1)} %get-tuple-element.27.order_ref, bf16[8,96,512]{2,1,0:T(8,128)(2,1)S(1)} %all-to-all-done.1.got_ref, ...), custom_call_target="tpu_custom_call" | custom-call | flops 49999998976 | tf_op jit(solution)/shard_map/keep/pallas_call | solution.py:330
  33.8 0.5 collective-permute-done.3
  34.3 29.5 %all_to_all.15 = f32[32,1,1152]{2,1,0:T(1,128)S(1)} all-to-all(f32[32,1,1152]{2,1,0:T(1,128)S(1)} %bitcast.19), channel_id=1, replica_groups={{0,16,32,48,64,80,96,112,128,144,160,176,192,208,224,240,256,272,288,30..., dimensions={0} | all-to-all | bytes 294912 | tf_op jit(solution)/shard_map/all_to_all | solution.py:341
  63.8 0.0 copy-done.1
  63.8 0.8 %total.1 = f32[2,3,4,48]{3,2,1,0:T(4,128)} custom-call(s32[1,3]{1,0:T(1,128)S(1)} %bitcast.18, f32[288,128]{1,0:T(8,128)S(1)} %bitcast.14), custom_call_target="tpu_custom_call" | custom-call | tf_op jit(solution)/shard_map/total/pallas_call | solution.py:343
  (4 shorter events, 0.1 us)
Async XLA Ops:
  0.0 20.8 %collective-permute-start = (bf16[288,512]{1,0:T(8,128)(2,1)}, bf16[288,512]{1,0:T(8,128)(2,1)S(1)}, u32[]{:S(2)}, u32[]{:S(2)}) collective-permute-start(bf16[288,512]{1,0:T(8,128)(2,1)} %bitcast.20), channel_id=1, source_target_pairs={{0,504},{8,16},{16,8},{24,32},{32,24},{40,48},{48,40},{56,64},{64,... | collective-permute-start | bytes 884744 | tf_op jit(solution)/shard_map/ppermute | solution.py:300
  13.5 2.2 %copy-start.3 = (bf16[6,48,1,512]{3,1,2,0:T(8,128)(2,1)S(1)}, bf16[6,48,1,512]{3,1,2,0:T(8,128)(2,1)}, u32[]{:S(2)}) copy-start(bf16[6,48,1,512]{3,1,2,0:T(8,128)(2,1)} %param.7) | copy-start | bytes 884740
  13.5 2.2 %copy-start.4 = (s32[64]{0:T(128)S(1)}, s32[64]{0:T(128)}, u32[]{:S(2)}) copy-start(s32[64]{0:T(128)} %param.11) | copy-start | bytes 772
  15.7 5.0 %copy-start = (bf16[3,18,1,512]{3,1,2,0:T(8,128)(2,1)S(1)}, bf16[3,18,1,512]{3,1,2,0:T(8,128)(2,1)}, u32[]{:S(2)}) copy-start(bf16[3,18,1,512]{3,1,2,0:T(8,128)(2,1)} %param.8) | copy-start | bytes 165892
  15.7 8.9 %copy-start.2 = (s32[4,3]{1,0:T(4,128)S(1)}, s32[4,3]{1,0:T(4,128)}, u32[]{:S(2)}) copy-start(s32[4,3]{1,0:T(4,128)} %momenta_ref.1) | copy-start | bytes 148
  15.8 14.3 %all-to-all-start.1 = ((bf16[8,96,512]{2,1,0:T(8,128)(2,1)}), bf16[8,96,512]{2,1,0:T(8,128)(2,1)S(1)}, u32[]{:S(2)}, u32[]{:S(2)}) async-start(bf16[8,96,512]{2,1,0:T(8,128)(2,1)} %get-tuple-element.28), calls=%async_computation.1 | async-start | bytes 1572864 | tf_op jit(solution)/shard_map/all_to_all | solution.py:308
  20.8 8.8 %collective-permute-start.1 = (bf16[18,512]{1,0:T(8,128)(2,1)S(1)}, bf16[18,512]{1,0:T(8,128)(2,1)S(1)}, u32[]{:S(2)}, u32[]{:S(2)}) collective-permute-start(bf16[18,512]{1,0:T(8,128)(2,1)S(1)} %slice_bitcast_fusion), channel_id=1, source_target_pairs={{0,8},{8,16},{16,24},{24,32},{32,40},{40,48},{48,56},{56,64},{64,7... | collective-permute-start | bytes 55304 | tf_op jit(solution)/shard_map/ppermute | solution.py:323
  22.7 6.8 %collective-permute-start.2 = (bf16[288,512]{1,0:T(8,128)(2,1)S(1)}, bf16[288,512]{1,0:T(8,128)(2,1)S(1)}, u32[]{:S(2)}, u32[]{:S(2)}) collective-permute-start(bf16[288,512]{1,0:T(8,128)(2,1)S(1)} %bitcast.22), channel_id=1, source_target_pairs={{0,8},{8,0},{16,24},{24,16},{32,40},{40,32},{48,56},{56,48},{64,72... | collective-permute-start | bytes 884744 | tf_op jit(solution)/shard_map/ppermute | solution.py:322
  31.0 32.8 %copy-start.1 = (s32[3]{0:T(128)S(1)}, s32[3]{0:T(128)}, u32[]{:S(2)}) copy-start(s32[3]{0:T(128)} %param.10) | copy-start | bytes 40
  31.0 3.3 %collective-permute-start.3 = (f32[288,128]{1,0:T(8,128)S(1)}, f32[288,128]{1,0:T(8,128)S(1)}, u32[]{:S(2)}, u32[]{:S(2)}) collective-permute-start(f32[288,128]{1,0:T(8,128)S(1)} %send.1), channel_id=1, source_target_pairs={{0,8},{8,0},{16,24},{24,16},{32,40},{40,32},{48,56},{56,48},{64,72... | collective-permute-start | bytes 442376 | tf_op jit(solution)/shard_map/ppermute | solution.py:338
